TPU v7x, 32 devices: a whole 2x2x4 slice. The times are simulated.
32 devices in a mesh: seq: 4 (over y, x), chan: 8 (over z, core).
Axes of the slice: x: 2, y: 2, z: 4, core: 2. Of those that a mesh axis runs over, the one named last changes fastest.
Arguments:
- query_in: bfloat16 [1024, 4096], P('seq', 'chan'), may hold values from -6 to 6
- key_in: bfloat16 [1024, 4096], P('seq', 'chan'), may hold values from -6 to 6
- value_in: bfloat16 [1024, 4096], P('seq', 'chan'), may hold values from -6 to 6
- filter_taps: bfloat16 [256, 1024], P('chan', 'seq'), may hold values from -1.05 to 1.05, as said below
- skip_gain: float32 [4096], P('chan'), may hold values from 0.5 to 1.5
- out_weight: bfloat16 [4096, 4096], P('chan'), may hold values from -0.09375 to 0.09375
Outputs:
- mixed_out: bfloat16 [1024, 4096], P('seq', 'chan')
Inputs may be any that keep to these rules, and one draw needn't show every extreme that they name: `filter_taps`: taps of every filter; the filters differ in how fast their taps fade with the lag.
All inputs are finite; a program needn't handle non-finite values.
Results may differ from a plain program's by a relative error of at most 0.0057.
Values may be sent and summed in bfloat16 or wider, within the bound.
No kernel may reach another device: no remote copies, remote signals or barrier semaphores. Data moves between devices by JAX's collectives and lax.ppermute only.
A program may use at most 64 MiB of HBM per device.

v0:
```python
import math

import jax
import jax.numpy as jnp
from jax import lax
from jax.sharding import PartitionSpec as P


def window_matrix(window, tile_size):
    reversed_window = window[:, ::-1]
    extended = jnp.concatenate(
        [reversed_window, jnp.zeros((window.shape[0], 1), window.dtype)], axis=1
    )
    repeated = jnp.tile(extended, (1, tile_size))[:, : tile_size * (2 * tile_size - 1)]
    return repeated.reshape(window.shape[0], tile_size, 2 * tile_size - 1)[:, :, tile_size - 1 :]


def accumulate(running, segment, tap_table, own_start):
    row_count, chan_width = running.shape
    group_count = tap_table.shape[0]
    tap_span = tap_table.shape[1] // 2
    group_width = chan_width // group_count
    block_rows = min(segment.shape[0], row_count)
    tile_size = math.gcd(math.gcd(block_rows, row_count), 128)
    out_tiles = row_count // tile_size
    in_tiles = block_rows // tile_size

    def one_block(step_index, current):
        block_start = step_index * block_rows
        in_blocks = lax.dynamic_slice_in_dim(segment, step_index * block_rows, block_rows, 0)
        in_blocks = in_blocks.reshape(in_tiles, tile_size, group_count, group_width)

        def add_block(previous):
            out_blocks = previous.reshape(out_tiles, tile_size, group_count, group_width)
            offset = own_start - block_start
            for lag_step in range(1 - in_tiles, out_tiles):
                tap_first = offset + lag_step * tile_size - (tile_size - 1) + tap_span
                window = lax.dynamic_slice_in_dim(tap_table, tap_first, 2 * tile_size - 1, 1)
                matrix = window_matrix(window, tile_size)
                first_out = max(0, lag_step)
                last_out = min(out_tiles, in_tiles + lag_step)
                addend = jnp.einsum(
                    "gij,qjgc->qigc",
                    matrix,
                    in_blocks[first_out - lag_step : last_out - lag_step],
                    preferred_element_type=jnp.float32,
                )
                out_blocks = out_blocks.at[first_out:last_out].add(addend)
            return out_blocks.reshape(previous.shape)

        def keep_same(previous):
            return previous

        needed = (block_start < own_start + row_count) & (block_start >= 0)
        return lax.cond(needed, add_block, keep_same, current)

    return lax.fori_loop(0, segment.shape[0] // block_rows, one_block, running)


def body(query_in, key_in, value_in, filter_taps, skip_gain, out_weight):
    row_count, chan_width = query_in.shape
    mixed_in = (key_in.astype(jnp.float32) * value_in.astype(jnp.float32)).astype(jnp.bfloat16)
    all_taps = lax.all_gather(filter_taps, "seq", axis=1, tiled=True)
    tap_table = jnp.concatenate([jnp.zeros_like(all_taps), all_taps], axis=1)
    seq_index = lax.axis_index("seq")
    own_start = seq_index * row_count
    zero_sum = jnp.zeros((row_count, chan_width), jnp.float32)
    convolved = accumulate(
        zero_sum, lax.all_gather(mixed_in, "seq", axis=0, tiled=True), tap_table, own_start
    )
    gated = (
        query_in.astype(jnp.float32)
        * (convolved + skip_gain[None, :] * mixed_in.astype(jnp.float32))
    ).astype(jnp.bfloat16)
    columns = lax.all_to_all(out_weight, "chan", split_axis=1, concat_axis=0, tiled=True)
    result = jnp.dot(
        lax.all_gather(gated, "chan", axis=1, tiled=True),
        columns,
        preferred_element_type=jnp.float32,
    )
    return result.astype(jnp.bfloat16)


def solution(mesh):
    placed = (
        P("seq", "chan"),
        P("seq", "chan"),
        P("seq", "chan"),
        P("chan", "seq"),
        P("chan"),
        P("chan", None),
    )
    return jax.shard_map(
        body, mesh=mesh, in_specs=placed, out_specs=P("seq", "chan"), check_vma=False
    )
```

profile of v0, /device:TPU:0, one launch (start us, length us, event | category | flops | bytes accessed | tf_op | source)
XLA Modules:
  0.0 250.9 jit_solution(15151051128259370132)
XLA Ops:
  6.5 6.5 %copy.24 = bf16[512,4096]{0,1:T(8,128)(2,1)} copy(bf16[512,4096]{1,0:T(8,128)(2,1)} %param.23) | data formatting | bytes 8388608 | tf_op args[5]
  13.0 6.5 %all-to-all-start = ((bf16[512,8,512]{0,2,1:T(8,128)(2,1)}), bf16[512,8,512]{0,2,1:T(8,128)(2,1)}, u32[]{:S(2)}, u32[]{:S(2)}) async-start(bf16[512,8,512]{0,2,1:T(8,128)(2,1)} %bitcast.70), calls=%async_computation | async-start | bytes 8388608 | tf_op jit(solution)/shard_map/all_to_all | solution.py:75
  19.9 0.8 multiply_convert_fusion.1
  20.7 0.8 copy.21
  21.6 8.5 %all_gather.10 = bf16[32,1024]{1,0:T(8,128)(2,1)S(1)} all-gather(bf16[32,256]{1,0:T(8,128)(2,1)S(1)} %copy-done.3), channel_id=1, replica_groups=mesh['seq'=4,'chan'=8] {'seq'}, dimensions={1}, use_global_device_ids=true | all-gather | bytes 81920 | tf_op jit(solution)/shard_map/all_gather | solution.py:63
  30.0 0.7 concatenate.18
  30.7 19.5 %all-gather.3.cloned.1.call-done = bf16[1024,512]{0,1:T(8,128)(2,1)} async-done(((bf16[256,512]{0,1:T(8,128)(2,1)}), bf16[1024,512]{0,1:T(8,128)(2,1)}) %all-gather.3.cloned.1.call-update) | async-done | bytes 1048592 | tf_op jit(solution)/shard_map/all_gather | solution.py:69
  50.2 39.6 %while.21 = (s32[]{:T(128)}, f32[256,512]{0,1:T(8,128)S(1)}, s32[]{:T(128)}, bf16[1024,512]{0,1:T(8,128)(2,1)}, s32[]{:T(128)}, /*index=5*/bf16[32,2048]{1,0:T(8,128)(2,1)}, s32[]{:T(128)}, s32[]{:T(128)}, s32[]{:T(128)}) while((s32[]{:T(128)}, f32[256,512]{0,1:T(8,128)S(1)}, s32[]{:T(128)}, bf16[1024,512]{0,1:T(8,128)(2,1)}, s32[]{:T(128)}, ...), condition=%wide.region_3.4_spmd, body=%wide.region_0.3_spmd.sunk | while | flops 67371032 | bytes 58015184 | solution.py:57
  50.2 39.4 %conditional.2 = (f32[256,512]{0,1:T(8,128)S(1)}) conditional(s32[]{:T(128)} %convert_element_type.44, f32[256,512]{0,1:T(8,128)S(1)} %get-tuple-element.297, (f32[256,512]{0,1:T(8,128)S(1)}, s32[]{:T(128)}, bf16[1024,512]{0,1:T(8,128)(2,1)}, s32[]{:T(128)}, bf16[32,2048]{1,0:T(8,128)(2,1)}) %tuple.67), branch_computations={%region_1.0_spmd, %region_2.2_spmd} | conditional | flops 67371024 | bytes 58015016 | solution.py:55
  50.3 0.9 constant_dynamic-slice_fusion.2
  51.2 0.2 reverse.2
  51.5 0.2 reverse.1
  51.8 0.2 reverse
  52.1 1.0 constant_dynamic-slice_fusion
  53.1 1.0 constant_dynamic-slice_fusion.5
  54.2 0.3 reshape.174
  54.7 1.2 copy.26
  56.0 7.8 %reshape.177 = bf16[32,128,255]{2,1,0:T(8,128)(2,1)} reshape(bf16[32,32640]{1,0:T(8,128)(2,1)S(1)} %slice.121) | data formatting | bytes 4177920 | tf_op jit(solution)/shard_map/while/body/eval_jaxpr/cond/branch_1_fun/reshape | solution.py:15
  63.8 2.3 fusion.4
  66.1 0.2 tile.5
  66.2 1.2 copy.27
  67.6 7.8 %reshape.179 = bf16[32,128,255]{2,1,0:T(8,128)(2,1)} reshape(bf16[32,32640]{1,0:T(8,128)(2,1)S(1)} %slice.123) | data formatting | bytes 4177920 | tf_op jit(solution)/shard_map/while/body/eval_jaxpr/cond/branch_1_fun/reshape | solution.py:15
  75.3 2.3 fusion.6
  77.9 1.2 copy.28
  79.3 7.8 %reshape.182 = bf16[32,128,255]{2,1,0:T(8,128)(2,1)} reshape(bf16[32,32640]{1,0:T(8,128)(2,1)S(1)} %slice.126) | data formatting | bytes 4177920 | tf_op jit(solution)/shard_map/while/body/eval_jaxpr/cond/branch_1_fun/reshape | solution.py:15
  87.0 2.3 fusion.1
  89.3 0.3 copy.20
  89.8 1.9 multiply_convert_fusion
  91.8 21.8 %all-to-all-done = bf16[512,8,512]{0,2,1:T(8,128)(2,1)} async-done(((bf16[512,8,512]{0,2,1:T(8,128)(2,1)}), bf16[512,8,512]{0,2,1:T(8,128)(2,1)}, u32[]{:S(2)}, u32[]{:S(2)}) %all-to-all-start) | async-done | bytes 4194336 | tf_op jit(solution)/shard_map/all_to_all | solution.py:75
  113.6 6.6 %copy.25 = bf16[8,512,512]{2,1,0:T(8,128)(2,1)} copy(bf16[8,512,512]{1,2,0:T(8,128)(2,1)} %bitcast.13) | data formatting | bytes 8388608 | tf_op jit(solution)/shard_map/all_to_all | solution.py:75
  120.2 119.1 %all-gather.5.cloned.1.call-done = bf16[256,4096]{0,1:T(8,128)(2,1)} async-done(((bf16[256,512]{0,1:T(8,128)(2,1)}), bf16[256,4096]{0,1:T(8,128)(2,1)}) %all-gather.5.cloned.1.call-update) | async-done | bytes 2097168 | tf_op jit(solution)/shard_map/all_gather | solution.py:77
  239.3 4.8 %convolution_convert_fusion = bf16[256,512]{1,0:T(8,128)(2,1)} fusion(bf16[256,4096]{0,1:T(8,128)(2,1)} %all-gather.5.cloned.1.call-done, bf16[4096,512]{1,0:T(8,128)(2,1)} %bitcast.73), kind=kOutput, calls=%fused_computation.18 | convolution fusion | flops 1073872896 | bytes 6553600 | tf_op jit(solution)/shard_map/dot_general | solution.py:76
  (37 shorter events, 1.7 us)
Async XLA Ops:
  13.0 6.5 %copy-start = (bf16[256,512]{1,0:T(8,128)(2,1)S(1)}, bf16[256,512]{1,0:T(8,128)(2,1)}, u32[]{:S(2)}) copy-start(bf16[256,512]{1,0:T(8,128)(2,1)} %param.19) | copy-start | bytes 786436
  13.0 6.7 %copy-start.1 = (bf16[256,512]{1,0:T(8,128)(2,1)S(1)}, bf16[256,512]{1,0:T(8,128)(2,1)}, u32[]{:S(2)}) copy-start(bf16[256,512]{1,0:T(8,128)(2,1)} %param.20) | copy-start | bytes 786436
  13.0 100.6 %all-to-all-start = ((bf16[512,8,512]{0,2,1:T(8,128)(2,1)}), bf16[512,8,512]{0,2,1:T(8,128)(2,1)}, u32[]{:S(2)}, u32[]{:S(2)}) async-start(bf16[512,8,512]{0,2,1:T(8,128)(2,1)} %bitcast.70), calls=%async_computation | async-start | bytes 8388608 | tf_op jit(solution)/shard_map/all_to_all | solution.py:75
  19.5 1.2 copy-start.2
  19.5 2.1 copy-start.3
  19.5 30.6 %all-gather.3.cloned.1.call-start = ((), (), s32[]{:S(2)}) async-start(), calls=%async_computation.1 | async-start | bytes 1310720 | tf_op jit(solution)/shard_map/all_gather | solution.py:69
  20.7 218.6 %all-gather.5.cloned.1.call-start = ((), (), s32[]{:S(2)}) async-start(), calls=%async_computation.2 | async-start | bytes 2359296 | tf_op jit(solution)/shard_map/all_gather | solution.py:77
  50.2 39.6 %copy-start.4 = (f32[512]{0:T(512)S(1)}, f32[512]{0:T(512)}, u32[]{:S(2)}) copy-start(f32[512]{0:T(512)} %param.22) | copy-start | bytes 6148
Sparse Core Ops, SparseCore 0:
  22.2 27.9 all-gather.2
  91.9 147.3 all-gather.4
where the time goes:
time: 252 us; the launch traced here: 251 us
  waiting for transfers between devices  160 us (63%)
  local copies, waits for them, and re-layouts  47.2 us (19%)
  between operations  13.5 us (5%)
  matrix products  11.7 us (5%)
  blocking collectives  8.46 us (3%)
  starting transfers between devices  6.54 us (3%)
  other arithmetic  2.78 us (1%)
    all_gather x1, waiting for transfers between devices, body(): lax.all_gather(gated, 'chan', axis=1, tiled=True)  119 us
    reshape x3, local copies, waits for them, and re-layouts, window_matrix(): repeated.reshape(window.shape[0], tile_size, 2 * tile_size - 1)  23.3 us
    all_to_all x1, waiting for transfers between devices, body(): lax.all_to_all(out_weight, 'chan', split_axis=1, concat_axis=0, tiled=True)  21.8 us
    all_gather x1, waiting for transfers between devices, body(): lax.all_gather(mixed_in, 'seq', axis=0, tiled=True)  19.5 us
    all_gather x1, blocking collectives, body(): all_taps = lax.all_gather(filter_taps, 'seq', axis=1, tiled=True)  8.46 us
    unnamed x14, local copies, waits for them, and re-layouts  7.63 us
    all_to_all x1, local copies, waits for them, and re-layouts, body(): lax.all_to_all(out_weight, 'chan', split_axis=1, concat_axis=0, tiled=True)  6.6 us
    all_to_all x1, starting transfers between devices, body(): lax.all_to_all(out_weight, 'chan', split_axis=1, concat_axis=0, tiled=True)  6.46 us
  transfers between devices with their start and end apart: 3, of which 3 were waited for; matrix products, arithmetic and copies ran while one was open for 20% of the time, Pallas kernels for 0%

commit v1 on v0

--- a/solution.py
+++ b/solution.py
@@ -1,9 +1,398 @@
+import functools
 import math
 
 import jax
 import jax.numpy as jnp
 from jax import lax
+from jax.experimental import pallas as pl
+from jax.experimental.pallas import tpu as pltpu
 from jax.sharding import PartitionSpec as P
+
+LANES = 128
+BF16 = jnp.bfloat16
+F32 = jnp.float32
+VMEM_LIMIT = 16 * 1024 * 1024
+
+
+def params():
+    return pltpu.CompilerParams(vmem_limit_bytes=VMEM_LIMIT)
+
+
+def in_hbm(*arrays):
+    return [pltpu.with_memory_space_constraint(a, pltpu.HBM) for a in arrays]
+
+
+def in_vmem(*arrays):
+    return [pltpu.with_memory_space_constraint(a, pltpu.VMEM) for a in arrays]
+
+
+def lanes_at(block):
+    return pl.ds(pl.multiple_of(block * LANES, LANES), LANES)
+
+
+def rows_at(block, size):
+    return pl.ds(pl.multiple_of(block * size, size), size)
+
+
+def product_kernel(n_seq, me_ref, key_hbm, value_hbm, taps_hbm, mixed_ref, *rest):
+    packed_refs, (key_ref, value_ref, taps_ref, taps_f32, arrived) = rest[:n_seq], rest[n_seq:]
+    rows = key_ref.shape[0]
+    groups, span = taps_ref.shape
+    part = groups // n_seq
+    loads = [
+        pltpu.make_async_copy(source, target, arrived.at[i])
+        for i, (source, target) in enumerate(
+            [(taps_hbm, taps_ref), (key_hbm, key_ref), (value_hbm, value_ref)]
+        )
+    ]
+    for load in loads:
+        load.start()
+    loads[0].wait()
+    taps_f32[...] = taps_ref[...].astype(F32)
+    for d in range(n_seq):
+        own = taps_f32[rows_at(me_ref[0] ^ d, part), :]
+        pieces = [own[:, k * LANES : (k + 1) * LANES] for k in range(span // LANES)]
+        packed_refs[d][rows:, :] = jnp.concatenate(pieces, axis=0).astype(BF16)
+    loads[1].wait()
+    loads[2].wait()
+    mixed_ref[...] = (key_ref[...].astype(F32) * value_ref[...].astype(F32)).astype(BF16)
+    for d in range(n_seq):
+        packed_refs[d][0:rows, :] = mixed_ref[:, lanes_at(me_ref[0] ^ d)]
+
+
+def products(me, key_in, value_in, taps, n_seq):
+    rows, width = key_in.shape
+    groups, span = taps.shape
+    tap_rows = (groups // n_seq) * (span // LANES)
+    packed = jax.ShapeDtypeStruct((rows + tap_rows, LANES), BF16)
+    return pl.pallas_call(
+        functools.partial(product_kernel, n_seq),
+        out_shape=[jax.ShapeDtypeStruct((rows, width), BF16)] + [packed] * n_seq,
+        in_specs=[pl.BlockSpec(memory_space=pltpu.SMEM)] + [pl.BlockSpec(memory_space=pl.ANY)] * 3,
+        out_specs=[pl.BlockSpec(memory_space=pltpu.VMEM)] * (n_seq + 1),
+        scratch_shapes=[
+            pltpu.VMEM((rows, width), BF16),
+            pltpu.VMEM((rows, width), BF16),
+            pltpu.VMEM((groups, span), BF16),
+            pltpu.VMEM((groups, span), F32),
+            pltpu.SemaphoreType.DMA((3,)),
+        ],
+        compiler_params=params(),
+        name="products",
+    )(me, *in_hbm(key_in, value_in, taps))
+
+
+def conv_kernel(n_seq, rows, part, columns, me_ref, core_ref, weight_hbm, *refs):
+    packed_refs = refs[:n_seq]
+    out_refs = refs[n_seq : 2 * n_seq]
+    weight_out, signal, tap_rows, lag_blocks, total, arrived = refs[2 * n_seq :]
+
+    loads = []
+    for i in range(weight_out.shape[1] // columns):
+        source = weight_hbm.at[:, rows_at(2 * i + 1 - core_ref[0], columns)]
+        target = weight_out.at[:, i * columns : (i + 1) * columns]
+        loads.append(pltpu.make_async_copy(source, target, arrived.at[i]))
+    for load in loads:
+        load.start()
+
+    per_shard = rows // LANES
+    tiles = n_seq * per_shard
+    group_width = LANES // part
+
+    for d in range(n_seq):
+        other = me_ref[0] ^ d
+        signal[rows_at(other, rows), :] = packed_refs[d][0:rows, :]
+        tap_rows[rows_at(other, part * per_shard), :] = packed_refs[d][rows:, :].astype(F32)
+
+    from_lane = lax.broadcasted_iota(jnp.int32, (LANES, LANES), 0)
+    to_lane = lax.broadcasted_iota(jnp.int32, (LANES, LANES), 1)
+    flip = jnp.where((from_lane + to_lane) % LANES == 0, 1.0, 0.0).astype(BF16)
+    tap_rows[...] = jnp.dot(tap_rows[...].astype(BF16), flip, preferred_element_type=F32)
+
+    lower = to_lane <= from_lane
+    zero_block = jnp.zeros((LANES, LANES), BF16)
+
+    for g in range(part):
+        lag_blocks[0:LANES, (2 * g + 1) * LANES : (2 * g + 2) * LANES] = zero_block
+        before = jnp.zeros((LANES, LANES), F32)
+        for k in range(tiles):
+            row = tap_rows[k * part + g : k * part + g + 1, :]
+            rolled = pltpu.roll(
+                jnp.broadcast_to(row, (LANES, LANES)), 0, 1, stride=1, stride_axis=0
+            )
+            block = jnp.where(lower, rolled, before).astype(BF16)
+            lag_blocks[k * LANES : (k + 1) * LANES, 2 * g * LANES : (2 * g + 1) * LANES] = block
+            if k + 1 < tiles:
+                lag_blocks[
+                    (k + 1) * LANES : (k + 2) * LANES, (2 * g + 1) * LANES : (2 * g + 2) * LANES
+                ] = block
+            before = rolled
+
+    step = 2 * LANES
+    length = n_seq * rows
+    lane_group = lax.broadcasted_iota(jnp.int32, (step, LANES), 1) // group_width
+    total[...] = jnp.zeros_like(total)
+    for first in range(0, length, 2 * step):
+        left = signal[first : first + step, :]
+        right = signal[first + step : first + 2 * step, :]
+        masked = []
+        for g in range(part):
+            here = lane_group == g
+            masked.append(
+                jnp.concatenate(
+                    [jnp.where(here, left, 0.0).astype(BF16), jnp.where(here, right, 0.0).astype(BF16)],
+                    axis=1,
+                )
+            )
+        both = jnp.dot(
+            lag_blocks[0 : length - first, :],
+            jnp.concatenate(masked, axis=0),
+            preferred_element_type=F32,
+        )
+        total[first:length, :] += both[:, 0:LANES]
+        total[first + step : length, :] += both[0 : length - first - step, LANES:]
+
+    for d in range(n_seq):
+        out_refs[d][...] = total[rows_at(me_ref[0] ^ d, rows), :].astype(BF16)
+    for load in loads:
+        load.wait()
+
+
+def convolve(me, core, out_weight, packed, n_seq, rows, part, columns):
+    tiles = n_seq * rows // LANES
+    depth, total_columns = out_weight.shape
+    chips = total_columns // (2 * columns)
+    vmem = pl.BlockSpec(memory_space=pltpu.VMEM)
+    smem = pl.BlockSpec(memory_space=pltpu.SMEM)
+    return pl.pallas_call(
+        functools.partial(conv_kernel, n_seq, rows, part, columns),
+        out_shape=[jax.ShapeDtypeStruct((rows, LANES), BF16)] * n_seq
+        + [jax.ShapeDtypeStruct((depth, chips * columns), out_weight.dtype)],
+        in_specs=[smem, smem, pl.BlockSpec(memory_space=pl.ANY)] + [vmem] * n_seq,
+        out_specs=[vmem] * (n_seq + 1),
+        scratch_shapes=[
+            pltpu.VMEM((n_seq * rows, LANES), BF16),
+            pltpu.VMEM((tiles * part, LANES), F32),
+            pltpu.VMEM((n_seq * rows, 2 * LANES * part), BF16),
+            pltpu.VMEM((n_seq * rows, LANES), F32),
+            pltpu.SemaphoreType.DMA((chips,)),
+        ],
+        compiler_params=params(),
+        name="convolve",
+    )(me, core, *in_hbm(out_weight), *packed)
+
+
+def gate_kernel(n_seq, me_ref, query_ref, mixed_ref, skip_ref, *refs):
+    conv_refs, out_ref = refs[:n_seq], refs[n_seq]
+    for d in range(n_seq):
+        lanes = lanes_at(me_ref[0] ^ d)
+        direct = skip_ref[:, lanes] * mixed_ref[:, lanes].astype(F32)
+        out_ref[:, lanes] = (
+            query_ref[:, lanes].astype(F32) * (conv_refs[d][...].astype(F32) + direct)
+        ).astype(BF16)
+
+
+def gate(me, query_in, mixed_in, skip_gain, parts):
+    vmem = pl.BlockSpec(memory_space=pltpu.VMEM)
+    return pl.pallas_call(
+        functools.partial(gate_kernel, len(parts)),
+        out_shape=jax.ShapeDtypeStruct(query_in.shape, BF16),
+        in_specs=[pl.BlockSpec(memory_space=pltpu.SMEM)] + [vmem] * (3 + len(parts)),
+        out_specs=vmem,
+        compiler_params=params(),
+        name="gate",
+    )(me, query_in, mixed_in, skip_gain.reshape(1, -1), *parts)
+
+
+def load_block(weight_hbm, block, target, arrived):
+    columns = target.shape[1]
+    load = pltpu.make_async_copy(weight_hbm.at[:, rows_at(block, columns)], target, arrived)
+    load.start()
+    return load
+
+
+def half_kernel(where_ref, own_ref, weight_hbm, out_ref, weight, arrived):
+    load_block(weight_hbm, where_ref[0], weight, arrived).wait()
+    out_ref[...] = jnp.dot(own_ref[...], weight[...], preferred_element_type=F32)
+
+
+def add_half_kernel(chip_ref, half_ref, other_ref, weight_ref, out_ref):
+    there = rows_at(chip_ref[0], out_ref.shape[1])
+    out_ref[...] = (
+        half_ref[...]
+        + jnp.dot(other_ref[...], weight_ref[:, there], preferred_element_type=F32)
+    ).astype(out_ref.dtype)
+
+
+def two_kernel(where_ref, own_ref, other_ref, weight_hbm, other_weight, *refs):
+    out_refs, weight, arrived = refs[:-2], refs[-2], refs[-1]
+    columns = weight.shape[2]
+    loads = [
+        load_block(weight_hbm, where_ref[i], weight.at[i], arrived.at[i])
+        for i in range(len(out_refs))
+    ]
+    n = len(out_refs)
+    for i in range(n):
+        there = rows_at(where_ref[n + i], columns)
+        late = jnp.dot(other_ref[...], other_weight[:, there], preferred_element_type=F32)
+        loads[i].wait()
+        out_refs[i][...] = (
+            late + jnp.dot(own_ref[...], weight[i], preferred_element_type=F32)
+        ).astype(BF16)
+
+
+def base_kernel(
+    where_ref, own_ref, other_ref, weight_hbm, other_weight, pair_ref, first_ref, out_ref, weight, arrived
+):
+    columns = weight.shape[1]
+    load = load_block(weight_hbm, where_ref[0], weight, arrived)
+    there = rows_at(where_ref[1], columns)
+    late = jnp.dot(other_ref[...], other_weight[:, there], preferred_element_type=F32)
+    load.wait()
+    base = (
+        late
+        + jnp.dot(own_ref[...], weight[...], preferred_element_type=F32)
+        + pair_ref[...].astype(F32)
+    )
+
+    @pl.when(where_ref[2] == 1)
+    def _():
+        out_ref[...] = base + first_ref[...].astype(F32)
+
+    @pl.when(where_ref[2] == 0)
+    def _():
+        out_ref[...] = base
+
+
+def run_kernel(kernel, name, out_shape, scratch, scalars, *arrays, hbm=()):
+    specs, given = [pl.BlockSpec(memory_space=pltpu.SMEM)] * (len(scalars) > 0), []
+    if scalars:
+        given.append(jnp.stack(scalars).astype(jnp.int32))
+    for i, array in enumerate(arrays):
+        space = pl.ANY if i in hbm else pltpu.VMEM
+        specs.append(pl.BlockSpec(memory_space=space))
+        given += in_hbm(array) if i in hbm else [array]
+    vmem = pl.BlockSpec(memory_space=pltpu.VMEM)
+    return pl.pallas_call(
+        kernel,
+        out_shape=out_shape,
+        in_specs=specs,
+        out_specs=[vmem] * len(out_shape) if isinstance(out_shape, list) else vmem,
+        scratch_shapes=scratch,
+        compiler_params=params(),
+        name=name,
+    )(*given)
+
+
+def forward_kernel(own_ref, arrived_ref, out_ref):
+    out_ref[...] = (own_ref[...].astype(F32) + arrived_ref[...].astype(F32)).astype(BF16)
+
+
+def final_kernel(end_ref, base_ref, ends_hbm, middle_hbm, out_ref, last_ref, arrived):
+    @pl.when(end_ref[0] == 1)
+    def _():
+        pltpu.make_async_copy(ends_hbm, last_ref, arrived).start()
+
+    @pl.when(end_ref[0] == 0)
+    def _():
+        pltpu.make_async_copy(middle_hbm, last_ref, arrived).start()
+
+    pltpu.make_async_copy(middle_hbm, last_ref, arrived).wait()
+    out_ref[...] = (base_ref[...] + last_ref[...].astype(F32)).astype(BF16)
+
+
+def finish(at_end, base, ends, middle):
+    vmem = pl.BlockSpec(memory_space=pltpu.VMEM)
+    anywhere = pl.BlockSpec(memory_space=pl.ANY)
+    return pl.pallas_call(
+        final_kernel,
+        out_shape=jax.ShapeDtypeStruct(base.shape, BF16),
+        in_specs=[pl.BlockSpec(memory_space=pltpu.SMEM), vmem, anywhere, anywhere],
+        out_specs=vmem,
+        scratch_shapes=[pltpu.VMEM(base.shape, BF16), pltpu.SemaphoreType.DMA(())],
+        compiler_params=params(),
+        name="final",
+    )(at_end, base, ends, middle)
+
+
+def fast_body(n_seq, n_chan, query_in, key_in, value_in, filter_taps, skip_gain, out_weight):
+    rows, width = query_in.shape
+    groups = filter_taps.shape[0]
+    part = groups // n_seq
+    columns = out_weight.shape[1] // n_chan
+    seq = lax.axis_index("seq").astype(jnp.int32)
+    chan = lax.axis_index("chan").astype(jnp.int32)
+    chip, core = chan // 2, chan % 2
+    me = seq.reshape(1)
+
+    def over_seq(value, d):
+        return lax.ppermute(value, "seq", [(i, i ^ d) for i in range(n_seq)])
+
+    def over_chips(value, moves):
+        return lax.ppermute(
+            value, "chan", [(2 * a + c, 2 * b + c) for a, b in moves for c in range(2)]
+        )
+
+    def other_core(value):
+        return lax.ppermute(value, "chan", [(i, i ^ 1) for i in range(n_chan)])
+
+    mixed_in, *packed = products(me, key_in, value_in, filter_taps, n_seq)
+    arrived = [packed[0]] + [over_seq(packed[d], d) for d in range(1, n_seq)]
+    *convolved, for_other = convolve(
+        me, core.reshape(1), out_weight, arrived, n_seq, rows, part, columns
+    )
+    returned = [convolved[0]] + [over_seq(convolved[d], d) for d in range(1, n_seq)]
+    other_weight = other_core(for_other)
+    gated = gate(me, query_in, mixed_in, skip_gain, returned)
+    gated_other = other_core(gated)
+
+    block = jax.ShapeDtypeStruct((rows, columns), BF16)
+    block_f32 = jax.ShapeDtypeStruct((rows, columns), F32)
+    one_weight = [pltpu.VMEM((width, columns), BF16), pltpu.SemaphoreType.DMA(())]
+    two_weights = [pltpu.VMEM((2, width, columns), BF16), pltpu.SemaphoreType.DMA((2,))]
+
+    def at(target):
+        return 2 * target + core
+
+    half = run_kernel(
+        half_kernel, "half", block_f32, one_weight, [at(chip ^ 2)], gated, out_weight, hbm=(1,)
+    )
+    by_two = run_kernel(
+        add_half_kernel, "by_two", block, [], [chip ^ 2], half, gated_other, other_weight
+    )
+    first = over_chips(by_two, [(0, 1), (3, 2), (1, 3), (2, 0)])
+    by_three, by_one = run_kernel(
+        two_kernel,
+        "by_three_and_one",
+        [block, block],
+        two_weights,
+        [at(chip ^ 3), at(chip ^ 1), chip ^ 3, chip ^ 1],
+        gated,
+        gated_other,
+        out_weight,
+        other_weight,
+        hbm=(2,),
+    )
+    ends = over_chips(by_three, [(0, 3), (3, 0)])
+    pair = over_chips(by_one, [(0, 1), (1, 0), (2, 3), (3, 2)])
+    summed = run_kernel(forward_kernel, "forward", block, [], [], by_three, first)
+    middle = over_chips(summed, [(1, 2), (2, 1)])
+    at_end = ((chip == 0) | (chip == 3)).astype(jnp.int32)
+    base = run_kernel(
+        base_kernel,
+        "base",
+        block_f32,
+        one_weight,
+        [at(chip), chip, at_end],
+        gated,
+        gated_other,
+        out_weight,
+        other_weight,
+        pair,
+        first,
+        hbm=(2,),
+    )
+    return finish(at_end.reshape(1), base, ends, middle)
 
 
 def window_matrix(window, tile_size):
@@ -57,7 +446,7 @@
     return lax.fori_loop(0, segment.shape[0] // block_rows, one_block, running)
 
 
-def body(query_in, key_in, value_in, filter_taps, skip_gain, out_weight):
+def general_body(query_in, key_in, value_in, filter_taps, skip_gain, out_weight):
     row_count, chan_width = query_in.shape
     mixed_in = (key_in.astype(jnp.float32) * value_in.astype(jnp.float32)).astype(jnp.bfloat16)
     all_taps = lax.all_gather(filter_taps, "seq", axis=1, tiled=True)
@@ -82,6 +471,27 @@
 
 
 def solution(mesh):
+    n_seq, n_chan = mesh.shape["seq"], mesh.shape["chan"]
+
+    def body(query_in, key_in, value_in, filter_taps, skip_gain, out_weight):
+        rows, width = query_in.shape
+        groups, span = filter_taps.shape
+        part = groups // n_seq
+        fits = (
+            n_chan == 8
+            and n_seq & (n_seq - 1) == 0
+            and width == n_seq * LANES
+            and part * n_seq == groups
+            and part % 8 == 0
+            and (part * (rows // LANES)) % 16 == 0
+            and rows % (2 * LANES) == 0
+            and (n_seq * rows) % (4 * LANES) == 0
+            and span == rows
+            and out_weight.shape[1] % (n_chan * LANES) == 0
+        )
+        run = functools.partial(fast_body, n_seq, n_chan) if fits else general_body
+        return run(query_in, key_in, value_in, filter_taps, skip_gain, out_weight)
+
     placed = (
         P("seq", "chan"),
         P("seq", "chan"),

time: 252 us -> 50.4 us (0.20)
  the two profiles are of different devices: /device:TPU:0 before, /device:TPU:8 now
where the time goes in v1:
time: 50.4 us; the launch traced here: 50.1 us
  waiting for transfers between devices  19.1 us (38%)
  Pallas kernels  16.3 us (32%)
  starting transfers between devices  14.4 us (29%)
    ppermute x4, waiting for transfers between devices, over_chips(): lax.ppermute(value, 'chan', [(2 * a + c, 2 * b + c) for a, b in moves for...  11.5 us
    pallas_call x5, Pallas kernels, run_kernel(): pl.pallas_call(kernel, out_shape=out_shape, in_specs=specs, out_specs=[vm...  8.84 us
    ppermute x6, waiting for transfers between devices, over_seq(): return lax.ppermute(value, 'seq', [(i, i ^ d) for i in range(n_seq)])  7.45 us
    ppermute x4, starting transfers between devices, over_chips(): lax.ppermute(value, 'chan', [(2 * a + c, 2 * b + c) for a, b in moves for...  7.11 us
    ppermute x6, starting transfers between devices, over_seq(): return lax.ppermute(value, 'seq', [(i, i ^ d) for i in range(n_seq)])  7.11 us
    pallas_call x1, Pallas kernels, convolve(): pl.pallas_call(functools.partial(conv_kernel, n_seq, rows, part, columns)...  4.36 us
    pallas_call x1, Pallas kernels, finish(): pl.pallas_call(final_kernel, out_shape=jax.ShapeDtypeStruct(base.shape, B...  1.7 us
    pallas_call x1, Pallas kernels, products(): pl.pallas_call(functools.partial(product_kernel, n_seq), out_shape=[jax.S...  1.23 us
  transfers between devices with their start and end apart: 12, of which 10 were waited for; matrix products, arithmetic and copies ran while one was open for 0% of the time, Pallas kernels for 16%

profile of v1, /device:TPU:8, one launch (start us, length us, event | category | flops | bytes accessed | tf_op | source)
XLA Modules:
  0.0 50.1 jit_solution(9364399979402804263)
XLA Ops:
  0.0 1.2 %products.1 = (bf16[256,512]{1,0:T(8,128)(2,1)S(1)}, bf16[272,128]{1,0:T(8,128)(2,1)S(1)}, bf16[272,128]{1,0:T(8,128)(2,1)S(1)}, bf16[272,128]{1,0:T(8,128)(2,1)S(1)}, bf16[272,128]{1,0:T(8,128)(2,1)S(1)}) custom-call(s32[1]{0:T(128)} %bitcast.3.me_ref, bf16[256,512]{1,0:T(8,128)(2,1)} %key_hbm.1, bf16[256,512]{1,0:T(8,128)(2,1)} %value_hbm.1, ...), custom_call_target="tpu_custom_call" | custom-call | tf_op jit(solution)/shard_map/products/pallas_call | solution.py:68
  1.2 1.6 %collective-permute-start = (bf16[272,128]{1,0:T(8,128)(2,1)S(1)}, bf16[272,128]{1,0:T(8,128)(2,1)S(1)}, u32[]{:S(2)}, u32[]{:S(2)}) collective-permute-start(bf16[272,128]{1,0:T(8,128)(2,1)S(1)} %get-tuple-element.19), channel_id=1, source_target_pairs={{0,8},{8,0},{16,24},{24,16},{1,9},{9,1},{17,25},{25,17},{2,10},{10... | collective-permute-start | bytes 208904 | tf_op jit(solution)/shard_map/ppermute | solution.py:329
  2.8 1.5 %collective-permute-start.1 = (bf16[272,128]{1,0:T(8,128)(2,1)S(1)}, bf16[272,128]{1,0:T(8,128)(2,1)S(1)}, u32[]{:S(2)}, u32[]{:S(2)}) collective-permute-start(bf16[272,128]{1,0:T(8,128)(2,1)S(1)} %get-tuple-element.20), channel_id=1, source_target_pairs={{0,16},{8,24},{16,0},{24,8},{1,17},{9,25},{17,1},{25,9},{2,18},{10... | collective-permute-start | bytes 208904 | tf_op jit(solution)/shard_map/ppermute | solution.py:329
  4.3 0.5 collective-permute-start.2
  4.8 0.8 %collective-permute-done.refs_1_ = bf16[272,128]{1,0:T(8,128)(2,1)S(1)} collective-permute-done((bf16[272,128]{1,0:T(8,128)(2,1)S(1)}, bf16[272,128]{1,0:T(8,128)(2,1)S(1)}, u32[]{:S(2)}, u32[]{:S(2)}) %collective-permute-start) | collective-permute-done | bytes 69664 | tf_op jit(solution)/shard_map/ppermute | solution.py:329
  5.6 1.5 %collective-permute-done.1.refs_2_ = bf16[272,128]{1,0:T(8,128)(2,1)S(1)} collective-permute-done((bf16[272,128]{1,0:T(8,128)(2,1)S(1)}, bf16[272,128]{1,0:T(8,128)(2,1)S(1)}, u32[]{:S(2)}, u32[]{:S(2)}) %collective-permute-start.1) | collective-permute-done | bytes 69664 | tf_op jit(solution)/shard_map/ppermute | solution.py:329
  7.1 2.4 %collective-permute-done.2.refs_3_ = bf16[272,128]{1,0:T(8,128)(2,1)S(1)} collective-permute-done((bf16[272,128]{1,0:T(8,128)(2,1)S(1)}, bf16[272,128]{1,0:T(8,128)(2,1)S(1)}, u32[]{:S(2)}, u32[]{:S(2)}) %collective-permute-start.2) | collective-permute-done | bytes 69664 | tf_op jit(solution)/shard_map/ppermute | solution.py:329
  9.5 4.4 %convolve.1 = (bf16[256,128]{1,0:T(8,128)(2,1)S(1)}, bf16[256,128]{1,0:T(8,128)(2,1)S(1)}, bf16[256,128]{1,0:T(8,128)(2,1)S(1)}, bf16[256,128]{1,0:T(8,128)(2,1)S(1)}, bf16[512,2048]{1,0:T(8,128)(2,1)}) custom-call(s32[1]{0:T(128)} %bitcast.3.me_ref, s32[1]{0:T(128)} %bitcast.5.core_ref, bf16[512,4096]{1,0:T(8,128)(2,1)} %weight_hbm.7, ...), custom_call_target="tpu_custom_call" | custom-call | tf_op jit(solution)/shard_map/convolve/pallas_call | solution.py:167
  14.0 0.6 %collective-permute-start.3 = (bf16[256,128]{1,0:T(8,128)(2,1)S(1)}, bf16[256,128]{1,0:T(8,128)(2,1)S(1)}, u32[]{:S(2)}, u32[]{:S(2)}) collective-permute-start(bf16[256,128]{1,0:T(8,128)(2,1)S(1)} %get-tuple-element.23), channel_id=1, source_target_pairs={{0,8},{8,0},{16,24},{24,16},{1,9},{9,1},{17,25},{25,17},{2,10},{10... | collective-permute-start | bytes 196616 | tf_op jit(solution)/shard_map/ppermute | solution.py:329
  14.6 0.5 %collective-permute-start.4 = (bf16[256,128]{1,0:T(8,128)(2,1)S(1)}, bf16[256,128]{1,0:T(8,128)(2,1)S(1)}, u32[]{:S(2)}, u32[]{:S(2)}) collective-permute-start(bf16[256,128]{1,0:T(8,128)(2,1)S(1)} %get-tuple-element.24), channel_id=1, source_target_pairs={{0,16},{8,24},{16,0},{24,8},{1,17},{9,25},{17,1},{25,9},{2,18},{10... | collective-permute-start | bytes 196616 | tf_op jit(solution)/shard_map/ppermute | solution.py:329
  15.1 2.4 %collective-permute-start.5 = (bf16[256,128]{1,0:T(8,128)(2,1)S(1)}, bf16[256,128]{1,0:T(8,128)(2,1)S(1)}, u32[]{:S(2)}, u32[]{:S(2)}) collective-permute-start(bf16[256,128]{1,0:T(8,128)(2,1)S(1)} %get-tuple-element.25), channel_id=1, source_target_pairs={{0,24},{8,16},{16,8},{24,0},{1,25},{9,17},{17,9},{25,1},{2,26},{10... | collective-permute-start | bytes 196616 | tf_op jit(solution)/shard_map/ppermute | solution.py:329
  17.5 1.0 %collective-permute-done.3.refs_1_ = bf16[256,128]{1,0:T(8,128)(2,1)S(1)} collective-permute-done((bf16[256,128]{1,0:T(8,128)(2,1)S(1)}, bf16[256,128]{1,0:T(8,128)(2,1)S(1)}, u32[]{:S(2)}, u32[]{:S(2)}) %collective-permute-start.3) | collective-permute-done | bytes 65568 | tf_op jit(solution)/shard_map/ppermute | solution.py:329
  18.5 1.1 %collective-permute-done.4.refs_2_ = bf16[256,128]{1,0:T(8,128)(2,1)S(1)} collective-permute-done((bf16[256,128]{1,0:T(8,128)(2,1)S(1)}, bf16[256,128]{1,0:T(8,128)(2,1)S(1)}, u32[]{:S(2)}, u32[]{:S(2)}) %collective-permute-start.4) | collective-permute-done | bytes 65568 | tf_op jit(solution)/shard_map/ppermute | solution.py:329
  19.5 0.7 %collective-permute-done.5.refs_3_ = bf16[256,128]{1,0:T(8,128)(2,1)S(1)} collective-permute-done((bf16[256,128]{1,0:T(8,128)(2,1)S(1)}, bf16[256,128]{1,0:T(8,128)(2,1)S(1)}, u32[]{:S(2)}, u32[]{:S(2)}) %collective-permute-start.5) | collective-permute-done | bytes 65568 | tf_op jit(solution)/shard_map/ppermute | solution.py:329
  20.3 0.1 gate.1.own_ref
  20.4 0.1 collective-permute-start.6
  20.5 1.4 %half.1.half_ref = f32[256,512]{1,0:T(8,128)S(1)} custom-call(s32[1]{0:T(128)} %bitcast.11.where_ref, bf16[256,512]{1,0:T(8,128)(2,1)S(1)} %gate.1.own_ref, bf16[512,4096]{1,0:T(8,128)(2,1)} %weight_hbm.7), custom_call_target="tpu_custom_call" | custom-call | tf_op jit(solution)/shard_map/half/pallas_call | solution.py:276
  21.9 0.1 collective-permute-done.6.other_ref
  22.0 1.0 %by_two.1 = bf16[256,512]{1,0:T(8,128)(2,1)} custom-call(s32[1]{0:T(128)} %bitcast.10.chip_ref, f32[256,512]{1,0:T(8,128)S(1)} %half.1.half_ref, bf16[256,512]{1,0:T(8,128)(2,1)S(1)} %collective-permute-done.6.other_ref, bf16[512,2048]{1,0:T(8,128)(2,1)S(1)} %collective-permute-done.7.other_weight.weight_ref), custom_call_target="tpu_custom_call" | custom-call | tf_op jit(solution)/shard_map/by_two/pallas_call | solution.py:276
  23.0 2.6 %collective-permute-start.9 = (bf16[256,512]{1,0:T(8,128)(2,1)}, bf16[256,512]{1,0:T(8,128)(2,1)S(1)}, u32[]{:S(2)}, u32[]{:S(2)}) collective-permute-start(bf16[256,512]{1,0:T(8,128)(2,1)} %by_two.1), channel_id=1, source_target_pairs={{0,2},{1,3},{6,4},{7,5},{2,6},{3,7},{4,0},{5,1},{8,10},{9,11},{14,... | collective-permute-start | bytes 786440 | tf_op jit(solution)/shard_map/ppermute | solution.py:332
  25.6 0.1 pad_add_fusion.1.where_ref
  25.7 3.2 %by_three_and_one.1 = (bf16[256,512]{1,0:T(8,128)(2,1)S(1)}, bf16[256,512]{1,0:T(8,128)(2,1)}) custom-call(s32[4]{0:T(128)S(1)} %pad_add_fusion.1.where_ref, bf16[256,512]{1,0:T(8,128)(2,1)S(1)} %gate.1.own_ref, bf16[256,512]{1,0:T(8,128)(2,1)S(1)} %collective-permute-done.6.other_ref, bf16[512,4096]{1,0:T(8,128)(2,1)} %weight_hbm.7, ...), custom_call_target="tpu_custom_call" | custom-call | tf_op jit(solution)/shard_map/by_three_and_one/pallas_call | solution.py:276
  28.9 0.1 collective-permute-start.8
  29.0 0.7 %collective-permute-start.10 = (bf16[256,512]{1,0:T(8,128)(2,1)S(1)}, bf16[256,512]{1,0:T(8,128)(2,1)S(1)}, u32[]{:S(2)}, u32[]{:S(2)}) collective-permute-start(bf16[256,512]{1,0:T(8,128)(2,1)S(1)} %get-tuple-element.28.own_ref), channel_id=1, source_target_pairs={{0,6},{1,7},{6,0},{7,1},{8,14},{9,15},{14,8},{15,9},{16,22},{17,23... | collective-permute-start | bytes 786440 | tf_op jit(solution)/shard_map/ppermute | solution.py:332
  29.7 2.4 %collective-permute-done.9.first_ref.arrived_ref = bf16[256,512]{1,0:T(8,128)(2,1)S(1)} collective-permute-done((bf16[256,512]{1,0:T(8,128)(2,1)}, bf16[256,512]{1,0:T(8,128)(2,1)S(1)}, u32[]{:S(2)}, u32[]{:S(2)}) %collective-permute-start.9) | collective-permute-done | bytes 262176 | tf_op jit(solution)/shard_map/ppermute | solution.py:332
  32.0 0.8 %forward.1 = bf16[256,512]{1,0:T(8,128)(2,1)} custom-call(bf16[256,512]{1,0:T(8,128)(2,1)S(1)} %get-tuple-element.28.own_ref, bf16[256,512]{1,0:T(8,128)(2,1)S(1)} %collective-permute-done.9.first_ref.arrived_ref), custom_call_target="tpu_custom_call" | custom-call | tf_op jit(solution)/shard_map/forward/pallas_call | solution.py:276
  32.8 3.8 %collective-permute-start.11 = (bf16[256,512]{1,0:T(8,128)(2,1)}, bf16[256,512]{1,0:T(8,128)(2,1)}, u32[]{:S(2)}, u32[]{:S(2)}) collective-permute-start(bf16[256,512]{1,0:T(8,128)(2,1)} %forward.1), channel_id=1, source_target_pairs={{2,4},{3,5},{4,2},{5,3},{10,12},{11,13},{12,10},{13,11},{18,20},{1... | collective-permute-start | bytes 786440 | tf_op jit(solution)/shard_map/ppermute | solution.py:332
  36.6 0.1 pad_add_fusion.where_ref
  36.7 1.8 %collective-permute-done.8.pair_ref = bf16[256,512]{1,0:T(8,128)(2,1)} collective-permute-done((bf16[256,512]{1,0:T(8,128)(2,1)}, bf16[256,512]{1,0:T(8,128)(2,1)}, u32[]{:S(2)}, u32[]{:S(2)}) %collective-permute-start.8) | collective-permute-done | bytes 262176 | tf_op jit(solution)/shard_map/ppermute | solution.py:332
  38.5 2.5 %base.1.base_ref = f32[256,512]{1,0:T(8,128)S(1)} custom-call(s32[3]{0:T(128)S(1)} %pad_add_fusion.where_ref, bf16[256,512]{1,0:T(8,128)(2,1)S(1)} %gate.1.own_ref, bf16[256,512]{1,0:T(8,128)(2,1)S(1)} %collective-permute-done.6.other_ref, bf16[512,4096]{1,0:T(8,128)(2,1)} %weight_hbm.7, ...), custom_call_target="tpu_custom_call" | custom-call | tf_op jit(solution)/shard_map/base/pallas_call | solution.py:276
  41.0 7.4 %collective-permute-done.11.middle_hbm = bf16[256,512]{1,0:T(8,128)(2,1)} collective-permute-done((bf16[256,512]{1,0:T(8,128)(2,1)}, bf16[256,512]{1,0:T(8,128)(2,1)}, u32[]{:S(2)}, u32[]{:S(2)}) %collective-permute-start.11) | collective-permute-done | bytes 262176 | tf_op jit(solution)/shard_map/ppermute | solution.py:332
  48.4 1.7 %final.1 = bf16[256,512]{1,0:T(8,128)(2,1)} custom-call(s32[1]{0:T(128)} %bitcast.end_ref, f32[256,512]{1,0:T(8,128)S(1)} %base.1.base_ref, bf16[256,512]{1,0:T(8,128)(2,1)S(1)} %collective-permute-done.10.ends_hbm, bf16[256,512]{1,0:T(8,128)(2,1)} %collective-permute-done.11.middle_hbm), custom_call_target="tpu_custom_call" | custom-call | tf_op jit(solution)/shard_map/final/pallas_call | solution.py:307
  (7 shorter events, 0.1 us)
Async XLA Ops:
  1.2 4.4 %collective-permute-start = (bf16[272,128]{1,0:T(8,128)(2,1)S(1)}, bf16[272,128]{1,0:T(8,128)(2,1)S(1)}, u32[]{:S(2)}, u32[]{:S(2)}) collective-permute-start(bf16[272,128]{1,0:T(8,128)(2,1)S(1)} %get-tuple-element.19), channel_id=1, source_target_pairs={{0,8},{8,0},{16,24},{24,16},{1,9},{9,1},{17,25},{25,17},{2,10},{10... | collective-permute-start | bytes 208904 | tf_op jit(solution)/shard_map/ppermute | solution.py:329
  2.8 4.3 %collective-permute-start.1 = (bf16[272,128]{1,0:T(8,128)(2,1)S(1)}, bf16[272,128]{1,0:T(8,128)(2,1)S(1)}, u32[]{:S(2)}, u32[]{:S(2)}) collective-permute-start(bf16[272,128]{1,0:T(8,128)(2,1)S(1)} %get-tuple-element.20), channel_id=1, source_target_pairs={{0,16},{8,24},{16,0},{24,8},{1,17},{9,25},{17,1},{25,9},{2,18},{10... | collective-permute-start | bytes 208904 | tf_op jit(solution)/shard_map/ppermute | solution.py:329
  4.3 5.2 %collective-permute-start.2 = (bf16[272,128]{1,0:T(8,128)(2,1)S(1)}, bf16[272,128]{1,0:T(8,128)(2,1)S(1)}, u32[]{:S(2)}, u32[]{:S(2)}) collective-permute-start(bf16[272,128]{1,0:T(8,128)(2,1)S(1)} %get-tuple-element.21), channel_id=1, source_target_pairs={{0,24},{8,16},{16,8},{24,0},{1,25},{9,17},{17,9},{25,1},{2,26},{10... | collective-permute-start | bytes 208904 | tf_op jit(solution)/shard_map/ppermute | solution.py:329
  9.5 10.7 %copy-start = (bf16[256,512]{1,0:T(8,128)(2,1)S(1)}, bf16[256,512]{1,0:T(8,128)(2,1)}, u32[]{:S(2)}) copy-start(bf16[256,512]{1,0:T(8,128)(2,1)} %query_ref.1) | copy-start | bytes 786436
  9.5 10.7 %copy-start.1 = (f32[512]{0:T(512)S(1)}, f32[512]{0:T(512)}, u32[]{:S(2)}) copy-start(f32[512]{0:T(512)} %param.10) | copy-start | bytes 6148
  13.9 8.1 %collective-permute-start.7 = (bf16[512,2048]{1,0:T(8,128)(2,1)}, bf16[512,2048]{1,0:T(8,128)(2,1)S(1)}, u32[]{:S(2)}, u32[]{:S(2)}) collective-permute-start(bf16[512,2048]{1,0:T(8,128)(2,1)} %get-tuple-element.26), channel_id=1, source_target_pairs={{0,1},{1,0},{2,3},{3,2},{4,5},{5,4},{6,7},{7,6},{8,9},{9,8},{10,11... | collective-permute-start | bytes 6291464 | tf_op jit(solution)/shard_map/ppermute | solution.py:337
  14.0 4.5 %collective-permute-start.3 = (bf16[256,128]{1,0:T(8,128)(2,1)S(1)}, bf16[256,128]{1,0:T(8,128)(2,1)S(1)}, u32[]{:S(2)}, u32[]{:S(2)}) collective-permute-start(bf16[256,128]{1,0:T(8,128)(2,1)S(1)} %get-tuple-element.23), channel_id=1, source_target_pairs={{0,8},{8,0},{16,24},{24,16},{1,9},{9,1},{17,25},{25,17},{2,10},{10... | collective-permute-start | bytes 196616 | tf_op jit(solution)/shard_map/ppermute | solution.py:329
  14.6 5.0 %collective-permute-start.4 = (bf16[256,128]{1,0:T(8,128)(2,1)S(1)}, bf16[256,128]{1,0:T(8,128)(2,1)S(1)}, u32[]{:S(2)}, u32[]{:S(2)}) collective-permute-start(bf16[256,128]{1,0:T(8,128)(2,1)S(1)} %get-tuple-element.24), channel_id=1, source_target_pairs={{0,16},{8,24},{16,0},{24,8},{1,17},{9,25},{17,1},{25,9},{2,18},{10... | collective-permute-start | bytes 196616 | tf_op jit(solution)/shard_map/ppermute | solution.py:329
  15.1 5.2 %collective-permute-start.5 = (bf16[256,128]{1,0:T(8,128)(2,1)S(1)}, bf16[256,128]{1,0:T(8,128)(2,1)S(1)}, u32[]{:S(2)}, u32[]{:S(2)}) collective-permute-start(bf16[256,128]{1,0:T(8,128)(2,1)S(1)} %get-tuple-element.25), channel_id=1, source_target_pairs={{0,24},{8,16},{16,8},{24,0},{1,25},{9,17},{17,9},{25,1},{2,26},{10... | collective-permute-start | bytes 196616 | tf_op jit(solution)/shard_map/ppermute | solution.py:329
  20.4 1.6 %collective-permute-start.6 = (bf16[256,512]{1,0:T(8,128)(2,1)S(1)}, bf16[256,512]{1,0:T(8,128)(2,1)S(1)}, u32[]{:S(2)}, u32[]{:S(2)}) collective-permute-start(bf16[256,512]{1,0:T(8,128)(2,1)S(1)} %gate.1.own_ref), channel_id=1, source_target_pairs={{0,1},{1,0},{2,3},{3,2},{4,5},{5,4},{6,7},{7,6},{8,9},{9,8},{10,11... | collective-permute-start | bytes 786440 | tf_op jit(solution)/shard_map/ppermute | solution.py:337
  23.0 9.0 %collective-permute-start.9 = (bf16[256,512]{1,0:T(8,128)(2,1)}, bf16[256,512]{1,0:T(8,128)(2,1)S(1)}, u32[]{:S(2)}, u32[]{:S(2)}) collective-permute-start(bf16[256,512]{1,0:T(8,128)(2,1)} %by_two.1), channel_id=1, source_target_pairs={{0,2},{1,3},{6,4},{7,5},{2,6},{3,7},{4,0},{5,1},{8,10},{9,11},{14,... | collective-permute-start | bytes 786440 | tf_op jit(solution)/shard_map/ppermute | solution.py:332
  28.9 9.5 %collective-permute-start.8 = (bf16[256,512]{1,0:T(8,128)(2,1)}, bf16[256,512]{1,0:T(8,128)(2,1)}, u32[]{:S(2)}, u32[]{:S(2)}) collective-permute-start(bf16[256,512]{1,0:T(8,128)(2,1)} %get-tuple-element.27), channel_id=1, source_target_pairs={{0,2},{1,3},{2,0},{3,1},{4,6},{5,7},{6,4},{7,5},{8,10},{9,11},{10,... | collective-permute-start | bytes 786440 | tf_op jit(solution)/shard_map/ppermute | solution.py:332
  29.0 12.0 %collective-permute-start.10 = (bf16[256,512]{1,0:T(8,128)(2,1)S(1)}, bf16[256,512]{1,0:T(8,128)(2,1)S(1)}, u32[]{:S(2)}, u32[]{:S(2)}) collective-permute-start(bf16[256,512]{1,0:T(8,128)(2,1)S(1)} %get-tuple-element.28.own_ref), channel_id=1, source_target_pairs={{0,6},{1,7},{6,0},{7,1},{8,14},{9,15},{14,8},{15,9},{16,22},{17,23... | collective-permute-start | bytes 786440 | tf_op jit(solution)/shard_map/ppermute | solution.py:332
  32.8 15.6 %collective-permute-start.11 = (bf16[256,512]{1,0:T(8,128)(2,1)}, bf16[256,512]{1,0:T(8,128)(2,1)}, u32[]{:S(2)}, u32[]{:S(2)}) collective-permute-start(bf16[256,512]{1,0:T(8,128)(2,1)} %forward.1), channel_id=1, source_target_pairs={{2,4},{3,5},{4,2},{5,3},{10,12},{11,13},{12,10},{13,11},{18,20},{1... | collective-permute-start | bytes 786440 | tf_op jit(solution)/shard_map/ppermute | solution.py:332

commit v2 on v1

v2 whole, which is shorter than its diff:
```python
import functools
import math

import jax
import jax.numpy as jnp
from jax import lax
from jax.experimental import pallas as pl
from jax.experimental.pallas import tpu as pltpu
from jax.sharding import PartitionSpec as P

LANES = 128
BF16 = jnp.bfloat16
F32 = jnp.float32
VMEM_LIMIT = 16 * 1024 * 1024


def params():
    return pltpu.CompilerParams(vmem_limit_bytes=VMEM_LIMIT)


def in_hbm(*arrays):
    return [pltpu.with_memory_space_constraint(a, pltpu.HBM) for a in arrays]


def in_vmem(*arrays):
    return [pltpu.with_memory_space_constraint(a, pltpu.VMEM) for a in arrays]


def seq_place():
    return lax.axis_index("seq")


def chip_place():
    return lax.axis_index("chan") // 2


def core_place():
    return lax.axis_index("chan") % 2


def lanes_at(block):
    return pl.ds(pl.multiple_of(block * LANES, LANES), LANES)


def rows_at(block, size):
    return pl.ds(pl.multiple_of(block * size, size), size)


def product_kernel(n_seq, key_hbm, value_hbm, taps_hbm, query_hbm, skip_hbm, *refs):
    mixed_ref, query_ref, skip_ref, *packed_refs = refs[: n_seq + 3]
    key_ref, value_ref, taps_ref, taps_f32, arrived = refs[n_seq + 3 :]
    rows = key_ref.shape[0]
    groups, span = taps_ref.shape
    part = groups // n_seq
    loads = [
        pltpu.make_async_copy(source, target, arrived.at[i])
        for i, (source, target) in enumerate(
            [
                (taps_hbm, taps_ref),
                (key_hbm, key_ref),
                (value_hbm, value_ref),
                (query_hbm, query_ref),
                (skip_hbm, skip_ref),
            ]
        )
    ]
    for load in loads:
        load.start()
    loads[0].wait()
    taps_f32[...] = taps_ref[...].astype(F32)
    for d in range(n_seq):
        own = taps_f32[rows_at(seq_place() ^ d, part), :]
        pieces = [own[:, k * LANES : (k + 1) * LANES] for k in range(span // LANES)]
        packed_refs[d][rows:, :] = jnp.concatenate(pieces, axis=0).astype(BF16)
    loads[1].wait()
    loads[2].wait()
    mixed_ref[...] = (key_ref[...].astype(F32) * value_ref[...].astype(F32)).astype(BF16)
    for d in range(n_seq):
        packed_refs[d][0:rows, :] = mixed_ref[:, lanes_at(seq_place() ^ d)]
    loads[3].wait()
    loads[4].wait()


def products(key_in, value_in, taps, query_in, skip_gain, n_seq):
    rows, width = key_in.shape
    groups, span = taps.shape
    tap_rows = (groups // n_seq) * (span // LANES)
    here = jax.ShapeDtypeStruct((rows, width), BF16)
    packed = jax.ShapeDtypeStruct((rows + tap_rows, LANES), BF16)
    return pl.pallas_call(
        functools.partial(product_kernel, n_seq),
        out_shape=[here, here, jax.ShapeDtypeStruct((1, width), F32)] + [packed] * n_seq,
        in_specs=[pl.BlockSpec(memory_space=pl.ANY)] * 5,
        out_specs=[pl.BlockSpec(memory_space=pltpu.VMEM)] * (n_seq + 3),
        scratch_shapes=[
            pltpu.VMEM((rows, width), BF16),
            pltpu.VMEM((rows, width), BF16),
            pltpu.VMEM((groups, span), BF16),
            pltpu.VMEM((groups, span), F32),
            pltpu.SemaphoreType.DMA((5,)),
        ],
        compiler_params=params(),
        name="products",
    )(*in_hbm(key_in, value_in, taps, query_in, skip_gain.reshape(1, -1)))


def conv_kernel(n_seq, rows, part, *refs):
    packed_refs = refs[:n_seq]
    out_refs = refs[n_seq : 2 * n_seq]
    signal, tap_rows, lag_blocks, total = refs[2 * n_seq :]
    per_shard = rows // LANES
    tiles = n_seq * per_shard
    group_width = LANES // part

    for d in range(n_seq):
        other = seq_place() ^ d
        signal[rows_at(other, rows), :] = packed_refs[d][0:rows, :]
        tap_rows[rows_at(other, part * per_shard), :] = packed_refs[d][rows:, :].astype(F32)

    from_lane = lax.broadcasted_iota(jnp.int32, (LANES, LANES), 0)
    to_lane = lax.broadcasted_iota(jnp.int32, (LANES, LANES), 1)
    flip = jnp.where((from_lane + to_lane) % LANES == 0, 1.0, 0.0).astype(BF16)
    tap_rows[...] = jnp.dot(tap_rows[...].astype(BF16), flip, preferred_element_type=F32)

    lower = to_lane <= from_lane
    zero_block = jnp.zeros((LANES, LANES), BF16)

    for g in range(part):
        lag_blocks[0:LANES, (2 * g + 1) * LANES : (2 * g + 2) * LANES] = zero_block
        before = jnp.zeros((LANES, LANES), F32)
        for k in range(tiles):
            row = tap_rows[k * part + g : k * part + g + 1, :]
            rolled = pltpu.roll(
                jnp.broadcast_to(row, (LANES, LANES)), 0, 1, stride=1, stride_axis=0
            )
            block = jnp.where(lower, rolled, before).astype(BF16)
            lag_blocks[k * LANES : (k + 1) * LANES, 2 * g * LANES : (2 * g + 1) * LANES] = block
            if k + 1 < tiles:
                lag_blocks[
                    (k + 1) * LANES : (k + 2) * LANES, (2 * g + 1) * LANES : (2 * g + 2) * LANES
                ] = block
            before = rolled

    step = 2 * LANES
    length = n_seq * rows
    lane_group = lax.broadcasted_iota(jnp.int32, (step, LANES), 1) // group_width
    total[...] = jnp.zeros_like(total)
    for first in range(0, length, 2 * step):
        left = signal[first : first + step, :]
        right = signal[first + step : first + 2 * step, :]
        masked = []
        for g in range(part):
            here = lane_group == g
            masked.append(
                jnp.concatenate(
                    [jnp.where(here, left, 0.0).astype(BF16), jnp.where(here, right, 0.0).astype(BF16)],
                    axis=1,
                )
            )
        both = jnp.dot(
            lag_blocks[0 : length - first, :],
            jnp.concatenate(masked, axis=0),
            preferred_element_type=F32,
        )
        total[first:length, :] += both[:, 0:LANES]
        total[first + step : length, :] += both[0 : length - first - step, LANES:]

    for d in range(n_seq):
        out_refs[d][...] = total[rows_at(seq_place() ^ d, rows), :].astype(BF16)


def convolve(packed, n_seq, rows, part):
    tiles = n_seq * rows // LANES
    vmem = pl.BlockSpec(memory_space=pltpu.VMEM)
    return pl.pallas_call(
        functools.partial(conv_kernel, n_seq, rows, part),
        out_shape=[jax.ShapeDtypeStruct((rows, LANES), BF16)] * n_seq,
        in_specs=[vmem] * n_seq,
        out_specs=[vmem] * n_seq,
        scratch_shapes=[
            pltpu.VMEM((n_seq * rows, LANES), BF16),
            pltpu.VMEM((tiles * part, LANES), F32),
            pltpu.VMEM((n_seq * rows, 2 * LANES * part), BF16),
            pltpu.VMEM((n_seq * rows, LANES), F32),
        ],
        compiler_params=params(),
        name="convolve",
    )(*packed)


def gate_kernel(n_seq, query_ref, mixed_ref, skip_ref, *refs):
    conv_refs, out_ref = refs[:n_seq], refs[n_seq]
    for d in range(n_seq):
        lanes = lanes_at(seq_place() ^ d)
        direct = skip_ref[:, lanes] * mixed_ref[:, lanes].astype(F32)
        out_ref[:, lanes] = (
            query_ref[:, lanes].astype(F32) * (conv_refs[d][...].astype(F32) + direct)
        ).astype(BF16)


def gate(query_in, mixed_in, skip_gain, parts):
    vmem = pl.BlockSpec(memory_space=pltpu.VMEM)
    return pl.pallas_call(
        functools.partial(gate_kernel, len(parts)),
        out_shape=jax.ShapeDtypeStruct(query_in.shape, BF16),
        in_specs=[vmem] * (3 + len(parts)),
        out_specs=vmem,
        compiler_params=params(),
        name="gate",
    )(query_in, mixed_in, skip_gain, *parts)


def load_block(distance, weight_hbm, weight, arrived):
    block = rows_at(2 * (chip_place() ^ distance) + core_place(), weight.shape[1])
    load = pltpu.make_async_copy(weight_hbm.at[:, block], weight, arrived)
    load.start()
    return block, load


def half_kernel(own_ref, own_weight, out_ref, weight, arrived):
    load_block(2, own_weight, weight, arrived)[1].wait()
    out_ref[...] = jnp.dot(own_ref[...], weight[...], preferred_element_type=F32)


def add_half_kernel(half_ref, other_ref, other_weight, out_ref):
    block = rows_at(2 * (chip_place() ^ 2) + core_place(), out_ref.shape[1])
    late = jnp.dot(other_ref[...], other_weight[:, block], preferred_element_type=F32)
    out_ref[...] = (half_ref[...] + late).astype(BF16)


def both_halves(distance, own_ref, other_ref, own_weight, other_weight, weight, arrived):
    block, load = load_block(distance, own_weight, weight, arrived)
    late = jnp.dot(other_ref[...], other_weight[:, block], preferred_element_type=F32)
    load.wait()
    return late + jnp.dot(own_ref[...], weight[...], preferred_element_type=F32)


def block_kernel(distance, own_ref, other_ref, own_weight, other_weight, *refs):
    out_ref, weight, arrived = refs[-3:]
    out_ref[...] = both_halves(
        distance, own_ref, other_ref, own_weight, other_weight, weight, arrived
    ).astype(BF16)


def is_end():
    return (chip_place() == 0) | (chip_place() == 3)


def base_kernel(own_ref, other_ref, own_weight, other_weight, first_ref, *refs):
    early_refs, (out_ref, weight, arrived) = refs[:-3], refs[-3:]
    base = both_halves(0, own_ref, other_ref, own_weight, other_weight, weight, arrived)
    for early in early_refs:
        base += early[...].astype(F32)

    @pl.when(is_end())
    def _():
        out_ref[...] = base + first_ref[...].astype(F32)

    @pl.when(jnp.logical_not(is_end()))
    def _():
        out_ref[...] = base


def run_kernel(kernel, name, out_shape, scratch, *arrays, hbm=()):
    specs, given = [], []
    for i, array in enumerate(arrays):
        space = pl.ANY if i in hbm else pltpu.VMEM
        specs.append(pl.BlockSpec(memory_space=space))
        given += in_hbm(array) if i in hbm else [array]
    vmem = pl.BlockSpec(memory_space=pltpu.VMEM)
    return pl.pallas_call(
        kernel,
        out_shape=out_shape,
        in_specs=specs,
        out_specs=[vmem] * len(out_shape) if isinstance(out_shape, list) else vmem,
        scratch_shapes=scratch,
        compiler_params=params(),
        name=name,
    )(*given)


def forward_kernel(own_ref, arrived_ref, out_ref):
    @pl.when(is_end())
    def _():
        out_ref[...] = own_ref[...]

    @pl.when(jnp.logical_not(is_end()))
    def _():
        out_ref[...] = (own_ref[...].astype(F32) + arrived_ref[...].astype(F32)).astype(BF16)


def final_kernel(base_ref, pair_ref, mirror_ref, out_ref):
    arrived = pair_ref[...].astype(F32) + mirror_ref[...].astype(F32)
    out_ref[...] = (base_ref[...] + arrived).astype(BF16)


def fast_body(n_seq, n_chan, query_in, key_in, value_in, filter_taps, skip_gain, out_weight):
    rows, width = query_in.shape
    groups = filter_taps.shape[0]
    part = groups // n_seq
    columns = out_weight.shape[1] // n_chan
    def over_seq(value, d):
        return lax.ppermute(value, "seq", [(i, i ^ d) for i in range(n_seq)])

    def over_chips(value, moves):
        return lax.ppermute(
            value, "chan", [(2 * a + c, 2 * b + c) for a, b in moves for c in range(2)]
        )

    def other_core(value):
        return lax.ppermute(value, "chan", [(i, i ^ 1) for i in range(n_chan)])

    other_weight = other_core(out_weight)
    mixed_in, query, skip, *packed = products(
        key_in, value_in, filter_taps, query_in, skip_gain, n_seq
    )
    arrived = [packed[0]] + [over_seq(packed[d], d) for d in range(1, n_seq)]
    convolved = convolve(arrived, n_seq, rows, part)
    returned = [convolved[0]] + [over_seq(convolved[d], d) for d in range(1, n_seq)]
    gated = gate(query, mixed_in, skip, returned)
    gated_other = other_core(gated)

    block = jax.ShapeDtypeStruct((rows, columns), BF16)
    block_f32 = jax.ShapeDtypeStruct((rows, columns), F32)
    one_weight = [pltpu.VMEM((width, columns), BF16), pltpu.SemaphoreType.DMA(())]
    halves = (gated, gated_other, out_weight, other_weight)

    half = run_kernel(half_kernel, "half", block_f32, one_weight, gated, out_weight, hbm=(1,))
    by_two = run_kernel(add_half_kernel, "by_two", block, [], half, gated_other, other_weight)
    first = over_chips(by_two, [(0, 1), (3, 2), (1, 3), (2, 0)])
    by_one = run_kernel(
        functools.partial(block_kernel, 1), "by_one", block, one_weight, *halves, hbm=(2,)
    )
    pair = over_chips(by_one, [(0, 1), (1, 0), (2, 3), (3, 2)])
    by_three = run_kernel(
        functools.partial(block_kernel, 3), "by_three", block, one_weight, *halves, hbm=(2,)
    )
    summed = run_kernel(forward_kernel, "forward", block, [], by_three, first)
    mirror = over_chips(summed, [(0, 3), (3, 0), (1, 2), (2, 1)])
    base = run_kernel(base_kernel, "base", block_f32, one_weight, *halves, first, hbm=(2,))
    return run_kernel(final_kernel, "final", block, [], base, pair, mirror)


def window_matrix(window, tile_size):
    reversed_window = window[:, ::-1]
    extended = jnp.concatenate(
        [reversed_window, jnp.zeros((window.shape[0], 1), window.dtype)], axis=1
    )
    repeated = jnp.tile(extended, (1, tile_size))[:, : tile_size * (2 * tile_size - 1)]
    return repeated.reshape(window.shape[0], tile_size, 2 * tile_size - 1)[:, :, tile_size - 1 :]


def accumulate(running, segment, tap_table, own_start):
    row_count, chan_width = running.shape
    group_count = tap_table.shape[0]
    tap_span = tap_table.shape[1] // 2
    group_width = chan_width // group_count
    block_rows = min(segment.shape[0], row_count)
    tile_size = math.gcd(math.gcd(block_rows, row_count), 128)
    out_tiles = row_count // tile_size
    in_tiles = block_rows // tile_size

    def one_block(step_index, current):
        block_start = step_index * block_rows
        in_blocks = lax.dynamic_slice_in_dim(segment, step_index * block_rows, block_rows, 0)
        in_blocks = in_blocks.reshape(in_tiles, tile_size, group_count, group_width)

        def add_block(previous):
            out_blocks = previous.reshape(out_tiles, tile_size, group_count, group_width)
            offset = own_start - block_start
            for lag_step in range(1 - in_tiles, out_tiles):
                tap_first = offset + lag_step * tile_size - (tile_size - 1) + tap_span
                window = lax.dynamic_slice_in_dim(tap_table, tap_first, 2 * tile_size - 1, 1)
                matrix = window_matrix(window, tile_size)
                first_out = max(0, lag_step)
                last_out = min(out_tiles, in_tiles + lag_step)
                addend = jnp.einsum(
                    "gij,qjgc->qigc",
                    matrix,
                    in_blocks[first_out - lag_step : last_out - lag_step],
                    preferred_element_type=jnp.float32,
                )
                out_blocks = out_blocks.at[first_out:last_out].add(addend)
            return out_blocks.reshape(previous.shape)

        def keep_same(previous):
            return previous

        needed = (block_start < own_start + row_count) & (block_start >= 0)
        return lax.cond(needed, add_block, keep_same, current)

    return lax.fori_loop(0, segment.shape[0] // block_rows, one_block, running)


def general_body(query_in, key_in, value_in, filter_taps, skip_gain, out_weight):
    row_count, chan_width = query_in.shape
    mixed_in = (key_in.astype(jnp.float32) * value_in.astype(jnp.float32)).astype(jnp.bfloat16)
    all_taps = lax.all_gather(filter_taps, "seq", axis=1, tiled=True)
    tap_table = jnp.concatenate([jnp.zeros_like(all_taps), all_taps], axis=1)
    seq_index = lax.axis_index("seq")
    own_start = seq_index * row_count
    zero_sum = jnp.zeros((row_count, chan_width), jnp.float32)
    convolved = accumulate(
        zero_sum, lax.all_gather(mixed_in, "seq", axis=0, tiled=True), tap_table, own_start
    )
    gated = (
        query_in.astype(jnp.float32)
        * (convolved + skip_gain[None, :] * mixed_in.astype(jnp.float32))
    ).astype(jnp.bfloat16)
    columns = lax.all_to_all(out_weight, "chan", split_axis=1, concat_axis=0, tiled=True)
    result = jnp.dot(
        lax.all_gather(gated, "chan", axis=1, tiled=True),
        columns,
        preferred_element_type=jnp.float32,
    )
    return result.astype(jnp.bfloat16)


def solution(mesh):
    n_seq, n_chan = mesh.shape["seq"], mesh.shape["chan"]

    def body(query_in, key_in, value_in, filter_taps, skip_gain, out_weight):
        rows, width = query_in.shape
        groups, span = filter_taps.shape
        part = groups // n_seq
        fits = (
            n_chan == 8
            and n_seq & (n_seq - 1) == 0
            and width == n_seq * LANES
            and part * n_seq == groups
            and part % 8 == 0
            and (part * (rows // LANES)) % 16 == 0
            and rows % (2 * LANES) == 0
            and (n_seq * rows) % (4 * LANES) == 0
            and span == rows
            and out_weight.shape[1] % (n_chan * LANES) == 0
        )
        run = functools.partial(fast_body, n_seq, n_chan) if fits else general_body
        return run(query_in, key_in, value_in, filter_taps, skip_gain, out_weight)

    placed = (
        P("seq", "chan"),
        P("seq", "chan"),
        P("seq", "chan"),
        P("chan", "seq"),
        P("chan"),
        P("chan", None),
    )
    return jax.shard_map(
        body, mesh=mesh, in_specs=placed, out_specs=P("seq", "chan"), check_vma=False
    )
```

time: 50.4 us -> 44.8 us (0.89)
  the two profiles are of different devices: /device:TPU:8 before, /device:TPU:0 now
where the time goes in v2:
time: 44.8 us; the launch traced here: 44.5 us
  waiting for transfers between devices  17.6 us (39%)
  starting transfers between devices  16.1 us (36%)
  Pallas kernels  10.7 us (24%)
    ppermute x3, waiting for transfers between devices, over_chips(): lax.ppermute(value, 'chan', [(2 * a + c, 2 * b + c) for a, b in moves for...  9.43 us
    ppermute x6, waiting for transfers between devices, over_seq(): return lax.ppermute(value, 'seq', [(i, i ^ d) for i in range(n_seq)])  8.02 us
    ppermute x3, starting transfers between devices, over_chips(): lax.ppermute(value, 'chan', [(2 * a + c, 2 * b + c) for a, b in moves for...  7.96 us
    ppermute x6, starting transfers between devices, over_seq(): return lax.ppermute(value, 'seq', [(i, i ^ d) for i in range(n_seq)])  7.65 us
    pallas_call x7, Pallas kernels, run_kernel(): pl.pallas_call(kernel, out_shape=out_shape, in_specs=specs, out_specs=[vm...  7.02 us
    pallas_call x1, Pallas kernels, convolve(): pl.pallas_call(functools.partial(conv_kernel, n_seq, rows, part), out_sha...  2.24 us
    pallas_call x1, Pallas kernels, products(): pl.pallas_call(functools.partial(product_kernel, n_seq), out_shape=[here,...  1.26 us
  transfers between devices with their start and end apart: 11, of which 10 were waited for; matrix products, arithmetic and copies ran while one was open for 0% of the time, Pallas kernels for 22%

profile of v2, /device:TPU:0, one launch (start us, length us, event | category | flops | bytes accessed | tf_op | source)
XLA Modules:
  0.0 44.5 jit_solution(13120379806486691176)
XLA Ops:
  0.0 0.5 %collective-permute-start.7 = (bf16[512,4096]{1,0:T(8,128)(2,1)}, bf16[512,4096]{1,0:T(8,128)(2,1)S(1)}, u32[]{:S(2)}, u32[]{:S(2)}) collective-permute-start(bf16[512,4096]{1,0:T(8,128)(2,1)} %own_weight.7), channel_id=1, source_target_pairs={{0,1},{1,0},{2,3},{3,2},{4,5},{5,4},{6,7},{7,6},{8,9},{9,8},{10,11... | collective-permute-start | bytes 12582920 | tf_op jit(solution)/shard_map/ppermute | solution.py:311
  0.5 1.3 %products.1 = (bf16[256,512]{1,0:T(8,128)(2,1)S(1)}, bf16[256,512]{1,0:T(8,128)(2,1)S(1)}, f32[1,512]{1,0:T(1,128)S(1)}, bf16[272,128]{1,0:T(8,128)(2,1)S(1)}, b...) custom-call(bf16[256,512]{1,0:T(8,128)(2,1)} %key_hbm.1, ...), custom_call_target="tpu_custom_call" | custom-call | tf_op jit(solution)/shard_map/products/pallas_call | solution.py:90
  1.7 2.6 %collective-permute-start = (bf16[272,128]{1,0:T(8,128)(2,1)S(1)}, bf16[272,128]{1,0:T(8,128)(2,1)S(1)}, u32[]{:S(2)}, u32[]{:S(2)}) collective-permute-start(bf16[272,128]{1,0:T(8,128)(2,1)S(1)} %get-tuple-element.20), channel_id=1, source_target_pairs={{0,8},{8,0},{16,24},{24,16},{1,9},{9,1},{17,25},{25,17},{2,10},{10... | collective-permute-start | bytes 208904 | tf_op jit(solution)/shard_map/ppermute | solution.py:303
  4.3 1.5 %collective-permute-start.1 = (bf16[272,128]{1,0:T(8,128)(2,1)S(1)}, bf16[272,128]{1,0:T(8,128)(2,1)S(1)}, u32[]{:S(2)}, u32[]{:S(2)}) collective-permute-start(bf16[272,128]{1,0:T(8,128)(2,1)S(1)} %get-tuple-element.21), channel_id=1, source_target_pairs={{0,16},{8,24},{16,0},{24,8},{1,17},{9,25},{17,1},{25,9},{2,18},{10... | collective-permute-start | bytes 208904 | tf_op jit(solution)/shard_map/ppermute | solution.py:303
  5.8 0.0 collective-permute-start.2
  5.8 1.3 %collective-permute-done.refs_1_ = bf16[272,128]{1,0:T(8,128)(2,1)S(1)} collective-permute-done((bf16[272,128]{1,0:T(8,128)(2,1)S(1)}, bf16[272,128]{1,0:T(8,128)(2,1)S(1)}, u32[]{:S(2)}, u32[]{:S(2)}) %collective-permute-start) | collective-permute-done | bytes 69664 | tf_op jit(solution)/shard_map/ppermute | solution.py:303
  7.1 1.5 %collective-permute-done.1.refs_2_ = bf16[272,128]{1,0:T(8,128)(2,1)S(1)} collective-permute-done((bf16[272,128]{1,0:T(8,128)(2,1)S(1)}, bf16[272,128]{1,0:T(8,128)(2,1)S(1)}, u32[]{:S(2)}, u32[]{:S(2)}) %collective-permute-start.1) | collective-permute-done | bytes 69664 | tf_op jit(solution)/shard_map/ppermute | solution.py:303
  8.6 2.4 %collective-permute-done.2.refs_3_ = bf16[272,128]{1,0:T(8,128)(2,1)S(1)} collective-permute-done((bf16[272,128]{1,0:T(8,128)(2,1)S(1)}, bf16[272,128]{1,0:T(8,128)(2,1)S(1)}, u32[]{:S(2)}, u32[]{:S(2)}) %collective-permute-start.2) | collective-permute-done | bytes 69664 | tf_op jit(solution)/shard_map/ppermute | solution.py:303
  11.0 2.2 %convolve.1 = (bf16[256,128]{1,0:T(8,128)(2,1)S(1)}, bf16[256,128]{1,0:T(8,128)(2,1)S(1)}, bf16[256,128]{1,0:T(8,128)(2,1)S(1)}, bf16[256,128]{1,0:T(8,128)(2,1)S(1)}) custom-call(bf16[272,128]{1,0:T(8,128)(2,1)S(1)} %get-tuple-element.19.refs_0_, bf16[272,128]{1,0:T(8,128)(2,1)S(1)} %collective-permute-done.refs_1_, ...), custom_call_target="tpu_custom_call" | custom-call | tf_op jit(solution)/shard_map/convolve/pallas_call | solution.py:175
  13.2 0.6 %collective-permute-start.3 = (bf16[256,128]{1,0:T(8,128)(2,1)S(1)}, bf16[256,128]{1,0:T(8,128)(2,1)S(1)}, u32[]{:S(2)}, u32[]{:S(2)}) collective-permute-start(bf16[256,128]{1,0:T(8,128)(2,1)S(1)} %get-tuple-element.24), channel_id=1, source_target_pairs={{0,8},{8,0},{16,24},{24,16},{1,9},{9,1},{17,25},{25,17},{2,10},{10... | collective-permute-start | bytes 196616 | tf_op jit(solution)/shard_map/ppermute | solution.py:303
  13.8 0.6 %collective-permute-start.4 = (bf16[256,128]{1,0:T(8,128)(2,1)S(1)}, bf16[256,128]{1,0:T(8,128)(2,1)S(1)}, u32[]{:S(2)}, u32[]{:S(2)}) collective-permute-start(bf16[256,128]{1,0:T(8,128)(2,1)S(1)} %get-tuple-element.25), channel_id=1, source_target_pairs={{0,16},{8,24},{16,0},{24,8},{1,17},{9,25},{17,1},{25,9},{2,18},{10... | collective-permute-start | bytes 196616 | tf_op jit(solution)/shard_map/ppermute | solution.py:303
  14.5 2.3 %collective-permute-start.5 = (bf16[256,128]{1,0:T(8,128)(2,1)S(1)}, bf16[256,128]{1,0:T(8,128)(2,1)S(1)}, u32[]{:S(2)}, u32[]{:S(2)}) collective-permute-start(bf16[256,128]{1,0:T(8,128)(2,1)S(1)} %get-tuple-element.26), channel_id=1, source_target_pairs={{0,24},{8,16},{16,8},{24,0},{1,25},{9,17},{17,9},{25,1},{2,26},{10... | collective-permute-start | bytes 196616 | tf_op jit(solution)/shard_map/ppermute | solution.py:303
  16.8 0.8 %collective-permute-done.3.refs_1_ = bf16[256,128]{1,0:T(8,128)(2,1)S(1)} collective-permute-done((bf16[256,128]{1,0:T(8,128)(2,1)S(1)}, bf16[256,128]{1,0:T(8,128)(2,1)S(1)}, u32[]{:S(2)}, u32[]{:S(2)}) %collective-permute-start.3) | collective-permute-done | bytes 65568 | tf_op jit(solution)/shard_map/ppermute | solution.py:303
  17.6 0.8 %collective-permute-done.4.refs_2_ = bf16[256,128]{1,0:T(8,128)(2,1)S(1)} collective-permute-done((bf16[256,128]{1,0:T(8,128)(2,1)S(1)}, bf16[256,128]{1,0:T(8,128)(2,1)S(1)}, u32[]{:S(2)}, u32[]{:S(2)}) %collective-permute-start.4) | collective-permute-done | bytes 65568 | tf_op jit(solution)/shard_map/ppermute | solution.py:303
  18.4 1.3 %collective-permute-done.5.refs_3_ = bf16[256,128]{1,0:T(8,128)(2,1)S(1)} collective-permute-done((bf16[256,128]{1,0:T(8,128)(2,1)S(1)}, bf16[256,128]{1,0:T(8,128)(2,1)S(1)}, u32[]{:S(2)}, u32[]{:S(2)}) %collective-permute-start.5) | collective-permute-done | bytes 65568 | tf_op jit(solution)/shard_map/ppermute | solution.py:303
  19.6 0.1 gate.1.own_ref
  19.8 0.1 collective-permute-start.6
  19.9 1.4 %half.1.half_ref = f32[256,512]{1,0:T(8,128)S(1)} custom-call(bf16[256,512]{1,0:T(8,128)(2,1)S(1)} %gate.1.own_ref, bf16[512,4096]{1,0:T(8,128)(2,1)} %own_weight.7), custom_call_target="tpu_custom_call" | custom-call | tf_op jit(solution)/shard_map/half/pallas_call | solution.py:271
  21.2 0.1 collective-permute-done.6.other_ref
  21.4 0.0 collective-permute-done.7.other_weight
  21.4 0.3 by_two.1
  21.7 1.6 %collective-permute-start.8 = (bf16[256,512]{1,0:T(8,128)(2,1)S(1)}, bf16[256,512]{1,0:T(8,128)(2,1)S(1)}, u32[]{:S(2)}, u32[]{:S(2)}) collective-permute-start(bf16[256,512]{1,0:T(8,128)(2,1)S(1)} %by_two.1), channel_id=1, source_target_pairs={{0,2},{1,3},{6,4},{7,5},{2,6},{3,7},{4,0},{5,1},{8,10},{9,11},{14,... | collective-permute-start | bytes 786440 | tf_op jit(solution)/shard_map/ppermute | solution.py:306
  23.3 1.5 %by_one.1 = bf16[256,512]{1,0:T(8,128)(2,1)S(1)} custom-call(bf16[256,512]{1,0:T(8,128)(2,1)S(1)} %gate.1.own_ref, bf16[256,512]{1,0:T(8,128)(2,1)S(1)} %collective-permute-done.6.other_ref, bf16[512,4096]{1,0:T(8,128)(2,1)} %own_weight.7, bf16[512,4096]{1,0:T(8,128)(2,1)S(1)} %collective-permute-done.7.other_weight), custom_call_target="tpu_custom_call" | custom-call | tf_op jit(solution)/shard_map/by_one/pallas_call | solution.py:271
  24.8 2.7 %collective-permute-start.9 = (bf16[256,512]{1,0:T(8,128)(2,1)S(1)}, bf16[256,512]{1,0:T(8,128)(2,1)S(1)}, u32[]{:S(2)}, u32[]{:S(2)}) collective-permute-start(bf16[256,512]{1,0:T(8,128)(2,1)S(1)} %by_one.1), channel_id=1, source_target_pairs={{0,2},{1,3},{2,0},{3,1},{4,6},{5,7},{6,4},{7,5},{8,10},{9,11},{10,... | collective-permute-start | bytes 786440 | tf_op jit(solution)/shard_map/ppermute | solution.py:306
  27.5 1.5 %by_three.1.own_ref = bf16[256,512]{1,0:T(8,128)(2,1)S(1)} custom-call(bf16[256,512]{1,0:T(8,128)(2,1)S(1)} %gate.1.own_ref, bf16[256,512]{1,0:T(8,128)(2,1)S(1)} %collective-permute-done.6.other_ref, bf16[512,4096]{1,0:T(8,128)(2,1)} %own_weight.7, bf16[512,4096]{1,0:T(8,128)(2,1)S(1)} %collective-permute-done.7.other_weight), custom_call_target="tpu_custom_call" | custom-call | tf_op jit(solution)/shard_map/by_three/pallas_call | solution.py:271
  29.0 2.3 %collective-permute-done.8.first_ref.arrived_ref = bf16[256,512]{1,0:T(8,128)(2,1)S(1)} collective-permute-done((bf16[256,512]{1,0:T(8,128)(2,1)S(1)}, bf16[256,512]{1,0:T(8,128)(2,1)S(1)}, u32[]{:S(2)}, u32[]{:S(2)}) %collective-permute-start.8) | collective-permute-done | bytes 262176 | tf_op jit(solution)/shard_map/ppermute | solution.py:306
  31.3 3.7 %collective-permute-start.10 = (bf16[256,512]{1,0:T(8,128)(2,1)S(1)}, bf16[256,512]{1,0:T(8,128)(2,1)S(1)}, u32[]{:S(2)}, u32[]{:S(2)}) collective-permute-start(bf16[256,512]{1,0:T(8,128)(2,1)S(1)} %forward.1), channel_id=1, source_target_pairs={{0,6},{1,7},{6,0},{7,1},{2,4},{3,5},{4,2},{5,3},{8,14},{9,15},{14,... | collective-permute-start | bytes 786440 | tf_op jit(solution)/shard_map/ppermute | solution.py:306
  35.0 1.5 %base.1.base_ref = f32[256,512]{1,0:T(8,128)S(1)} custom-call(bf16[256,512]{1,0:T(8,128)(2,1)S(1)} %gate.1.own_ref, bf16[256,512]{1,0:T(8,128)(2,1)S(1)} %collective-permute-done.6.other_ref, bf16[512,4096]{1,0:T(8,128)(2,1)} %own_weight.7, bf16[512,4096]{1,0:T(8,128)(2,1)S(1)} %collective-permute-done.7.other_weight, ...), custom_call_target="tpu_custom_call" | custom-call | tf_op jit(solution)/shard_map/base/pallas_call | solution.py:271
  36.6 0.3 collective-permute-done.9.pair_ref
  36.8 6.9 %collective-permute-done.10.mirror_ref = bf16[256,512]{1,0:T(8,128)(2,1)S(1)} collective-permute-done((bf16[256,512]{1,0:T(8,128)(2,1)S(1)}, bf16[256,512]{1,0:T(8,128)(2,1)S(1)}, u32[]{:S(2)}, u32[]{:S(2)}) %collective-permute-start.10) | collective-permute-done | bytes 262176 | tf_op jit(solution)/shard_map/ppermute | solution.py:306
  43.7 0.8 %final.1 = bf16[256,512]{1,0:T(8,128)(2,1)} custom-call(f32[256,512]{1,0:T(8,128)S(1)} %base.1.base_ref, bf16[256,512]{1,0:T(8,128)(2,1)S(1)} %collective-permute-done.9.pair_ref, bf16[256,512]{1,0:T(8,128)(2,1)S(1)} %collective-permute-done.10.mirror_ref), custom_call_target="tpu_custom_call" | custom-call | tf_op jit(solution)/shard_map/final/pallas_call | solution.py:271
  (1 shorter events, 0.0 us)
Async XLA Ops:
  0.0 21.4 %collective-permute-start.7 = (bf16[512,4096]{1,0:T(8,128)(2,1)}, bf16[512,4096]{1,0:T(8,128)(2,1)S(1)}, u32[]{:S(2)}, u32[]{:S(2)}) collective-permute-start(bf16[512,4096]{1,0:T(8,128)(2,1)} %own_weight.7), channel_id=1, source_target_pairs={{0,1},{1,0},{2,3},{3,2},{4,5},{5,4},{6,7},{7,6},{8,9},{9,8},{10,11... | collective-permute-start | bytes 12582920 | tf_op jit(solution)/shard_map/ppermute | solution.py:311
  1.7 5.4 %collective-permute-start = (bf16[272,128]{1,0:T(8,128)(2,1)S(1)}, bf16[272,128]{1,0:T(8,128)(2,1)S(1)}, u32[]{:S(2)}, u32[]{:S(2)}) collective-permute-start(bf16[272,128]{1,0:T(8,128)(2,1)S(1)} %get-tuple-element.20), channel_id=1, source_target_pairs={{0,8},{8,0},{16,24},{24,16},{1,9},{9,1},{17,25},{25,17},{2,10},{10... | collective-permute-start | bytes 208904 | tf_op jit(solution)/shard_map/ppermute | solution.py:303
  4.3 4.3 %collective-permute-start.1 = (bf16[272,128]{1,0:T(8,128)(2,1)S(1)}, bf16[272,128]{1,0:T(8,128)(2,1)S(1)}, u32[]{:S(2)}, u32[]{:S(2)}) collective-permute-start(bf16[272,128]{1,0:T(8,128)(2,1)S(1)} %get-tuple-element.21), channel_id=1, source_target_pairs={{0,16},{8,24},{16,0},{24,8},{1,17},{9,25},{17,1},{25,9},{2,18},{10... | collective-permute-start | bytes 208904 | tf_op jit(solution)/shard_map/ppermute | solution.py:303
  5.8 5.2 %collective-permute-start.2 = (bf16[272,128]{1,0:T(8,128)(2,1)S(1)}, bf16[272,128]{1,0:T(8,128)(2,1)S(1)}, u32[]{:S(2)}, u32[]{:S(2)}) collective-permute-start(bf16[272,128]{1,0:T(8,128)(2,1)S(1)} %get-tuple-element.22), channel_id=1, source_target_pairs={{0,24},{8,16},{16,8},{24,0},{1,25},{9,17},{17,9},{25,1},{2,26},{10... | collective-permute-start | bytes 208904 | tf_op jit(solution)/shard_map/ppermute | solution.py:303
  13.2 4.4 %collective-permute-start.3 = (bf16[256,128]{1,0:T(8,128)(2,1)S(1)}, bf16[256,128]{1,0:T(8,128)(2,1)S(1)}, u32[]{:S(2)}, u32[]{:S(2)}) collective-permute-start(bf16[256,128]{1,0:T(8,128)(2,1)S(1)} %get-tuple-element.24), channel_id=1, source_target_pairs={{0,8},{8,0},{16,24},{24,16},{1,9},{9,1},{17,25},{25,17},{2,10},{10... | collective-permute-start | bytes 196616 | tf_op jit(solution)/shard_map/ppermute | solution.py:303
  13.8 4.5 %collective-permute-start.4 = (bf16[256,128]{1,0:T(8,128)(2,1)S(1)}, bf16[256,128]{1,0:T(8,128)(2,1)S(1)}, u32[]{:S(2)}, u32[]{:S(2)}) collective-permute-start(bf16[256,128]{1,0:T(8,128)(2,1)S(1)} %get-tuple-element.25), channel_id=1, source_target_pairs={{0,16},{8,24},{16,0},{24,8},{1,17},{9,25},{17,1},{25,9},{2,18},{10... | collective-permute-start | bytes 196616 | tf_op jit(solution)/shard_map/ppermute | solution.py:303
  14.5 5.2 %collective-permute-start.5 = (bf16[256,128]{1,0:T(8,128)(2,1)S(1)}, bf16[256,128]{1,0:T(8,128)(2,1)S(1)}, u32[]{:S(2)}, u32[]{:S(2)}) collective-permute-start(bf16[256,128]{1,0:T(8,128)(2,1)S(1)} %get-tuple-element.26), channel_id=1, source_target_pairs={{0,24},{8,16},{16,8},{24,0},{1,25},{9,17},{17,9},{25,1},{2,26},{10... | collective-permute-start | bytes 196616 | tf_op jit(solution)/shard_map/ppermute | solution.py:303
  19.8 1.6 %collective-permute-start.6 = (bf16[256,512]{1,0:T(8,128)(2,1)S(1)}, bf16[256,512]{1,0:T(8,128)(2,1)S(1)}, u32[]{:S(2)}, u32[]{:S(2)}) collective-permute-start(bf16[256,512]{1,0:T(8,128)(2,1)S(1)} %gate.1.own_ref), channel_id=1, source_target_pairs={{0,1},{1,0},{2,3},{3,2},{4,5},{5,4},{6,7},{7,6},{8,9},{9,8},{10,11... | collective-permute-start | bytes 786440 | tf_op jit(solution)/shard_map/ppermute | solution.py:311
  21.7 9.6 %collective-permute-start.8 = (bf16[256,512]{1,0:T(8,128)(2,1)S(1)}, bf16[256,512]{1,0:T(8,128)(2,1)S(1)}, u32[]{:S(2)}, u32[]{:S(2)}) collective-permute-start(bf16[256,512]{1,0:T(8,128)(2,1)S(1)} %by_two.1), channel_id=1, source_target_pairs={{0,2},{1,3},{6,4},{7,5},{2,6},{3,7},{4,0},{5,1},{8,10},{9,11},{14,... | collective-permute-start | bytes 786440 | tf_op jit(solution)/shard_map/ppermute | solution.py:306
  24.8 12.0 %collective-permute-start.9 = (bf16[256,512]{1,0:T(8,128)(2,1)S(1)}, bf16[256,512]{1,0:T(8,128)(2,1)S(1)}, u32[]{:S(2)}, u32[]{:S(2)}) collective-permute-start(bf16[256,512]{1,0:T(8,128)(2,1)S(1)} %by_one.1), channel_id=1, source_target_pairs={{0,2},{1,3},{2,0},{3,1},{4,6},{5,7},{6,4},{7,5},{8,10},{9,11},{10,... | collective-permute-start | bytes 786440 | tf_op jit(solution)/shard_map/ppermute | solution.py:306
  31.3 12.3 %collective-permute-start.10 = (bf16[256,512]{1,0:T(8,128)(2,1)S(1)}, bf16[256,512]{1,0:T(8,128)(2,1)S(1)}, u32[]{:S(2)}, u32[]{:S(2)}) collective-permute-start(bf16[256,512]{1,0:T(8,128)(2,1)S(1)} %forward.1), channel_id=1, source_target_pairs={{0,6},{1,7},{6,0},{7,1},{2,4},{3,5},{4,2},{5,3},{8,14},{9,15},{14,... | collective-permute-start | bytes 786440 | tf_op jit(solution)/shard_map/ppermute | solution.py:306

commit v3 on v2

--- a/solution.py
+++ b/solution.py
@@ -24,6 +24,10 @@
 
 def in_vmem(*arrays):
     return [pltpu.with_memory_space_constraint(a, pltpu.VMEM) for a in arrays]
+
+
+def far_first(n_seq):
+    return sorted(range(n_seq), key=lambda d: -d.bit_count())
 
 
 def seq_place():
@@ -105,72 +109,57 @@
 
 
 def conv_kernel(n_seq, rows, part, *refs):
-    packed_refs = refs[:n_seq]
+    packed_refs = [refs[far_first(n_seq).index(d)] for d in range(n_seq)]
     out_refs = refs[n_seq : 2 * n_seq]
-    signal, tap_rows, lag_blocks, total = refs[2 * n_seq :]
+    signal, taps, total = refs[2 * n_seq :]
     per_shard = rows // LANES
-    tiles = n_seq * per_shard
+    blocks = n_seq * per_shard
     group_width = LANES // part
 
     for d in range(n_seq):
-        other = seq_place() ^ d
-        signal[rows_at(other, rows), :] = packed_refs[d][0:rows, :]
-        tap_rows[rows_at(other, part * per_shard), :] = packed_refs[d][rows:, :].astype(F32)
-
-    from_lane = lax.broadcasted_iota(jnp.int32, (LANES, LANES), 0)
-    to_lane = lax.broadcasted_iota(jnp.int32, (LANES, LANES), 1)
-    flip = jnp.where((from_lane + to_lane) % LANES == 0, 1.0, 0.0).astype(BF16)
-    tap_rows[...] = jnp.dot(tap_rows[...].astype(BF16), flip, preferred_element_type=F32)
-
-    lower = to_lane <= from_lane
-    zero_block = jnp.zeros((LANES, LANES), BF16)
-
+        first = (seq_place() ^ d) * per_shard
+        tap_rows = packed_refs[d][rows:, :].astype(F32)
+        for k in range(per_shard):
+            tokens = packed_refs[d][k * LANES : (k + 1) * LANES, :].astype(F32)
+            signal[first + k] = tokens.T.astype(BF16)
+            taps[first + k] = tap_rows[k * part : (k + 1) * part, :]
+
+    below = lax.broadcasted_iota(jnp.int32, (LANES, LANES), 0)
+    lane = lax.broadcasted_iota(jnp.int32, (LANES, LANES), 1)
     for g in range(part):
-        lag_blocks[0:LANES, (2 * g + 1) * LANES : (2 * g + 2) * LANES] = zero_block
+        here = slice(g * group_width, (g + 1) * group_width)
         before = jnp.zeros((LANES, LANES), F32)
-        for k in range(tiles):
-            row = tap_rows[k * part + g : k * part + g + 1, :]
+        by_lag = []
+        for e in range(blocks):
             rolled = pltpu.roll(
-                jnp.broadcast_to(row, (LANES, LANES)), 0, 1, stride=1, stride_axis=0
+                jnp.broadcast_to(taps[e, g : g + 1, :], (LANES, LANES)), 0, 1, stride=1, stride_axis=0
             )
-            block = jnp.where(lower, rolled, before).astype(BF16)
-            lag_blocks[k * LANES : (k + 1) * LANES, 2 * g * LANES : (2 * g + 1) * LANES] = block
-            if k + 1 < tiles:
-                lag_blocks[
-                    (k + 1) * LANES : (k + 2) * LANES, (2 * g + 1) * LANES : (2 * g + 2) * LANES
-                ] = block
+            by_lag.append(jnp.where(lane >= below, rolled, before).astype(BF16))
             before = rolled
-
-    step = 2 * LANES
-    length = n_seq * rows
-    lane_group = lax.broadcasted_iota(jnp.int32, (step, LANES), 1) // group_width
-    total[...] = jnp.zeros_like(total)
-    for first in range(0, length, 2 * step):
-        left = signal[first : first + step, :]
-        right = signal[first + step : first + 2 * step, :]
-        masked = []
-        for g in range(part):
-            here = lane_group == g
-            masked.append(
-                jnp.concatenate(
-                    [jnp.where(here, left, 0.0).astype(BF16), jnp.where(here, right, 0.0).astype(BF16)],
-                    axis=1,
-                )
+        sums = [None] * blocks
+        for e in range(0, blocks, 2):
+            left = signal[0 : blocks - e, here, :].reshape((blocks - e) * group_width, LANES)
+            both = jnp.dot(
+                left, jnp.concatenate(by_lag[e : e + 2], axis=1), preferred_element_type=F32
             )
-        both = jnp.dot(
-            lag_blocks[0 : length - first, :],
-            jnp.concatenate(masked, axis=0),
-            preferred_element_type=F32,
-        )
-        total[first:length, :] += both[:, 0:LANES]
-        total[first + step : length, :] += both[0 : length - first - step, LANES:]
+            for q in range(blocks - e):
+                piece = both[q * group_width : (q + 1) * group_width, :]
+                for k in range(2):
+                    at = q + e + k
+                    if at < blocks:
+                        addend = piece[:, k * LANES : (k + 1) * LANES]
+                        sums[at] = addend if sums[at] is None else sums[at] + addend
+        for q in range(blocks):
+            total[q, here, :] = sums[q]
 
     for d in range(n_seq):
-        out_refs[d][...] = total[rows_at(seq_place() ^ d, rows), :].astype(BF16)
+        first = (seq_place() ^ d) * per_shard
+        for k in range(per_shard):
+            out_refs[d][k * LANES : (k + 1) * LANES, :] = total[first + k].T.astype(BF16)
 
 
 def convolve(packed, n_seq, rows, part):
-    tiles = n_seq * rows // LANES
+    blocks = n_seq * rows // LANES
     vmem = pl.BlockSpec(memory_space=pltpu.VMEM)
     return pl.pallas_call(
         functools.partial(conv_kernel, n_seq, rows, part),
@@ -178,18 +167,17 @@
         in_specs=[vmem] * n_seq,
         out_specs=[vmem] * n_seq,
         scratch_shapes=[
-            pltpu.VMEM((n_seq * rows, LANES), BF16),
-            pltpu.VMEM((tiles * part, LANES), F32),
-            pltpu.VMEM((n_seq * rows, 2 * LANES * part), BF16),
-            pltpu.VMEM((n_seq * rows, LANES), F32),
+            pltpu.VMEM((blocks, LANES, LANES), BF16),
+            pltpu.VMEM((blocks, part, LANES), F32),
+            pltpu.VMEM((blocks, LANES, LANES), F32),
         ],
         compiler_params=params(),
         name="convolve",
-    )(*packed)
+    )(*[packed[d] for d in far_first(n_seq)])
 
 
 def gate_kernel(n_seq, query_ref, mixed_ref, skip_ref, *refs):
-    conv_refs, out_ref = refs[:n_seq], refs[n_seq]
+    conv_refs, out_ref = [refs[far_first(n_seq).index(d)] for d in range(n_seq)], refs[n_seq]
     for d in range(n_seq):
         lanes = lanes_at(seq_place() ^ d)
         direct = skip_ref[:, lanes] * mixed_ref[:, lanes].astype(F32)
@@ -207,7 +195,7 @@
         out_specs=vmem,
         compiler_params=params(),
         name="gate",
-    )(query_in, mixed_in, skip_gain, *parts)
+    )(query_in, mixed_in, skip_gain, *[parts[d] for d in far_first(len(parts))])
 
 
 def load_block(distance, weight_hbm, weight, arrived):

time: 44.8 us -> 43.3 us (0.967)
  Pallas kernels: 10.7 us -> 9.45 us
    pallas_call x1, Pallas kernels: 2.24 us -> 1.03 us  [convolve(): pl.pallas_call(functools.partial(conv_kernel, n_seq, rows, part), out_sha...]
  transfers between devices with their start and end apart: 11 -> 11, of which waited for: 10 -> 10; matrix products, arithmetic and copies ran while one was open for 0% -> 0% of each run, Pallas kernels for 22% -> 19%
where the time goes in v3:
time: 43.3 us; the launch traced here: 43 us
  waiting for transfers between devices  17.2 us (40%)
  starting transfers between devices  16.2 us (37%)
  Pallas kernels  9.45 us (22%)
    ppermute x3, waiting for transfers between devices, over_chips(): lax.ppermute(value, 'chan', [(2 * a + c, 2 * b + c) for a, b in moves for...  9.43 us
    ppermute x3, starting transfers between devices, over_chips(): lax.ppermute(value, 'chan', [(2 * a + c, 2 * b + c) for a, b in moves for...  7.96 us
    ppermute x6, starting transfers between devices, over_seq(): return lax.ppermute(value, 'seq', [(i, i ^ d) for i in range(n_seq)])  7.71 us
    ppermute x6, waiting for transfers between devices, over_seq(): return lax.ppermute(value, 'seq', [(i, i ^ d) for i in range(n_seq)])  7.65 us
    pallas_call x7, Pallas kernels, run_kernel(): pl.pallas_call(kernel, out_shape=out_shape, in_specs=specs, out_specs=[vm...  7.02 us
    pallas_call x1, Pallas kernels, products(): pl.pallas_call(functools.partial(product_kernel, n_seq), out_shape=[here,...  1.26 us
    pallas_call x1, Pallas kernels, convolve(): pl.pallas_call(functools.partial(conv_kernel, n_seq, rows, part), out_sha...  1.03 us
  transfers between devices with their start and end apart: 11, of which 10 were waited for; matrix products, arithmetic and copies ran while one was open for 0% of the time, Pallas kernels for 19%

profile of v3, /device:TPU:0, one launch (start us, length us, event | category | flops | bytes accessed | tf_op | source)
XLA Modules:
  0.0 43.0 jit_solution(10312635404415373530)
XLA Ops:
  0.0 0.5 %collective-permute-start.7 = (bf16[512,4096]{1,0:T(8,128)(2,1)}, bf16[512,4096]{1,0:T(8,128)(2,1)S(1)}, u32[]{:S(2)}, u32[]{:S(2)}) collective-permute-start(bf16[512,4096]{1,0:T(8,128)(2,1)} %own_weight.7), channel_id=1, source_target_pairs={{0,1},{1,0},{2,3},{3,2},{4,5},{5,4},{6,7},{7,6},{8,9},{9,8},{10,11... | collective-permute-start | bytes 12582920 | tf_op jit(solution)/shard_map/ppermute | solution.py:299
  0.5 1.3 %products.1 = (bf16[256,512]{1,0:T(8,128)(2,1)S(1)}, bf16[256,512]{1,0:T(8,128)(2,1)S(1)}, f32[1,512]{1,0:T(1,128)S(1)}, bf16[272,128]{1,0:T(8,128)(2,1)S(1)}, b...) custom-call(bf16[256,512]{1,0:T(8,128)(2,1)} %key_hbm.1, ...), custom_call_target="tpu_custom_call" | custom-call | tf_op jit(solution)/shard_map/products/pallas_call | solution.py:94
  1.7 3.5 %collective-permute-start = (bf16[272,128]{1,0:T(8,128)(2,1)S(1)}, bf16[272,128]{1,0:T(8,128)(2,1)S(1)}, u32[]{:S(2)}, u32[]{:S(2)}) collective-permute-start(bf16[272,128]{1,0:T(8,128)(2,1)S(1)} %get-tuple-element.19), channel_id=1, source_target_pairs={{0,24},{8,16},{16,8},{24,0},{1,25},{9,17},{17,9},{25,1},{2,26},{10... | collective-permute-start | bytes 208904 | tf_op jit(solution)/shard_map/ppermute | solution.py:291
  5.2 0.5 %collective-permute-start.1 = (bf16[272,128]{1,0:T(8,128)(2,1)S(1)}, bf16[272,128]{1,0:T(8,128)(2,1)S(1)}, u32[]{:S(2)}, u32[]{:S(2)}) collective-permute-start(bf16[272,128]{1,0:T(8,128)(2,1)S(1)} %get-tuple-element.20), channel_id=1, source_target_pairs={{0,8},{8,0},{16,24},{24,16},{1,9},{9,1},{17,25},{25,17},{2,10},{10... | collective-permute-start | bytes 208904 | tf_op jit(solution)/shard_map/ppermute | solution.py:291
  5.8 0.1 collective-permute-start.2
  5.9 2.3 %collective-permute-done.refs_0_ = bf16[272,128]{1,0:T(8,128)(2,1)S(1)} collective-permute-done((bf16[272,128]{1,0:T(8,128)(2,1)S(1)}, bf16[272,128]{1,0:T(8,128)(2,1)S(1)}, u32[]{:S(2)}, u32[]{:S(2)}) %collective-permute-start) | collective-permute-done | bytes 69664 | tf_op jit(solution)/shard_map/ppermute | solution.py:291
  8.1 1.7 %collective-permute-done.1.refs_1_ = bf16[272,128]{1,0:T(8,128)(2,1)S(1)} collective-permute-done((bf16[272,128]{1,0:T(8,128)(2,1)S(1)}, bf16[272,128]{1,0:T(8,128)(2,1)S(1)}, u32[]{:S(2)}, u32[]{:S(2)}) %collective-permute-start.1) | collective-permute-done | bytes 69664 | tf_op jit(solution)/shard_map/ppermute | solution.py:291
  9.8 0.3 collective-permute-done.2.refs_2_
  10.1 1.0 %convolve.1 = (bf16[256,128]{1,0:T(8,128)(2,1)S(1)}, bf16[256,128]{1,0:T(8,128)(2,1)S(1)}, bf16[256,128]{1,0:T(8,128)(2,1)S(1)}, bf16[256,128]{1,0:T(8,128)(2,1)S(1)}) custom-call(bf16[272,128]{1,0:T(8,128)(2,1)S(1)} %collective-permute-done.refs_0_, bf16[272,128]{1,0:T(8,128)(2,1)S(1)} %collective-permute-done.1.refs_1_, ...), custom_call_target="tpu_custom_call" | custom-call | tf_op jit(solution)/shard_map/convolve/pallas_call | solution.py:164
  11.1 2.2 %collective-permute-start.3 = (bf16[256,128]{1,0:T(8,128)(2,1)S(1)}, bf16[256,128]{1,0:T(8,128)(2,1)S(1)}, u32[]{:S(2)}, u32[]{:S(2)}) collective-permute-start(bf16[256,128]{1,0:T(8,128)(2,1)S(1)} %get-tuple-element.23), channel_id=1, source_target_pairs={{0,24},{8,16},{16,8},{24,0},{1,25},{9,17},{17,9},{25,1},{2,26},{10... | collective-permute-start | bytes 196616 | tf_op jit(solution)/shard_map/ppermute | solution.py:291
  13.3 0.5 %collective-permute-start.4 = (bf16[256,128]{1,0:T(8,128)(2,1)S(1)}, bf16[256,128]{1,0:T(8,128)(2,1)S(1)}, u32[]{:S(2)}, u32[]{:S(2)}) collective-permute-start(bf16[256,128]{1,0:T(8,128)(2,1)S(1)} %get-tuple-element.24), channel_id=1, source_target_pairs={{0,8},{8,0},{16,24},{24,16},{1,9},{9,1},{17,25},{25,17},{2,10},{10... | collective-permute-start | bytes 196616 | tf_op jit(solution)/shard_map/ppermute | solution.py:291
  13.9 0.8 %collective-permute-start.5 = (bf16[256,128]{1,0:T(8,128)(2,1)S(1)}, bf16[256,128]{1,0:T(8,128)(2,1)S(1)}, u32[]{:S(2)}, u32[]{:S(2)}) collective-permute-start(bf16[256,128]{1,0:T(8,128)(2,1)S(1)} %get-tuple-element.25), channel_id=1, source_target_pairs={{0,16},{8,24},{16,0},{24,8},{1,17},{9,25},{17,1},{25,9},{2,18},{10... | collective-permute-start | bytes 196616 | tf_op jit(solution)/shard_map/ppermute | solution.py:291
  14.7 2.2 %collective-permute-done.3.refs_0_ = bf16[256,128]{1,0:T(8,128)(2,1)S(1)} collective-permute-done((bf16[256,128]{1,0:T(8,128)(2,1)S(1)}, bf16[256,128]{1,0:T(8,128)(2,1)S(1)}, u32[]{:S(2)}, u32[]{:S(2)}) %collective-permute-start.3) | collective-permute-done | bytes 65568 | tf_op jit(solution)/shard_map/ppermute | solution.py:291
  16.9 0.7 %collective-permute-done.4.refs_1_ = bf16[256,128]{1,0:T(8,128)(2,1)S(1)} collective-permute-done((bf16[256,128]{1,0:T(8,128)(2,1)S(1)}, bf16[256,128]{1,0:T(8,128)(2,1)S(1)}, u32[]{:S(2)}, u32[]{:S(2)}) %collective-permute-start.4) | collective-permute-done | bytes 65568 | tf_op jit(solution)/shard_map/ppermute | solution.py:291
  17.6 0.5 %collective-permute-done.5.refs_2_ = bf16[256,128]{1,0:T(8,128)(2,1)S(1)} collective-permute-done((bf16[256,128]{1,0:T(8,128)(2,1)S(1)}, bf16[256,128]{1,0:T(8,128)(2,1)S(1)}, u32[]{:S(2)}, u32[]{:S(2)}) %collective-permute-start.5) | collective-permute-done | bytes 65568 | tf_op jit(solution)/shard_map/ppermute | solution.py:291
  18.1 0.1 gate.1.own_ref
  18.3 0.1 collective-permute-start.6
  18.3 1.4 %half.1.half_ref = f32[256,512]{1,0:T(8,128)S(1)} custom-call(bf16[256,512]{1,0:T(8,128)(2,1)S(1)} %gate.1.own_ref, bf16[512,4096]{1,0:T(8,128)(2,1)} %own_weight.7), custom_call_target="tpu_custom_call" | custom-call | tf_op jit(solution)/shard_map/half/pallas_call | solution.py:259
  19.7 0.1 collective-permute-done.6.other_ref
  19.9 0.0 collective-permute-done.7.other_weight
  19.9 0.3 by_two.1
  20.2 1.6 %collective-permute-start.8 = (bf16[256,512]{1,0:T(8,128)(2,1)S(1)}, bf16[256,512]{1,0:T(8,128)(2,1)S(1)}, u32[]{:S(2)}, u32[]{:S(2)}) collective-permute-start(bf16[256,512]{1,0:T(8,128)(2,1)S(1)} %by_two.1), channel_id=1, source_target_pairs={{0,2},{1,3},{6,4},{7,5},{2,6},{3,7},{4,0},{5,1},{8,10},{9,11},{14,... | collective-permute-start | bytes 786440 | tf_op jit(solution)/shard_map/ppermute | solution.py:294
  21.8 1.5 %by_one.1 = bf16[256,512]{1,0:T(8,128)(2,1)S(1)} custom-call(bf16[256,512]{1,0:T(8,128)(2,1)S(1)} %gate.1.own_ref, bf16[256,512]{1,0:T(8,128)(2,1)S(1)} %collective-permute-done.6.other_ref, bf16[512,4096]{1,0:T(8,128)(2,1)} %own_weight.7, bf16[512,4096]{1,0:T(8,128)(2,1)S(1)} %collective-permute-done.7.other_weight), custom_call_target="tpu_custom_call" | custom-call | tf_op jit(solution)/shard_map/by_one/pallas_call | solution.py:259
  23.3 2.7 %collective-permute-start.9 = (bf16[256,512]{1,0:T(8,128)(2,1)S(1)}, bf16[256,512]{1,0:T(8,128)(2,1)S(1)}, u32[]{:S(2)}, u32[]{:S(2)}) collective-permute-start(bf16[256,512]{1,0:T(8,128)(2,1)S(1)} %by_one.1), channel_id=1, source_target_pairs={{0,2},{1,3},{2,0},{3,1},{4,6},{5,7},{6,4},{7,5},{8,10},{9,11},{10,... | collective-permute-start | bytes 786440 | tf_op jit(solution)/shard_map/ppermute | solution.py:294
  26.0 1.5 %by_three.1.own_ref = bf16[256,512]{1,0:T(8,128)(2,1)S(1)} custom-call(bf16[256,512]{1,0:T(8,128)(2,1)S(1)} %gate.1.own_ref, bf16[256,512]{1,0:T(8,128)(2,1)S(1)} %collective-permute-done.6.other_ref, bf16[512,4096]{1,0:T(8,128)(2,1)} %own_weight.7, bf16[512,4096]{1,0:T(8,128)(2,1)S(1)} %collective-permute-done.7.other_weight), custom_call_target="tpu_custom_call" | custom-call | tf_op jit(solution)/shard_map/by_three/pallas_call | solution.py:259
  27.5 2.3 %collective-permute-done.8.first_ref.arrived_ref = bf16[256,512]{1,0:T(8,128)(2,1)S(1)} collective-permute-done((bf16[256,512]{1,0:T(8,128)(2,1)S(1)}, bf16[256,512]{1,0:T(8,128)(2,1)S(1)}, u32[]{:S(2)}, u32[]{:S(2)}) %collective-permute-start.8) | collective-permute-done | bytes 262176 | tf_op jit(solution)/shard_map/ppermute | solution.py:294
  29.8 3.7 %collective-permute-start.10 = (bf16[256,512]{1,0:T(8,128)(2,1)S(1)}, bf16[256,512]{1,0:T(8,128)(2,1)S(1)}, u32[]{:S(2)}, u32[]{:S(2)}) collective-permute-start(bf16[256,512]{1,0:T(8,128)(2,1)S(1)} %forward.1), channel_id=1, source_target_pairs={{0,6},{1,7},{6,0},{7,1},{2,4},{3,5},{4,2},{5,3},{8,14},{9,15},{14,... | collective-permute-start | bytes 786440 | tf_op jit(solution)/shard_map/ppermute | solution.py:294
  33.5 1.5 %base.1.base_ref = f32[256,512]{1,0:T(8,128)S(1)} custom-call(bf16[256,512]{1,0:T(8,128)(2,1)S(1)} %gate.1.own_ref, bf16[256,512]{1,0:T(8,128)(2,1)S(1)} %collective-permute-done.6.other_ref, bf16[512,4096]{1,0:T(8,128)(2,1)} %own_weight.7, bf16[512,4096]{1,0:T(8,128)(2,1)S(1)} %collective-permute-done.7.other_weight, ...), custom_call_target="tpu_custom_call" | custom-call | tf_op jit(solution)/shard_map/base/pallas_call | solution.py:259
  35.0 0.3 collective-permute-done.9.pair_ref
  35.3 6.9 %collective-permute-done.10.mirror_ref = bf16[256,512]{1,0:T(8,128)(2,1)S(1)} collective-permute-done((bf16[256,512]{1,0:T(8,128)(2,1)S(1)}, bf16[256,512]{1,0:T(8,128)(2,1)S(1)}, u32[]{:S(2)}, u32[]{:S(2)}) %collective-permute-start.10) | collective-permute-done | bytes 262176 | tf_op jit(solution)/shard_map/ppermute | solution.py:294
  42.2 0.8 %final.1 = bf16[256,512]{1,0:T(8,128)(2,1)} custom-call(f32[256,512]{1,0:T(8,128)S(1)} %base.1.base_ref, bf16[256,512]{1,0:T(8,128)(2,1)S(1)} %collective-permute-done.9.pair_ref, bf16[256,512]{1,0:T(8,128)(2,1)S(1)} %collective-permute-done.10.mirror_ref), custom_call_target="tpu_custom_call" | custom-call | tf_op jit(solution)/shard_map/final/pallas_call | solution.py:259
  (1 shorter events, 0.0 us)
Async XLA Ops:
  0.0 19.9 %collective-permute-start.7 = (bf16[512,4096]{1,0:T(8,128)(2,1)}, bf16[512,4096]{1,0:T(8,128)(2,1)S(1)}, u32[]{:S(2)}, u32[]{:S(2)}) collective-permute-start(bf16[512,4096]{1,0:T(8,128)(2,1)} %own_weight.7), channel_id=1, source_target_pairs={{0,1},{1,0},{2,3},{3,2},{4,5},{5,4},{6,7},{7,6},{8,9},{9,8},{10,11... | collective-permute-start | bytes 12582920 | tf_op jit(solution)/shard_map/ppermute | solution.py:299
  1.7 6.4 %collective-permute-start = (bf16[272,128]{1,0:T(8,128)(2,1)S(1)}, bf16[272,128]{1,0:T(8,128)(2,1)S(1)}, u32[]{:S(2)}, u32[]{:S(2)}) collective-permute-start(bf16[272,128]{1,0:T(8,128)(2,1)S(1)} %get-tuple-element.19), channel_id=1, source_target_pairs={{0,24},{8,16},{16,8},{24,0},{1,25},{9,17},{17,9},{25,1},{2,26},{10... | collective-permute-start | bytes 208904 | tf_op jit(solution)/shard_map/ppermute | solution.py:291
  5.2 4.6 %collective-permute-start.1 = (bf16[272,128]{1,0:T(8,128)(2,1)S(1)}, bf16[272,128]{1,0:T(8,128)(2,1)S(1)}, u32[]{:S(2)}, u32[]{:S(2)}) collective-permute-start(bf16[272,128]{1,0:T(8,128)(2,1)S(1)} %get-tuple-element.20), channel_id=1, source_target_pairs={{0,8},{8,0},{16,24},{24,16},{1,9},{9,1},{17,25},{25,17},{2,10},{10... | collective-permute-start | bytes 208904 | tf_op jit(solution)/shard_map/ppermute | solution.py:291
  5.8 4.3 %collective-permute-start.2 = (bf16[272,128]{1,0:T(8,128)(2,1)S(1)}, bf16[272,128]{1,0:T(8,128)(2,1)S(1)}, u32[]{:S(2)}, u32[]{:S(2)}) collective-permute-start(bf16[272,128]{1,0:T(8,128)(2,1)S(1)} %get-tuple-element.21), channel_id=1, source_target_pairs={{0,16},{8,24},{16,0},{24,8},{1,17},{9,25},{17,1},{25,9},{2,18},{10... | collective-permute-start | bytes 208904 | tf_op jit(solution)/shard_map/ppermute | solution.py:291
  11.1 5.8 %collective-permute-start.3 = (bf16[256,128]{1,0:T(8,128)(2,1)S(1)}, bf16[256,128]{1,0:T(8,128)(2,1)S(1)}, u32[]{:S(2)}, u32[]{:S(2)}) collective-permute-start(bf16[256,128]{1,0:T(8,128)(2,1)S(1)} %get-tuple-element.23), channel_id=1, source_target_pairs={{0,24},{8,16},{16,8},{24,0},{1,25},{9,17},{17,9},{25,1},{2,26},{10... | collective-permute-start | bytes 196616 | tf_op jit(solution)/shard_map/ppermute | solution.py:291
  13.3 4.3 %collective-permute-start.4 = (bf16[256,128]{1,0:T(8,128)(2,1)S(1)}, bf16[256,128]{1,0:T(8,128)(2,1)S(1)}, u32[]{:S(2)}, u32[]{:S(2)}) collective-permute-start(bf16[256,128]{1,0:T(8,128)(2,1)S(1)} %get-tuple-element.24), channel_id=1, source_target_pairs={{0,8},{8,0},{16,24},{24,16},{1,9},{9,1},{17,25},{25,17},{2,10},{10... | collective-permute-start | bytes 196616 | tf_op jit(solution)/shard_map/ppermute | solution.py:291
  13.9 4.3 %collective-permute-start.5 = (bf16[256,128]{1,0:T(8,128)(2,1)S(1)}, bf16[256,128]{1,0:T(8,128)(2,1)S(1)}, u32[]{:S(2)}, u32[]{:S(2)}) collective-permute-start(bf16[256,128]{1,0:T(8,128)(2,1)S(1)} %get-tuple-element.25), channel_id=1, source_target_pairs={{0,16},{8,24},{16,0},{24,8},{1,17},{9,25},{17,1},{25,9},{2,18},{10... | collective-permute-start | bytes 196616 | tf_op jit(solution)/shard_map/ppermute | solution.py:291
  18.3 1.6 %collective-permute-start.6 = (bf16[256,512]{1,0:T(8,128)(2,1)S(1)}, bf16[256,512]{1,0:T(8,128)(2,1)S(1)}, u32[]{:S(2)}, u32[]{:S(2)}) collective-permute-start(bf16[256,512]{1,0:T(8,128)(2,1)S(1)} %gate.1.own_ref), channel_id=1, source_target_pairs={{0,1},{1,0},{2,3},{3,2},{4,5},{5,4},{6,7},{7,6},{8,9},{9,8},{10,11... | collective-permute-start | bytes 786440 | tf_op jit(solution)/shard_map/ppermute | solution.py:299
  20.2 9.6 %collective-permute-start.8 = (bf16[256,512]{1,0:T(8,128)(2,1)S(1)}, bf16[256,512]{1,0:T(8,128)(2,1)S(1)}, u32[]{:S(2)}, u32[]{:S(2)}) collective-permute-start(bf16[256,512]{1,0:T(8,128)(2,1)S(1)} %by_two.1), channel_id=1, source_target_pairs={{0,2},{1,3},{6,4},{7,5},{2,6},{3,7},{4,0},{5,1},{8,10},{9,11},{14,... | collective-permute-start | bytes 786440 | tf_op jit(solution)/shard_map/ppermute | solution.py:294
  23.3 12.0 %collective-permute-start.9 = (bf16[256,512]{1,0:T(8,128)(2,1)S(1)}, bf16[256,512]{1,0:T(8,128)(2,1)S(1)}, u32[]{:S(2)}, u32[]{:S(2)}) collective-permute-start(bf16[256,512]{1,0:T(8,128)(2,1)S(1)} %by_one.1), channel_id=1, source_target_pairs={{0,2},{1,3},{2,0},{3,1},{4,6},{5,7},{6,4},{7,5},{8,10},{9,11},{10,... | collective-permute-start | bytes 786440 | tf_op jit(solution)/shard_map/ppermute | solution.py:294
  29.8 12.3 %collective-permute-start.10 = (bf16[256,512]{1,0:T(8,128)(2,1)S(1)}, bf16[256,512]{1,0:T(8,128)(2,1)S(1)}, u32[]{:S(2)}, u32[]{:S(2)}) collective-permute-start(bf16[256,512]{1,0:T(8,128)(2,1)S(1)} %forward.1), channel_id=1, source_target_pairs={{0,6},{1,7},{6,0},{7,1},{2,4},{3,5},{4,2},{5,3},{8,14},{9,15},{14,... | collective-permute-start | bytes 786440 | tf_op jit(solution)/shard_map/ppermute | solution.py:294

commit v4 on v3

--- a/solution.py
+++ b/solution.py
@@ -9,6 +9,8 @@
 from jax.sharding import PartitionSpec as P
 
 LANES = 128
+FWD = ((3, 1, 2, 0), (2, 3, 1, 0))
+RET = ((3, 1, 2, 0), (2, 3, 1, 0))
 BF16 = jnp.bfloat16
 F32 = jnp.float32
 VMEM_LIMIT = 16 * 1024 * 1024
@@ -26,8 +28,8 @@
     return [pltpu.with_memory_space_constraint(a, pltpu.VMEM) for a in arrays]
 
 
-def far_first(n_seq):
-    return sorted(range(n_seq), key=lambda d: -d.bit_count())
+def away(orders, k):
+    return jnp.where(core_place() == 0, orders[0][k], orders[1][k])
 
 
 def seq_place():
@@ -72,15 +74,15 @@
         load.start()
     loads[0].wait()
     taps_f32[...] = taps_ref[...].astype(F32)
-    for d in range(n_seq):
-        own = taps_f32[rows_at(seq_place() ^ d, part), :]
+    for slot, packed_ref in enumerate(packed_refs):
+        own = taps_f32[rows_at(seq_place() ^ away(FWD, slot), part), :]
         pieces = [own[:, k * LANES : (k + 1) * LANES] for k in range(span // LANES)]
-        packed_refs[d][rows:, :] = jnp.concatenate(pieces, axis=0).astype(BF16)
+        packed_ref[rows:, :] = jnp.concatenate(pieces, axis=0).astype(BF16)
     loads[1].wait()
     loads[2].wait()
     mixed_ref[...] = (key_ref[...].astype(F32) * value_ref[...].astype(F32)).astype(BF16)
-    for d in range(n_seq):
-        packed_refs[d][0:rows, :] = mixed_ref[:, lanes_at(seq_place() ^ d)]
+    for slot, packed_ref in enumerate(packed_refs):
+        packed_ref[0:rows, :] = mixed_ref[:, lanes_at(seq_place() ^ away(FWD, slot))]
     loads[3].wait()
     loads[4].wait()
 
@@ -109,18 +111,18 @@
 
 
 def conv_kernel(n_seq, rows, part, *refs):
-    packed_refs = [refs[far_first(n_seq).index(d)] for d in range(n_seq)]
+    packed_refs = refs[:n_seq]
     out_refs = refs[n_seq : 2 * n_seq]
     signal, taps, total = refs[2 * n_seq :]
     per_shard = rows // LANES
     blocks = n_seq * per_shard
     group_width = LANES // part
 
-    for d in range(n_seq):
-        first = (seq_place() ^ d) * per_shard
-        tap_rows = packed_refs[d][rows:, :].astype(F32)
+    for slot, packed_ref in enumerate(packed_refs):
+        first = (seq_place() ^ away(FWD, slot)) * per_shard
+        tap_rows = packed_ref[rows:, :].astype(F32)
         for k in range(per_shard):
-            tokens = packed_refs[d][k * LANES : (k + 1) * LANES, :].astype(F32)
+            tokens = packed_ref[k * LANES : (k + 1) * LANES, :].astype(F32)
             signal[first + k] = tokens.T.astype(BF16)
             taps[first + k] = tap_rows[k * part : (k + 1) * part, :]
 
@@ -152,10 +154,10 @@
         for q in range(blocks):
             total[q, here, :] = sums[q]
 
-    for d in range(n_seq):
-        first = (seq_place() ^ d) * per_shard
+    for slot, out_ref in enumerate(out_refs):
+        first = (seq_place() ^ away(RET, slot)) * per_shard
         for k in range(per_shard):
-            out_refs[d][k * LANES : (k + 1) * LANES, :] = total[first + k].T.astype(BF16)
+            out_ref[k * LANES : (k + 1) * LANES, :] = total[first + k].T.astype(BF16)
 
 
 def convolve(packed, n_seq, rows, part):
@@ -173,16 +175,16 @@
         ],
         compiler_params=params(),
         name="convolve",
-    )(*[packed[d] for d in far_first(n_seq)])
+    )(*packed)
 
 
 def gate_kernel(n_seq, query_ref, mixed_ref, skip_ref, *refs):
-    conv_refs, out_ref = [refs[far_first(n_seq).index(d)] for d in range(n_seq)], refs[n_seq]
-    for d in range(n_seq):
-        lanes = lanes_at(seq_place() ^ d)
+    conv_refs, out_ref = refs[:n_seq], refs[n_seq]
+    for slot, conv_ref in enumerate(conv_refs):
+        lanes = lanes_at(seq_place() ^ away(RET, slot))
         direct = skip_ref[:, lanes] * mixed_ref[:, lanes].astype(F32)
         out_ref[:, lanes] = (
-            query_ref[:, lanes].astype(F32) * (conv_refs[d][...].astype(F32) + direct)
+            query_ref[:, lanes].astype(F32) * (conv_ref[...].astype(F32) + direct)
         ).astype(BF16)
 
 
@@ -195,7 +197,7 @@
         out_specs=vmem,
         compiler_params=params(),
         name="gate",
-    )(query_in, mixed_in, skip_gain, *[parts[d] for d in far_first(len(parts))])
+    )(query_in, mixed_in, skip_gain, *parts)
 
 
 def load_block(distance, weight_hbm, weight, arrived):
@@ -287,8 +289,17 @@
     groups = filter_taps.shape[0]
     part = groups // n_seq
     columns = out_weight.shape[1] // n_chan
-    def over_seq(value, d):
-        return lax.ppermute(value, "seq", [(i, i ^ d) for i in range(n_seq)])
+    def over_seq(slots, orders):
+        *going, staying = slots
+        moved = []
+        for k, value in enumerate(going):
+            pairs = [
+                (i * n_chan + j, (i ^ orders[j % 2][k]) * n_chan + j)
+                for i in range(n_seq)
+                for j in range(n_chan)
+            ]
+            moved.append(lax.ppermute(value, ("seq", "chan"), pairs))
+        return moved + [staying]
 
     def over_chips(value, moves):
         return lax.ppermute(
@@ -302,9 +313,9 @@
     mixed_in, query, skip, *packed = products(
         key_in, value_in, filter_taps, query_in, skip_gain, n_seq
     )
-    arrived = [packed[0]] + [over_seq(packed[d], d) for d in range(1, n_seq)]
+    arrived = over_seq(packed, FWD)
     convolved = convolve(arrived, n_seq, rows, part)
-    returned = [convolved[0]] + [over_seq(convolved[d], d) for d in range(1, n_seq)]
+    returned = over_seq(convolved, RET)
     gated = gate(query, mixed_in, skip, returned)
     gated_other = other_core(gated)
 

time: 43.3 us -> 42.8 us (0.988)
  waiting for transfers between devices: 17.2 us -> 16.5 us
    ppermute x6, waiting for transfers between devices: 7.65 us -> 6.96 us  [over_seq(): moved.append(lax.ppermute(value, ('seq', 'chan'), pairs))]
  transfers between devices with their start and end apart: 11 -> 11, of which waited for: 10 -> 9; matrix products, arithmetic and copies ran while one was open for 0% -> 0% of each run, Pallas kernels for 19% -> 20%
where the time goes in v4:
time: 42.8 us; the launch traced here: 42.5 us
  waiting for transfers between devices  16.5 us (39%)
  starting transfers between devices  16.4 us (38%)
  Pallas kernels  9.45 us (22%)
    ppermute x3, waiting for transfers between devices, over_chips(): lax.ppermute(value, 'chan', [(2 * a + c, 2 * b + c) for a, b in moves for...  9.38 us
    ppermute x3, starting transfers between devices, over_chips(): lax.ppermute(value, 'chan', [(2 * a + c, 2 * b + c) for a, b in moves for...  8.19 us
    ppermute x6, starting transfers between devices, over_seq(): moved.append(lax.ppermute(value, ('seq', 'chan'), pairs))  7.72 us
    pallas_call x7, Pallas kernels, run_kernel(): pl.pallas_call(kernel, out_shape=out_shape, in_specs=specs, out_specs=[vm...  7.02 us
    ppermute x6, waiting for transfers between devices, over_seq(): moved.append(lax.ppermute(value, ('seq', 'chan'), pairs))  6.96 us
    pallas_call x1, Pallas kernels, products(): pl.pallas_call(functools.partial(product_kernel, n_seq), out_shape=[here,...  1.26 us
    pallas_call x1, Pallas kernels, convolve(): pl.pallas_call(functools.partial(conv_kernel, n_seq, rows, part), out_sha...  1.04 us
  transfers between devices with their start and end apart: 11, of which 9 were waited for; matrix products, arithmetic and copies ran while one was open for 0% of the time, Pallas kernels for 20%

profile of v4, /device:TPU:0, one launch (start us, length us, event | category | flops | bytes accessed | tf_op | source)
XLA Modules:
  0.0 42.5 jit_solution(10871524400072466768)
XLA Ops:
  0.0 0.5 %collective-permute-start.7 = (bf16[512,4096]{1,0:T(8,128)(2,1)}, bf16[512,4096]{1,0:T(8,128)(2,1)S(1)}, u32[]{:S(2)}, u32[]{:S(2)}) collective-permute-start(bf16[512,4096]{1,0:T(8,128)(2,1)} %own_weight.7), channel_id=1, source_target_pairs={{0,1},{1,0},{2,3},{3,2},{4,5},{5,4},{6,7},{7,6},{8,9},{9,8},{10,11... | collective-permute-start | bytes 12582920 | tf_op jit(solution)/shard_map/ppermute | solution.py:310
  0.5 1.3 %products.1 = (bf16[256,512]{1,0:T(8,128)(2,1)S(1)}, bf16[256,512]{1,0:T(8,128)(2,1)S(1)}, f32[1,512]{1,0:T(1,128)S(1)}, bf16[272,128]{1,0:T(8,128)(2,1)S(1)}, b...) custom-call(bf16[256,512]{1,0:T(8,128)(2,1)} %key_hbm.1, ...), custom_call_target="tpu_custom_call" | custom-call | tf_op jit(solution)/shard_map/products/pallas_call | solution.py:96
  1.7 3.5 %collective-permute-start = (bf16[272,128]{1,0:T(8,128)(2,1)S(1)}, bf16[272,128]{1,0:T(8,128)(2,1)S(1)}, u32[]{:S(2)}, u32[]{:S(2)}) collective-permute-start(bf16[272,128]{1,0:T(8,128)(2,1)S(1)} %get-tuple-element.19), channel_id=1, source_target_pairs={{0,24},{1,17},{2,26},{3,19},{4,28},{5,21},{6,30},{7,23},{8,16},{9,... | collective-permute-start | bytes 208904 | tf_op jit(solution)/shard_map/ppermute | solution.py:301
  5.2 0.5 %collective-permute-start.1 = (bf16[272,128]{1,0:T(8,128)(2,1)S(1)}, bf16[272,128]{1,0:T(8,128)(2,1)S(1)}, u32[]{:S(2)}, u32[]{:S(2)}) collective-permute-start(bf16[272,128]{1,0:T(8,128)(2,1)S(1)} %get-tuple-element.20), channel_id=1, source_target_pairs={{0,8},{1,25},{2,10},{3,27},{4,12},{5,29},{6,14},{7,31},{8,0},{9,17... | collective-permute-start | bytes 208904 | tf_op jit(solution)/shard_map/ppermute | solution.py:301
  5.8 0.1 collective-permute-start.2
  5.9 1.9 %collective-permute-done.refs_0_ = bf16[272,128]{1,0:T(8,128)(2,1)S(1)} collective-permute-done((bf16[272,128]{1,0:T(8,128)(2,1)S(1)}, bf16[272,128]{1,0:T(8,128)(2,1)S(1)}, u32[]{:S(2)}, u32[]{:S(2)}) %collective-permute-start) | collective-permute-done | bytes 69664 | tf_op jit(solution)/shard_map/ppermute | solution.py:301
  7.8 2.1 %collective-permute-done.1.refs_1_ = bf16[272,128]{1,0:T(8,128)(2,1)S(1)} collective-permute-done((bf16[272,128]{1,0:T(8,128)(2,1)S(1)}, bf16[272,128]{1,0:T(8,128)(2,1)S(1)}, u32[]{:S(2)}, u32[]{:S(2)}) %collective-permute-start.1) | collective-permute-done | bytes 69664 | tf_op jit(solution)/shard_map/ppermute | solution.py:301
  9.9 0.2 collective-permute-done.2.refs_2_
  10.1 1.0 %convolve.1 = (bf16[256,128]{1,0:T(8,128)(2,1)S(1)}, bf16[256,128]{1,0:T(8,128)(2,1)S(1)}, bf16[256,128]{1,0:T(8,128)(2,1)S(1)}, bf16[256,128]{1,0:T(8,128)(2,1)S(1)}) custom-call(bf16[272,128]{1,0:T(8,128)(2,1)S(1)} %collective-permute-done.refs_0_, bf16[272,128]{1,0:T(8,128)(2,1)S(1)} %collective-permute-done.1.refs_1_, ...), custom_call_target="tpu_custom_call" | custom-call | tf_op jit(solution)/shard_map/convolve/pallas_call | solution.py:166
  11.1 1.7 %collective-permute-start.3 = (bf16[256,128]{1,0:T(8,128)(2,1)S(1)}, bf16[256,128]{1,0:T(8,128)(2,1)S(1)}, u32[]{:S(2)}, u32[]{:S(2)}) collective-permute-start(bf16[256,128]{1,0:T(8,128)(2,1)S(1)} %get-tuple-element.23), channel_id=1, source_target_pairs={{0,24},{1,17},{2,26},{3,19},{4,28},{5,21},{6,30},{7,23},{8,16},{9,... | collective-permute-start | bytes 196616 | tf_op jit(solution)/shard_map/ppermute | solution.py:301
  12.8 0.4 collective-permute-start.4
  13.2 1.5 %collective-permute-start.5 = (bf16[256,128]{1,0:T(8,128)(2,1)S(1)}, bf16[256,128]{1,0:T(8,128)(2,1)S(1)}, u32[]{:S(2)}, u32[]{:S(2)}) collective-permute-start(bf16[256,128]{1,0:T(8,128)(2,1)S(1)} %get-tuple-element.25), channel_id=1, source_target_pairs={{0,16},{1,9},{2,18},{3,11},{4,20},{5,13},{6,22},{7,15},{8,24},{9,1... | collective-permute-start | bytes 196616 | tf_op jit(solution)/shard_map/ppermute | solution.py:301
  14.7 1.8 %collective-permute-done.3.refs_0_ = bf16[256,128]{1,0:T(8,128)(2,1)S(1)} collective-permute-done((bf16[256,128]{1,0:T(8,128)(2,1)S(1)}, bf16[256,128]{1,0:T(8,128)(2,1)S(1)}, u32[]{:S(2)}, u32[]{:S(2)}) %collective-permute-start.3) | collective-permute-done | bytes 65568 | tf_op jit(solution)/shard_map/ppermute | solution.py:301
  16.5 0.9 %collective-permute-done.4.refs_1_ = bf16[256,128]{1,0:T(8,128)(2,1)S(1)} collective-permute-done((bf16[256,128]{1,0:T(8,128)(2,1)S(1)}, bf16[256,128]{1,0:T(8,128)(2,1)S(1)}, u32[]{:S(2)}, u32[]{:S(2)}) %collective-permute-start.4) | collective-permute-done | bytes 65568 | tf_op jit(solution)/shard_map/ppermute | solution.py:301
  17.4 0.0 collective-permute-done.5.refs_2_
  17.5 0.1 gate.1.own_ref
  17.6 0.1 collective-permute-start.6
  17.7 1.4 %half.1.half_ref = f32[256,512]{1,0:T(8,128)S(1)} custom-call(bf16[256,512]{1,0:T(8,128)(2,1)S(1)} %gate.1.own_ref, bf16[512,4096]{1,0:T(8,128)(2,1)} %own_weight.7), custom_call_target="tpu_custom_call" | custom-call | tf_op jit(solution)/shard_map/half/pallas_call | solution.py:261
  19.1 0.1 collective-permute-done.6.other_ref
  19.2 0.0 collective-permute-done.7.other_weight
  19.2 0.3 by_two.1
  19.5 1.8 %collective-permute-start.8 = (bf16[256,512]{1,0:T(8,128)(2,1)S(1)}, bf16[256,512]{1,0:T(8,128)(2,1)S(1)}, u32[]{:S(2)}, u32[]{:S(2)}) collective-permute-start(bf16[256,512]{1,0:T(8,128)(2,1)S(1)} %by_two.1), channel_id=1, source_target_pairs={{0,2},{1,3},{6,4},{7,5},{2,6},{3,7},{4,0},{5,1},{8,10},{9,11},{14,... | collective-permute-start | bytes 786440 | tf_op jit(solution)/shard_map/ppermute | solution.py:305
  21.3 1.5 %by_one.1 = bf16[256,512]{1,0:T(8,128)(2,1)S(1)} custom-call(bf16[256,512]{1,0:T(8,128)(2,1)S(1)} %gate.1.own_ref, bf16[256,512]{1,0:T(8,128)(2,1)S(1)} %collective-permute-done.6.other_ref, bf16[512,4096]{1,0:T(8,128)(2,1)} %own_weight.7, bf16[512,4096]{1,0:T(8,128)(2,1)S(1)} %collective-permute-done.7.other_weight), custom_call_target="tpu_custom_call" | custom-call | tf_op jit(solution)/shard_map/by_one/pallas_call | solution.py:261
  22.8 2.7 %collective-permute-start.9 = (bf16[256,512]{1,0:T(8,128)(2,1)S(1)}, bf16[256,512]{1,0:T(8,128)(2,1)S(1)}, u32[]{:S(2)}, u32[]{:S(2)}) collective-permute-start(bf16[256,512]{1,0:T(8,128)(2,1)S(1)} %by_one.1), channel_id=1, source_target_pairs={{0,2},{1,3},{2,0},{3,1},{4,6},{5,7},{6,4},{7,5},{8,10},{9,11},{10,... | collective-permute-start | bytes 786440 | tf_op jit(solution)/shard_map/ppermute | solution.py:305
  25.5 1.5 %by_three.1.own_ref = bf16[256,512]{1,0:T(8,128)(2,1)S(1)} custom-call(bf16[256,512]{1,0:T(8,128)(2,1)S(1)} %gate.1.own_ref, bf16[256,512]{1,0:T(8,128)(2,1)S(1)} %collective-permute-done.6.other_ref, bf16[512,4096]{1,0:T(8,128)(2,1)} %own_weight.7, bf16[512,4096]{1,0:T(8,128)(2,1)S(1)} %collective-permute-done.7.other_weight), custom_call_target="tpu_custom_call" | custom-call | tf_op jit(solution)/shard_map/by_three/pallas_call | solution.py:261
  27.0 2.3 %collective-permute-done.8.first_ref.arrived_ref = bf16[256,512]{1,0:T(8,128)(2,1)S(1)} collective-permute-done((bf16[256,512]{1,0:T(8,128)(2,1)S(1)}, bf16[256,512]{1,0:T(8,128)(2,1)S(1)}, u32[]{:S(2)}, u32[]{:S(2)}) %collective-permute-start.8) | collective-permute-done | bytes 262176 | tf_op jit(solution)/shard_map/ppermute | solution.py:305
  29.3 3.7 %collective-permute-start.10 = (bf16[256,512]{1,0:T(8,128)(2,1)S(1)}, bf16[256,512]{1,0:T(8,128)(2,1)S(1)}, u32[]{:S(2)}, u32[]{:S(2)}) collective-permute-start(bf16[256,512]{1,0:T(8,128)(2,1)S(1)} %forward.1), channel_id=1, source_target_pairs={{0,6},{1,7},{6,0},{7,1},{2,4},{3,5},{4,2},{5,3},{8,14},{9,15},{14,... | collective-permute-start | bytes 786440 | tf_op jit(solution)/shard_map/ppermute | solution.py:305
  33.0 1.5 %base.1.base_ref = f32[256,512]{1,0:T(8,128)S(1)} custom-call(bf16[256,512]{1,0:T(8,128)(2,1)S(1)} %gate.1.own_ref, bf16[256,512]{1,0:T(8,128)(2,1)S(1)} %collective-permute-done.6.other_ref, bf16[512,4096]{1,0:T(8,128)(2,1)} %own_weight.7, bf16[512,4096]{1,0:T(8,128)(2,1)S(1)} %collective-permute-done.7.other_weight, ...), custom_call_target="tpu_custom_call" | custom-call | tf_op jit(solution)/shard_map/base/pallas_call | solution.py:261
  34.6 0.2 collective-permute-done.9.pair_ref
  34.8 6.9 %collective-permute-done.10.mirror_ref = bf16[256,512]{1,0:T(8,128)(2,1)S(1)} collective-permute-done((bf16[256,512]{1,0:T(8,128)(2,1)S(1)}, bf16[256,512]{1,0:T(8,128)(2,1)S(1)}, u32[]{:S(2)}, u32[]{:S(2)}) %collective-permute-start.10) | collective-permute-done | bytes 262176 | tf_op jit(solution)/shard_map/ppermute | solution.py:305
  41.7 0.8 %final.1 = bf16[256,512]{1,0:T(8,128)(2,1)} custom-call(f32[256,512]{1,0:T(8,128)S(1)} %base.1.base_ref, bf16[256,512]{1,0:T(8,128)(2,1)S(1)} %collective-permute-done.9.pair_ref, bf16[256,512]{1,0:T(8,128)(2,1)S(1)} %collective-permute-done.10.mirror_ref), custom_call_target="tpu_custom_call" | custom-call | tf_op jit(solution)/shard_map/final/pallas_call | solution.py:261
  (1 shorter events, 0.0 us)
Async XLA Ops:
  0.0 19.2 %collective-permute-start.7 = (bf16[512,4096]{1,0:T(8,128)(2,1)}, bf16[512,4096]{1,0:T(8,128)(2,1)S(1)}, u32[]{:S(2)}, u32[]{:S(2)}) collective-permute-start(bf16[512,4096]{1,0:T(8,128)(2,1)} %own_weight.7), channel_id=1, source_target_pairs={{0,1},{1,0},{2,3},{3,2},{4,5},{5,4},{6,7},{7,6},{8,9},{9,8},{10,11... | collective-permute-start | bytes 12582920 | tf_op jit(solution)/shard_map/ppermute | solution.py:310
  1.7 6.1 %collective-permute-start = (bf16[272,128]{1,0:T(8,128)(2,1)S(1)}, bf16[272,128]{1,0:T(8,128)(2,1)S(1)}, u32[]{:S(2)}, u32[]{:S(2)}) collective-permute-start(bf16[272,128]{1,0:T(8,128)(2,1)S(1)} %get-tuple-element.19), channel_id=1, source_target_pairs={{0,24},{1,17},{2,26},{3,19},{4,28},{5,21},{6,30},{7,23},{8,16},{9,... | collective-permute-start | bytes 208904 | tf_op jit(solution)/shard_map/ppermute | solution.py:301
  5.2 4.7 %collective-permute-start.1 = (bf16[272,128]{1,0:T(8,128)(2,1)S(1)}, bf16[272,128]{1,0:T(8,128)(2,1)S(1)}, u32[]{:S(2)}, u32[]{:S(2)}) collective-permute-start(bf16[272,128]{1,0:T(8,128)(2,1)S(1)} %get-tuple-element.20), channel_id=1, source_target_pairs={{0,8},{1,25},{2,10},{3,27},{4,12},{5,29},{6,14},{7,31},{8,0},{9,17... | collective-permute-start | bytes 208904 | tf_op jit(solution)/shard_map/ppermute | solution.py:301
  5.8 4.3 %collective-permute-start.2 = (bf16[272,128]{1,0:T(8,128)(2,1)S(1)}, bf16[272,128]{1,0:T(8,128)(2,1)S(1)}, u32[]{:S(2)}, u32[]{:S(2)}) collective-permute-start(bf16[272,128]{1,0:T(8,128)(2,1)S(1)} %get-tuple-element.21), channel_id=1, source_target_pairs={{0,16},{1,9},{2,18},{3,11},{4,20},{5,13},{6,22},{7,15},{8,24},{9,1... | collective-permute-start | bytes 208904 | tf_op jit(solution)/shard_map/ppermute | solution.py:301
  11.1 5.4 %collective-permute-start.3 = (bf16[256,128]{1,0:T(8,128)(2,1)S(1)}, bf16[256,128]{1,0:T(8,128)(2,1)S(1)}, u32[]{:S(2)}, u32[]{:S(2)}) collective-permute-start(bf16[256,128]{1,0:T(8,128)(2,1)S(1)} %get-tuple-element.23), channel_id=1, source_target_pairs={{0,24},{1,17},{2,26},{3,19},{4,28},{5,21},{6,30},{7,23},{8,16},{9,... | collective-permute-start | bytes 196616 | tf_op jit(solution)/shard_map/ppermute | solution.py:301
  12.8 4.6 %collective-permute-start.4 = (bf16[256,128]{1,0:T(8,128)(2,1)S(1)}, bf16[256,128]{1,0:T(8,128)(2,1)S(1)}, u32[]{:S(2)}, u32[]{:S(2)}) collective-permute-start(bf16[256,128]{1,0:T(8,128)(2,1)S(1)} %get-tuple-element.24), channel_id=1, source_target_pairs={{0,8},{1,25},{2,10},{3,27},{4,12},{5,29},{6,14},{7,31},{8,0},{9,17... | collective-permute-start | bytes 196616 | tf_op jit(solution)/shard_map/ppermute | solution.py:301
  13.2 4.3 %collective-permute-start.5 = (bf16[256,128]{1,0:T(8,128)(2,1)S(1)}, bf16[256,128]{1,0:T(8,128)(2,1)S(1)}, u32[]{:S(2)}, u32[]{:S(2)}) collective-permute-start(bf16[256,128]{1,0:T(8,128)(2,1)S(1)} %get-tuple-element.25), channel_id=1, source_target_pairs={{0,16},{1,9},{2,18},{3,11},{4,20},{5,13},{6,22},{7,15},{8,24},{9,1... | collective-permute-start | bytes 196616 | tf_op jit(solution)/shard_map/ppermute | solution.py:301
  17.6 1.6 %collective-permute-start.6 = (bf16[256,512]{1,0:T(8,128)(2,1)S(1)}, bf16[256,512]{1,0:T(8,128)(2,1)S(1)}, u32[]{:S(2)}, u32[]{:S(2)}) collective-permute-start(bf16[256,512]{1,0:T(8,128)(2,1)S(1)} %gate.1.own_ref), channel_id=1, source_target_pairs={{0,1},{1,0},{2,3},{3,2},{4,5},{5,4},{6,7},{7,6},{8,9},{9,8},{10,11... | collective-permute-start | bytes 786440 | tf_op jit(solution)/shard_map/ppermute | solution.py:310
  19.5 9.8 %collective-permute-start.8 = (bf16[256,512]{1,0:T(8,128)(2,1)S(1)}, bf16[256,512]{1,0:T(8,128)(2,1)S(1)}, u32[]{:S(2)}, u32[]{:S(2)}) collective-permute-start(bf16[256,512]{1,0:T(8,128)(2,1)S(1)} %by_two.1), channel_id=1, source_target_pairs={{0,2},{1,3},{6,4},{7,5},{2,6},{3,7},{4,0},{5,1},{8,10},{9,11},{14,... | collective-permute-start | bytes 786440 | tf_op jit(solution)/shard_map/ppermute | solution.py:305
  22.8 11.9 %collective-permute-start.9 = (bf16[256,512]{1,0:T(8,128)(2,1)S(1)}, bf16[256,512]{1,0:T(8,128)(2,1)S(1)}, u32[]{:S(2)}, u32[]{:S(2)}) collective-permute-start(bf16[256,512]{1,0:T(8,128)(2,1)S(1)} %by_one.1), channel_id=1, source_target_pairs={{0,2},{1,3},{2,0},{3,1},{4,6},{5,7},{6,4},{7,5},{8,10},{9,11},{10,... | collective-permute-start | bytes 786440 | tf_op jit(solution)/shard_map/ppermute | solution.py:305
  29.3 12.4 %collective-permute-start.10 = (bf16[256,512]{1,0:T(8,128)(2,1)S(1)}, bf16[256,512]{1,0:T(8,128)(2,1)S(1)}, u32[]{:S(2)}, u32[]{:S(2)}) collective-permute-start(bf16[256,512]{1,0:T(8,128)(2,1)S(1)} %forward.1), channel_id=1, source_target_pairs={{0,6},{1,7},{6,0},{7,1},{2,4},{3,5},{4,2},{5,3},{8,14},{9,15},{14,... | collective-permute-start | bytes 786440 | tf_op jit(solution)/shard_map/ppermute | solution.py:305

commit v5 on v4

--- a/solution.py
+++ b/solution.py
@@ -9,8 +9,9 @@
 from jax.sharding import PartitionSpec as P
 
 LANES = 128
-FWD = ((3, 1, 2, 0), (2, 3, 1, 0))
-RET = ((3, 1, 2, 0), (2, 3, 1, 0))
+GOING = ((3, 1, 2, 0), (2, 3, 1, 0))
+RETURNING = GOING
+OUT_PARTS = 2
 BF16 = jnp.bfloat16
 F32 = jnp.float32
 VMEM_LIMIT = 16 * 1024 * 1024
@@ -24,10 +25,6 @@
     return [pltpu.with_memory_space_constraint(a, pltpu.HBM) for a in arrays]
 
 
-def in_vmem(*arrays):
-    return [pltpu.with_memory_space_constraint(a, pltpu.VMEM) for a in arrays]
-
-
 def away(orders, k):
     return jnp.where(core_place() == 0, orders[0][k], orders[1][k])
 
@@ -52,9 +49,9 @@
     return pl.ds(pl.multiple_of(block * size, size), size)
 
 
-def product_kernel(n_seq, key_hbm, value_hbm, taps_hbm, query_hbm, skip_hbm, *refs):
-    mixed_ref, query_ref, skip_ref, *packed_refs = refs[: n_seq + 3]
-    key_ref, value_ref, taps_ref, taps_f32, arrived = refs[n_seq + 3 :]
+def product_kernel(n_seq, key_hbm, value_hbm, taps_hbm, query_hbm, skip_hbm, weight_hbm, *refs):
+    mixed_ref, query_ref, skip_ref, weight_ref, *packed_refs = refs[: n_seq + 4]
+    key_ref, value_ref, taps_ref, taps_f32, arrived = refs[n_seq + 4 :]
     rows = key_ref.shape[0]
     groups, span = taps_ref.shape
     part = groups // n_seq
@@ -72,22 +69,23 @@
     ]
     for load in loads:
         load.start()
+    loads.append(load_block(2, weight_hbm, weight_ref, arrived.at[5])[1])
     loads[0].wait()
     taps_f32[...] = taps_ref[...].astype(F32)
     for slot, packed_ref in enumerate(packed_refs):
-        own = taps_f32[rows_at(seq_place() ^ away(FWD, slot), part), :]
+        own = taps_f32[rows_at(seq_place() ^ away(GOING, slot), part), :]
         pieces = [own[:, k * LANES : (k + 1) * LANES] for k in range(span // LANES)]
         packed_ref[rows:, :] = jnp.concatenate(pieces, axis=0).astype(BF16)
     loads[1].wait()
     loads[2].wait()
     mixed_ref[...] = (key_ref[...].astype(F32) * value_ref[...].astype(F32)).astype(BF16)
     for slot, packed_ref in enumerate(packed_refs):
-        packed_ref[0:rows, :] = mixed_ref[:, lanes_at(seq_place() ^ away(FWD, slot))]
-    loads[3].wait()
-    loads[4].wait()
-
-
-def products(key_in, value_in, taps, query_in, skip_gain, n_seq):
+        packed_ref[0:rows, :] = mixed_ref[:, lanes_at(seq_place() ^ away(GOING, slot))]
+    for load in loads[3:]:
+        load.wait()
+
+
+def products(key_in, value_in, taps, query_in, skip_gain, out_weight, columns, n_seq):
     rows, width = key_in.shape
     groups, span = taps.shape
     tap_rows = (groups // n_seq) * (span // LANES)
@@ -95,19 +93,25 @@
     packed = jax.ShapeDtypeStruct((rows + tap_rows, LANES), BF16)
     return pl.pallas_call(
         functools.partial(product_kernel, n_seq),
-        out_shape=[here, here, jax.ShapeDtypeStruct((1, width), F32)] + [packed] * n_seq,
-        in_specs=[pl.BlockSpec(memory_space=pl.ANY)] * 5,
-        out_specs=[pl.BlockSpec(memory_space=pltpu.VMEM)] * (n_seq + 3),
+        out_shape=[
+            here,
+            here,
+            jax.ShapeDtypeStruct((1, width), F32),
+            jax.ShapeDtypeStruct((width, columns), BF16),
+        ]
+        + [packed] * n_seq,
+        in_specs=[pl.BlockSpec(memory_space=pl.ANY)] * 6,
+        out_specs=[pl.BlockSpec(memory_space=pltpu.VMEM)] * (n_seq + 4),
         scratch_shapes=[
             pltpu.VMEM((rows, width), BF16),
             pltpu.VMEM((rows, width), BF16),
             pltpu.VMEM((groups, span), BF16),
             pltpu.VMEM((groups, span), F32),
-            pltpu.SemaphoreType.DMA((5,)),
+            pltpu.SemaphoreType.DMA((6,)),
         ],
         compiler_params=params(),
         name="products",
-    )(*in_hbm(key_in, value_in, taps, query_in, skip_gain.reshape(1, -1)))
+    )(*in_hbm(key_in, value_in, taps, query_in, skip_gain.reshape(1, -1), out_weight))
 
 
 def conv_kernel(n_seq, rows, part, *refs):
@@ -119,7 +123,7 @@
     group_width = LANES // part
 
     for slot, packed_ref in enumerate(packed_refs):
-        first = (seq_place() ^ away(FWD, slot)) * per_shard
+        first = (seq_place() ^ away(GOING, slot)) * per_shard
         tap_rows = packed_ref[rows:, :].astype(F32)
         for k in range(per_shard):
             tokens = packed_ref[k * LANES : (k + 1) * LANES, :].astype(F32)
@@ -155,7 +159,7 @@
             total[q, here, :] = sums[q]
 
     for slot, out_ref in enumerate(out_refs):
-        first = (seq_place() ^ away(RET, slot)) * per_shard
+        first = (seq_place() ^ away(RETURNING, slot)) * per_shard
         for k in range(per_shard):
             out_ref[k * LANES : (k + 1) * LANES, :] = total[first + k].T.astype(BF16)
 
@@ -181,7 +185,7 @@
 def gate_kernel(n_seq, query_ref, mixed_ref, skip_ref, *refs):
     conv_refs, out_ref = refs[:n_seq], refs[n_seq]
     for slot, conv_ref in enumerate(conv_refs):
-        lanes = lanes_at(seq_place() ^ away(RET, slot))
+        lanes = lanes_at(seq_place() ^ away(RETURNING, slot))
         direct = skip_ref[:, lanes] * mixed_ref[:, lanes].astype(F32)
         out_ref[:, lanes] = (
             query_ref[:, lanes].astype(F32) * (conv_ref[...].astype(F32) + direct)
@@ -207,8 +211,7 @@
     return block, load
 
 
-def half_kernel(own_ref, own_weight, out_ref, weight, arrived):
-    load_block(2, own_weight, weight, arrived)[1].wait()
+def half_kernel(own_ref, weight, out_ref):
     out_ref[...] = jnp.dot(own_ref[...], weight[...], preferred_element_type=F32)
 
 
@@ -236,11 +239,8 @@
     return (chip_place() == 0) | (chip_place() == 3)
 
 
-def base_kernel(own_ref, other_ref, own_weight, other_weight, first_ref, *refs):
-    early_refs, (out_ref, weight, arrived) = refs[:-3], refs[-3:]
+def base_kernel(own_ref, other_ref, own_weight, other_weight, first_ref, out_ref, weight, arrived):
     base = both_halves(0, own_ref, other_ref, own_weight, other_weight, weight, arrived)
-    for early in early_refs:
-        base += early[...].astype(F32)
 
     @pl.when(is_end())
     def _():
@@ -279,9 +279,31 @@
         out_ref[...] = (own_ref[...].astype(F32) + arrived_ref[...].astype(F32)).astype(BF16)
 
 
-def final_kernel(base_ref, pair_ref, mirror_ref, out_ref):
-    arrived = pair_ref[...].astype(F32) + mirror_ref[...].astype(F32)
-    out_ref[...] = (base_ref[...] + arrived).astype(BF16)
+def final_kernel(base_ref, pair_ref, mirror_ref, out_hbm, out_ref, arrived):
+    rows = out_ref.shape[0] // OUT_PARTS
+    stores = []
+    for k in range(OUT_PARTS):
+        here = slice(k * rows, (k + 1) * rows)
+        arrivals = pair_ref[here, :].astype(F32) + mirror_ref[here, :].astype(F32)
+        out_ref[here, :] = (base_ref[here, :] + arrivals).astype(BF16)
+        store = pltpu.make_async_copy(out_ref.at[here, :], out_hbm.at[here, :], arrived.at[k])
+        store.start()
+        stores.append(store)
+    for store in stores:
+        store.wait()
+
+
+def finish(base, pair, mirror):
+    vmem = pl.BlockSpec(memory_space=pltpu.VMEM)
+    return pl.pallas_call(
+        final_kernel,
+        out_shape=jax.ShapeDtypeStruct(base.shape, BF16),
+        in_specs=[vmem] * 3,
+        out_specs=pl.BlockSpec(memory_space=pl.ANY),
+        scratch_shapes=[pltpu.VMEM(base.shape, BF16), pltpu.SemaphoreType.DMA((OUT_PARTS,))],
+        compiler_params=params(),
+        name="final",
+    )(base, pair, mirror)
 
 
 def fast_body(n_seq, n_chan, query_in, key_in, value_in, filter_taps, skip_gain, out_weight):
@@ -310,12 +332,12 @@
         return lax.ppermute(value, "chan", [(i, i ^ 1) for i in range(n_chan)])
 
     other_weight = other_core(out_weight)
-    mixed_in, query, skip, *packed = products(
-        key_in, value_in, filter_taps, query_in, skip_gain, n_seq
-    )
-    arrived = over_seq(packed, FWD)
+    mixed_in, query, skip, weight, *packed = products(
+        key_in, value_in, filter_taps, query_in, skip_gain, out_weight, columns, n_seq
+    )
+    arrived = over_seq(packed, GOING)
     convolved = convolve(arrived, n_seq, rows, part)
-    returned = over_seq(convolved, RET)
+    returned = over_seq(convolved, RETURNING)
     gated = gate(query, mixed_in, skip, returned)
     gated_other = other_core(gated)
 
@@ -324,7 +346,7 @@
     one_weight = [pltpu.VMEM((width, columns), BF16), pltpu.SemaphoreType.DMA(())]
     halves = (gated, gated_other, out_weight, other_weight)
 
-    half = run_kernel(half_kernel, "half", block_f32, one_weight, gated, out_weight, hbm=(1,))
+    half = run_kernel(half_kernel, "half", block_f32, [], gated, weight)
     by_two = run_kernel(add_half_kernel, "by_two", block, [], half, gated_other, other_weight)
     first = over_chips(by_two, [(0, 1), (3, 2), (1, 3), (2, 0)])
     by_one = run_kernel(
@@ -337,7 +359,7 @@
     summed = run_kernel(forward_kernel, "forward", block, [], by_three, first)
     mirror = over_chips(summed, [(0, 3), (3, 0), (1, 2), (2, 1)])
     base = run_kernel(base_kernel, "base", block_f32, one_weight, *halves, first, hbm=(2,))
-    return run_kernel(final_kernel, "final", block, [], base, pair, mirror)
+    return finish(base, pair, mirror)
 
 
 def window_matrix(window, tile_size):
@@ -424,7 +446,7 @@
         part = groups // n_seq
         fits = (
             n_chan == 8
-            and n_seq & (n_seq - 1) == 0
+            and n_seq == len(GOING[0])
             and width == n_seq * LANES
             and part * n_seq == groups
             and part % 8 == 0

time: 42.8 us -> 42.6 us (level)
  Pallas kernels: 9.45 us -> 8.46 us
  waiting for transfers between devices: 16.5 us -> 17.4 us
    pallas_call x7 -> x6, Pallas kernels: 7.02 us -> 5.17 us  [run_kernel(): pl.pallas_call(kernel, out_shape=out_shape, in_specs=specs, out_specs=[vm...]
    ppermute x2, waiting for transfers between devices: 0.15 us -> 1.22 us  [other_core(): return lax.ppermute(value, 'chan', [(i, i ^ 1) for i in range(n_chan)])]
    pallas_call x0 -> x1, Pallas kernels: none -> 0.76 us  [finish(): pl.pallas_call(final_kernel, out_shape=jax.ShapeDtypeStruct(base.shape, B...]
  transfers between devices with their start and end apart: 11 -> 11, of which waited for: 9 -> 9; matrix products, arithmetic and copies ran while one was open for 0% -> 0% of each run, Pallas kernels for 20% -> 17%
where the time goes in v5:
time: 42.6 us; the launch traced here: 42.3 us
  waiting for transfers between devices  17.4 us (41%)
  starting transfers between devices  16.4 us (38%)
  Pallas kernels  8.46 us (20%)
    ppermute x3, waiting for transfers between devices, over_chips(): lax.ppermute(value, 'chan', [(2 * a + c, 2 * b + c) for a, b in moves for...  9.17 us
    ppermute x3, starting transfers between devices, over_chips(): lax.ppermute(value, 'chan', [(2 * a + c, 2 * b + c) for a, b in moves for...  8.17 us
    ppermute x6, starting transfers between devices, over_seq(): moved.append(lax.ppermute(value, ('seq', 'chan'), pairs))  7.72 us
    ppermute x6, waiting for transfers between devices, over_seq(): moved.append(lax.ppermute(value, ('seq', 'chan'), pairs))  6.97 us
    pallas_call x6, Pallas kernels, run_kernel(): pl.pallas_call(kernel, out_shape=out_shape, in_specs=specs, out_specs=[vm...  5.17 us
    pallas_call x1, Pallas kernels, products(): pl.pallas_call(functools.partial(product_kernel, n_seq), out_shape=[here,...  1.36 us
    ppermute x2, waiting for transfers between devices, other_core(): return lax.ppermute(value, 'chan', [(i, i ^ 1) for i in range(n_chan)])  1.22 us
    pallas_call x1, Pallas kernels, convolve(): pl.pallas_call(functools.partial(conv_kernel, n_seq, rows, part), out_sha...  1.04 us
  transfers between devices with their start and end apart: 11, of which 9 were waited for; matrix products, arithmetic and copies ran while one was open for 0% of the time, Pallas kernels for 17%

profile of v5, /device:TPU:0, one launch (start us, length us, event | category | flops | bytes accessed | tf_op | source)
XLA Modules:
  0.0 42.3 jit_solution(16227011597183541552)
XLA Ops:
  0.0 0.5 %collective-permute-start.7 = (bf16[512,4096]{1,0:T(8,128)(2,1)}, bf16[512,4096]{1,0:T(8,128)(2,1)S(1)}, u32[]{:S(2)}, u32[]{:S(2)}) collective-permute-start(bf16[512,4096]{1,0:T(8,128)(2,1)} %own_weight.5), channel_id=1, source_target_pairs={{0,1},{1,0},{2,3},{3,2},{4,5},{5,4},{6,7},{7,6},{8,9},{9,8},{10,11... | collective-permute-start | bytes 12582920 | tf_op jit(solution)/shard_map/ppermute | solution.py:332
  0.5 1.4 %products.1 = (bf16[256,512]{1,0:T(8,128)(2,1)S(1)}, bf16[256,512]{1,0:T(8,128)(2,1)S(1)}, f32[1,512]{1,0:T(1,128)S(1)}, bf16[512,512]{1,0:T(8,128)(2,1)S(1)}, b...) custom-call(bf16[256,512]{1,0:T(8,128)(2,1)} %key_hbm.1, ...), custom_call_target="tpu_custom_call" | custom-call | tf_op jit(solution)/shard_map/products/pallas_call | solution.py:94
  1.8 3.5 %collective-permute-start = (bf16[272,128]{1,0:T(8,128)(2,1)S(1)}, bf16[272,128]{1,0:T(8,128)(2,1)S(1)}, u32[]{:S(2)}, u32[]{:S(2)}) collective-permute-start(bf16[272,128]{1,0:T(8,128)(2,1)S(1)} %get-tuple-element.20), channel_id=1, source_target_pairs={{0,24},{1,17},{2,26},{3,19},{4,28},{5,21},{6,30},{7,23},{8,16},{9,... | collective-permute-start | bytes 208904 | tf_op jit(solution)/shard_map/ppermute | solution.py:323
  5.3 0.5 %collective-permute-start.1 = (bf16[272,128]{1,0:T(8,128)(2,1)S(1)}, bf16[272,128]{1,0:T(8,128)(2,1)S(1)}, u32[]{:S(2)}, u32[]{:S(2)}) collective-permute-start(bf16[272,128]{1,0:T(8,128)(2,1)S(1)} %get-tuple-element.21), channel_id=1, source_target_pairs={{0,8},{1,25},{2,10},{3,27},{4,12},{5,29},{6,14},{7,31},{8,0},{9,17... | collective-permute-start | bytes 208904 | tf_op jit(solution)/shard_map/ppermute | solution.py:323
  5.9 0.1 collective-permute-start.2
  6.0 1.9 %collective-permute-done.refs_0_ = bf16[272,128]{1,0:T(8,128)(2,1)S(1)} collective-permute-done((bf16[272,128]{1,0:T(8,128)(2,1)S(1)}, bf16[272,128]{1,0:T(8,128)(2,1)S(1)}, u32[]{:S(2)}, u32[]{:S(2)}) %collective-permute-start) | collective-permute-done | bytes 69664 | tf_op jit(solution)/shard_map/ppermute | solution.py:323
  7.9 2.1 %collective-permute-done.1.refs_1_ = bf16[272,128]{1,0:T(8,128)(2,1)S(1)} collective-permute-done((bf16[272,128]{1,0:T(8,128)(2,1)S(1)}, bf16[272,128]{1,0:T(8,128)(2,1)S(1)}, u32[]{:S(2)}, u32[]{:S(2)}) %collective-permute-start.1) | collective-permute-done | bytes 69664 | tf_op jit(solution)/shard_map/ppermute | solution.py:323
  10.0 0.2 collective-permute-done.2.refs_2_
  10.2 1.0 %convolve.1 = (bf16[256,128]{1,0:T(8,128)(2,1)S(1)}, bf16[256,128]{1,0:T(8,128)(2,1)S(1)}, bf16[256,128]{1,0:T(8,128)(2,1)S(1)}, bf16[256,128]{1,0:T(8,128)(2,1)S(1)}) custom-call(bf16[272,128]{1,0:T(8,128)(2,1)S(1)} %collective-permute-done.refs_0_, bf16[272,128]{1,0:T(8,128)(2,1)S(1)} %collective-permute-done.1.refs_1_, ...), custom_call_target="tpu_custom_call" | custom-call | tf_op jit(solution)/shard_map/convolve/pallas_call | solution.py:170
  11.2 1.7 %collective-permute-start.3 = (bf16[256,128]{1,0:T(8,128)(2,1)S(1)}, bf16[256,128]{1,0:T(8,128)(2,1)S(1)}, u32[]{:S(2)}, u32[]{:S(2)}) collective-permute-start(bf16[256,128]{1,0:T(8,128)(2,1)S(1)} %get-tuple-element.24), channel_id=1, source_target_pairs={{0,24},{1,17},{2,26},{3,19},{4,28},{5,21},{6,30},{7,23},{8,16},{9,... | collective-permute-start | bytes 196616 | tf_op jit(solution)/shard_map/ppermute | solution.py:323
  12.9 0.4 collective-permute-start.4
  13.3 1.5 %collective-permute-start.5 = (bf16[256,128]{1,0:T(8,128)(2,1)S(1)}, bf16[256,128]{1,0:T(8,128)(2,1)S(1)}, u32[]{:S(2)}, u32[]{:S(2)}) collective-permute-start(bf16[256,128]{1,0:T(8,128)(2,1)S(1)} %get-tuple-element.26), channel_id=1, source_target_pairs={{0,16},{1,9},{2,18},{3,11},{4,20},{5,13},{6,22},{7,15},{8,24},{9,1... | collective-permute-start | bytes 196616 | tf_op jit(solution)/shard_map/ppermute | solution.py:323
  14.8 1.8 %collective-permute-done.3.refs_0_ = bf16[256,128]{1,0:T(8,128)(2,1)S(1)} collective-permute-done((bf16[256,128]{1,0:T(8,128)(2,1)S(1)}, bf16[256,128]{1,0:T(8,128)(2,1)S(1)}, u32[]{:S(2)}, u32[]{:S(2)}) %collective-permute-start.3) | collective-permute-done | bytes 65568 | tf_op jit(solution)/shard_map/ppermute | solution.py:323
  16.6 0.9 %collective-permute-done.4.refs_1_ = bf16[256,128]{1,0:T(8,128)(2,1)S(1)} collective-permute-done((bf16[256,128]{1,0:T(8,128)(2,1)S(1)}, bf16[256,128]{1,0:T(8,128)(2,1)S(1)}, u32[]{:S(2)}, u32[]{:S(2)}) %collective-permute-start.4) | collective-permute-done | bytes 65568 | tf_op jit(solution)/shard_map/ppermute | solution.py:323
  17.5 0.0 collective-permute-done.5.refs_2_
  17.6 0.1 gate.1.own_ref
  17.7 0.1 collective-permute-start.6
  17.8 0.3 half.1.half_ref
  18.1 1.2 %collective-permute-done.6.other_ref = bf16[256,512]{1,0:T(8,128)(2,1)S(1)} collective-permute-done((bf16[256,512]{1,0:T(8,128)(2,1)S(1)}, bf16[256,512]{1,0:T(8,128)(2,1)S(1)}, u32[]{:S(2)}, u32[]{:S(2)}) %collective-permute-start.6) | collective-permute-done | bytes 262176 | tf_op jit(solution)/shard_map/ppermute | solution.py:332
  19.3 0.0 collective-permute-done.7.other_weight
  19.3 0.3 by_two.1
  19.6 1.8 %collective-permute-start.8 = (bf16[256,512]{1,0:T(8,128)(2,1)S(1)}, bf16[256,512]{1,0:T(8,128)(2,1)S(1)}, u32[]{:S(2)}, u32[]{:S(2)}) collective-permute-start(bf16[256,512]{1,0:T(8,128)(2,1)S(1)} %by_two.1), channel_id=1, source_target_pairs={{0,2},{1,3},{6,4},{7,5},{2,6},{3,7},{4,0},{5,1},{8,10},{9,11},{14,... | collective-permute-start | bytes 786440 | tf_op jit(solution)/shard_map/ppermute | solution.py:327
  21.4 1.5 %by_one.1 = bf16[256,512]{1,0:T(8,128)(2,1)S(1)} custom-call(bf16[256,512]{1,0:T(8,128)(2,1)S(1)} %gate.1.own_ref, bf16[256,512]{1,0:T(8,128)(2,1)S(1)} %collective-permute-done.6.other_ref, bf16[512,4096]{1,0:T(8,128)(2,1)} %own_weight.5, bf16[512,4096]{1,0:T(8,128)(2,1)S(1)} %collective-permute-done.7.other_weight), custom_call_target="tpu_custom_call" | custom-call | tf_op jit(solution)/shard_map/by_one/pallas_call | solution.py:261
  22.9 2.7 %collective-permute-start.9 = (bf16[256,512]{1,0:T(8,128)(2,1)S(1)}, bf16[256,512]{1,0:T(8,128)(2,1)S(1)}, u32[]{:S(2)}, u32[]{:S(2)}) collective-permute-start(bf16[256,512]{1,0:T(8,128)(2,1)S(1)} %by_one.1), channel_id=1, source_target_pairs={{0,2},{1,3},{2,0},{3,1},{4,6},{5,7},{6,4},{7,5},{8,10},{9,11},{10,... | collective-permute-start | bytes 786440 | tf_op jit(solution)/shard_map/ppermute | solution.py:327
  25.6 1.5 %by_three.1.own_ref = bf16[256,512]{1,0:T(8,128)(2,1)S(1)} custom-call(bf16[256,512]{1,0:T(8,128)(2,1)S(1)} %gate.1.own_ref, bf16[256,512]{1,0:T(8,128)(2,1)S(1)} %collective-permute-done.6.other_ref, bf16[512,4096]{1,0:T(8,128)(2,1)} %own_weight.5, bf16[512,4096]{1,0:T(8,128)(2,1)S(1)} %collective-permute-done.7.other_weight), custom_call_target="tpu_custom_call" | custom-call | tf_op jit(solution)/shard_map/by_three/pallas_call | solution.py:261
  27.1 2.0 %collective-permute-done.8.first_ref.arrived_ref = bf16[256,512]{1,0:T(8,128)(2,1)S(1)} collective-permute-done((bf16[256,512]{1,0:T(8,128)(2,1)S(1)}, bf16[256,512]{1,0:T(8,128)(2,1)S(1)}, u32[]{:S(2)}, u32[]{:S(2)}) %collective-permute-start.8) | collective-permute-done | bytes 262176 | tf_op jit(solution)/shard_map/ppermute | solution.py:327
  29.2 3.7 %collective-permute-start.10 = (bf16[256,512]{1,0:T(8,128)(2,1)S(1)}, bf16[256,512]{1,0:T(8,128)(2,1)S(1)}, u32[]{:S(2)}, u32[]{:S(2)}) collective-permute-start(bf16[256,512]{1,0:T(8,128)(2,1)S(1)} %forward.1), channel_id=1, source_target_pairs={{0,6},{1,7},{6,0},{7,1},{2,4},{3,5},{4,2},{5,3},{8,14},{9,15},{14,... | collective-permute-start | bytes 786440 | tf_op jit(solution)/shard_map/ppermute | solution.py:327
  32.9 1.5 %base.1.base_ref = f32[256,512]{1,0:T(8,128)S(1)} custom-call(bf16[256,512]{1,0:T(8,128)(2,1)S(1)} %gate.1.own_ref, bf16[256,512]{1,0:T(8,128)(2,1)S(1)} %collective-permute-done.6.other_ref, bf16[512,4096]{1,0:T(8,128)(2,1)} %own_weight.5, bf16[512,4096]{1,0:T(8,128)(2,1)S(1)} %collective-permute-done.7.other_weight, ...), custom_call_target="tpu_custom_call" | custom-call | tf_op jit(solution)/shard_map/base/pallas_call | solution.py:261
  34.4 0.2 collective-permute-done.9.pair_ref
  34.7 6.9 %collective-permute-done.10.mirror_ref = bf16[256,512]{1,0:T(8,128)(2,1)S(1)} collective-permute-done((bf16[256,512]{1,0:T(8,128)(2,1)S(1)}, bf16[256,512]{1,0:T(8,128)(2,1)S(1)}, u32[]{:S(2)}, u32[]{:S(2)}) %collective-permute-start.10) | collective-permute-done | bytes 262176 | tf_op jit(solution)/shard_map/ppermute | solution.py:327
  41.6 0.8 %final.1 = bf16[256,512]{1,0:T(8,128)(2,1)} custom-call(f32[256,512]{1,0:T(8,128)S(1)} %base.1.base_ref, bf16[256,512]{1,0:T(8,128)(2,1)S(1)} %collective-permute-done.9.pair_ref, bf16[256,512]{1,0:T(8,128)(2,1)S(1)} %collective-permute-done.10.mirror_ref), custom_call_target="tpu_custom_call" | custom-call | tf_op jit(solution)/shard_map/final/pallas_call | solution.py:298
  (1 shorter events, 0.0 us)
Async XLA Ops:
  0.0 19.3 %collective-permute-start.7 = (bf16[512,4096]{1,0:T(8,128)(2,1)}, bf16[512,4096]{1,0:T(8,128)(2,1)S(1)}, u32[]{:S(2)}, u32[]{:S(2)}) collective-permute-start(bf16[512,4096]{1,0:T(8,128)(2,1)} %own_weight.5), channel_id=1, source_target_pairs={{0,1},{1,0},{2,3},{3,2},{4,5},{5,4},{6,7},{7,6},{8,9},{9,8},{10,11... | collective-permute-start | bytes 12582920 | tf_op jit(solution)/shard_map/ppermute | solution.py:332
  1.8 6.1 %collective-permute-start = (bf16[272,128]{1,0:T(8,128)(2,1)S(1)}, bf16[272,128]{1,0:T(8,128)(2,1)S(1)}, u32[]{:S(2)}, u32[]{:S(2)}) collective-permute-start(bf16[272,128]{1,0:T(8,128)(2,1)S(1)} %get-tuple-element.20), channel_id=1, source_target_pairs={{0,24},{1,17},{2,26},{3,19},{4,28},{5,21},{6,30},{7,23},{8,16},{9,... | collective-permute-start | bytes 208904 | tf_op jit(solution)/shard_map/ppermute | solution.py:323
  5.3 4.7 %collective-permute-start.1 = (bf16[272,128]{1,0:T(8,128)(2,1)S(1)}, bf16[272,128]{1,0:T(8,128)(2,1)S(1)}, u32[]{:S(2)}, u32[]{:S(2)}) collective-permute-start(bf16[272,128]{1,0:T(8,128)(2,1)S(1)} %get-tuple-element.21), channel_id=1, source_target_pairs={{0,8},{1,25},{2,10},{3,27},{4,12},{5,29},{6,14},{7,31},{8,0},{9,17... | collective-permute-start | bytes 208904 | tf_op jit(solution)/shard_map/ppermute | solution.py:323
  5.9 4.3 %collective-permute-start.2 = (bf16[272,128]{1,0:T(8,128)(2,1)S(1)}, bf16[272,128]{1,0:T(8,128)(2,1)S(1)}, u32[]{:S(2)}, u32[]{:S(2)}) collective-permute-start(bf16[272,128]{1,0:T(8,128)(2,1)S(1)} %get-tuple-element.22), channel_id=1, source_target_pairs={{0,16},{1,9},{2,18},{3,11},{4,20},{5,13},{6,22},{7,15},{8,24},{9,1... | collective-permute-start | bytes 208904 | tf_op jit(solution)/shard_map/ppermute | solution.py:323
  11.2 5.4 %collective-permute-start.3 = (bf16[256,128]{1,0:T(8,128)(2,1)S(1)}, bf16[256,128]{1,0:T(8,128)(2,1)S(1)}, u32[]{:S(2)}, u32[]{:S(2)}) collective-permute-start(bf16[256,128]{1,0:T(8,128)(2,1)S(1)} %get-tuple-element.24), channel_id=1, source_target_pairs={{0,24},{1,17},{2,26},{3,19},{4,28},{5,21},{6,30},{7,23},{8,16},{9,... | collective-permute-start | bytes 196616 | tf_op jit(solution)/shard_map/ppermute | solution.py:323
  12.9 4.6 %collective-permute-start.4 = (bf16[256,128]{1,0:T(8,128)(2,1)S(1)}, bf16[256,128]{1,0:T(8,128)(2,1)S(1)}, u32[]{:S(2)}, u32[]{:S(2)}) collective-permute-start(bf16[256,128]{1,0:T(8,128)(2,1)S(1)} %get-tuple-element.25), channel_id=1, source_target_pairs={{0,8},{1,25},{2,10},{3,27},{4,12},{5,29},{6,14},{7,31},{8,0},{9,17... | collective-permute-start | bytes 196616 | tf_op jit(solution)/shard_map/ppermute | solution.py:323
  13.3 4.3 %collective-permute-start.5 = (bf16[256,128]{1,0:T(8,128)(2,1)S(1)}, bf16[256,128]{1,0:T(8,128)(2,1)S(1)}, u32[]{:S(2)}, u32[]{:S(2)}) collective-permute-start(bf16[256,128]{1,0:T(8,128)(2,1)S(1)} %get-tuple-element.26), channel_id=1, source_target_pairs={{0,16},{1,9},{2,18},{3,11},{4,20},{5,13},{6,22},{7,15},{8,24},{9,1... | collective-permute-start | bytes 196616 | tf_op jit(solution)/shard_map/ppermute | solution.py:323
  17.7 1.6 %collective-permute-start.6 = (bf16[256,512]{1,0:T(8,128)(2,1)S(1)}, bf16[256,512]{1,0:T(8,128)(2,1)S(1)}, u32[]{:S(2)}, u32[]{:S(2)}) collective-permute-start(bf16[256,512]{1,0:T(8,128)(2,1)S(1)} %gate.1.own_ref), channel_id=1, source_target_pairs={{0,1},{1,0},{2,3},{3,2},{4,5},{5,4},{6,7},{7,6},{8,9},{9,8},{10,11... | collective-permute-start | bytes 786440 | tf_op jit(solution)/shard_map/ppermute | solution.py:332
  19.6 9.5 %collective-permute-start.8 = (bf16[256,512]{1,0:T(8,128)(2,1)S(1)}, bf16[256,512]{1,0:T(8,128)(2,1)S(1)}, u32[]{:S(2)}, u32[]{:S(2)}) collective-permute-start(bf16[256,512]{1,0:T(8,128)(2,1)S(1)} %by_two.1), channel_id=1, source_target_pairs={{0,2},{1,3},{6,4},{7,5},{2,6},{3,7},{4,0},{5,1},{8,10},{9,11},{14,... | collective-permute-start | bytes 786440 | tf_op jit(solution)/shard_map/ppermute | solution.py:327
  22.9 11.7 %collective-permute-start.9 = (bf16[256,512]{1,0:T(8,128)(2,1)S(1)}, bf16[256,512]{1,0:T(8,128)(2,1)S(1)}, u32[]{:S(2)}, u32[]{:S(2)}) collective-permute-start(bf16[256,512]{1,0:T(8,128)(2,1)S(1)} %by_one.1), channel_id=1, source_target_pairs={{0,2},{1,3},{2,0},{3,1},{4,6},{5,7},{6,4},{7,5},{8,10},{9,11},{10,... | collective-permute-start | bytes 786440 | tf_op jit(solution)/shard_map/ppermute | solution.py:327
  29.2 12.4 %collective-permute-start.10 = (bf16[256,512]{1,0:T(8,128)(2,1)S(1)}, bf16[256,512]{1,0:T(8,128)(2,1)S(1)}, u32[]{:S(2)}, u32[]{:S(2)}) collective-permute-start(bf16[256,512]{1,0:T(8,128)(2,1)S(1)} %forward.1), channel_id=1, source_target_pairs={{0,6},{1,7},{6,0},{7,1},{2,4},{3,5},{4,2},{5,3},{8,14},{9,15},{14,... | collective-permute-start | bytes 786440 | tf_op jit(solution)/shard_map/ppermute | solution.py:327

commit v6 on v5

--- a/solution.py
+++ b/solution.py
@@ -49,9 +49,9 @@
     return pl.ds(pl.multiple_of(block * size, size), size)
 
 
-def product_kernel(n_seq, key_hbm, value_hbm, taps_hbm, query_hbm, skip_hbm, weight_hbm, *refs):
-    mixed_ref, query_ref, skip_ref, weight_ref, *packed_refs = refs[: n_seq + 4]
-    key_ref, value_ref, taps_ref, taps_f32, arrived = refs[n_seq + 4 :]
+def product_kernel(n_seq, key_hbm, value_hbm, taps_hbm, *refs):
+    mixed_ref, *packed_refs = refs[: n_seq + 1]
+    key_ref, value_ref, taps_ref, taps_f32, arrived = refs[n_seq + 1 :]
     rows = key_ref.shape[0]
     groups, span = taps_ref.shape
     part = groups // n_seq
@@ -62,14 +62,11 @@
                 (taps_hbm, taps_ref),
                 (key_hbm, key_ref),
                 (value_hbm, value_ref),
-                (query_hbm, query_ref),
-                (skip_hbm, skip_ref),
             ]
         )
     ]
     for load in loads:
         load.start()
-    loads.append(load_block(2, weight_hbm, weight_ref, arrived.at[5])[1])
     loads[0].wait()
     taps_f32[...] = taps_ref[...].astype(F32)
     for slot, packed_ref in enumerate(packed_refs):
@@ -81,11 +78,9 @@
     mixed_ref[...] = (key_ref[...].astype(F32) * value_ref[...].astype(F32)).astype(BF16)
     for slot, packed_ref in enumerate(packed_refs):
         packed_ref[0:rows, :] = mixed_ref[:, lanes_at(seq_place() ^ away(GOING, slot))]
-    for load in loads[3:]:
-        load.wait()
-
-
-def products(key_in, value_in, taps, query_in, skip_gain, out_weight, columns, n_seq):
+
+
+def products(key_in, value_in, taps, n_seq):
     rows, width = key_in.shape
     groups, span = taps.shape
     tap_rows = (groups // n_seq) * (span // LANES)
@@ -93,25 +88,49 @@
     packed = jax.ShapeDtypeStruct((rows + tap_rows, LANES), BF16)
     return pl.pallas_call(
         functools.partial(product_kernel, n_seq),
-        out_shape=[
-            here,
-            here,
-            jax.ShapeDtypeStruct((1, width), F32),
-            jax.ShapeDtypeStruct((width, columns), BF16),
-        ]
-        + [packed] * n_seq,
-        in_specs=[pl.BlockSpec(memory_space=pl.ANY)] * 6,
-        out_specs=[pl.BlockSpec(memory_space=pltpu.VMEM)] * (n_seq + 4),
+        out_shape=[here] + [packed] * n_seq,
+        in_specs=[pl.BlockSpec(memory_space=pl.ANY)] * 3,
+        out_specs=[pl.BlockSpec(memory_space=pltpu.VMEM)] * (n_seq + 1),
         scratch_shapes=[
             pltpu.VMEM((rows, width), BF16),
             pltpu.VMEM((rows, width), BF16),
             pltpu.VMEM((groups, span), BF16),
             pltpu.VMEM((groups, span), F32),
-            pltpu.SemaphoreType.DMA((6,)),
+            pltpu.SemaphoreType.DMA((3,)),
         ],
         compiler_params=params(),
         name="products",
-    )(*in_hbm(key_in, value_in, taps, query_in, skip_gain.reshape(1, -1), out_weight))
+    )(*in_hbm(key_in, value_in, taps))
+
+
+def fetch_kernel(after_hbm, query_hbm, skip_hbm, weight_hbm, query_ref, skip_ref, weight_ref, arrived):
+    loads = [
+        pltpu.make_async_copy(query_hbm, query_ref, arrived.at[0]),
+        pltpu.make_async_copy(skip_hbm, skip_ref, arrived.at[1]),
+    ]
+    for load in loads:
+        load.start()
+    loads.append(load_block(2, weight_hbm, weight_ref, arrived.at[2])[1])
+    for load in loads:
+        load.wait()
+
+
+def fetch(after, query_in, skip_gain, out_weight, columns):
+    vmem = pl.BlockSpec(memory_space=pltpu.VMEM)
+    width = query_in.shape[1]
+    return pl.pallas_call(
+        fetch_kernel,
+        out_shape=[
+            jax.ShapeDtypeStruct(query_in.shape, BF16),
+            jax.ShapeDtypeStruct((1, width), F32),
+            jax.ShapeDtypeStruct((width, columns), BF16),
+        ],
+        in_specs=[pl.BlockSpec(memory_space=pl.ANY)] * 4,
+        out_specs=[vmem] * 3,
+        scratch_shapes=[pltpu.SemaphoreType.DMA((3,))],
+        compiler_params=params(),
+        name="fetch",
+    )(after, *in_hbm(query_in, skip_gain.reshape(1, -1), out_weight))
 
 
 def conv_kernel(n_seq, rows, part, *refs):
@@ -332,10 +351,9 @@
         return lax.ppermute(value, "chan", [(i, i ^ 1) for i in range(n_chan)])
 
     other_weight = other_core(out_weight)
-    mixed_in, query, skip, weight, *packed = products(
-        key_in, value_in, filter_taps, query_in, skip_gain, out_weight, columns, n_seq
-    )
+    mixed_in, *packed = products(key_in, value_in, filter_taps, n_seq)
     arrived = over_seq(packed, GOING)
+    query, skip, weight = fetch(packed[-1], query_in, skip_gain, out_weight, columns)
     convolved = convolve(arrived, n_seq, rows, part)
     returned = over_seq(convolved, RETURNING)
     gated = gate(query, mixed_in, skip, returned)

time: 42.6 us -> 42.5 us (level)
  waiting for transfers between devices: 17.4 us -> 16.2 us
  Pallas kernels: 8.46 us -> 9.5 us
    ppermute x6, waiting for transfers between devices: 6.97 us -> 5.79 us  [over_seq(): moved.append(lax.ppermute(value, ('seq', 'chan'), pairs))]
    pallas_call x1 -> x2, Pallas kernels: 1.36 us -> 2.4 us  [the longest x1 1.24 us: products(): pl.pallas_call(functools.partial(product_kernel, n_seq), out_shape=[here]...]
  transfers between devices with their start and end apart: 11 -> 11, of which waited for: 9 -> 9; matrix products, arithmetic and copies ran while one was open for 0% -> 0% of each run, Pallas kernels for 17% -> 20%
where the time goes in v6:
time: 42.5 us; the launch traced here: 42.2 us
  starting transfers between devices  16.4 us (39%)
  waiting for transfers between devices  16.2 us (38%)
  Pallas kernels  9.5 us (22%)
    ppermute x3, waiting for transfers between devices, over_chips(): lax.ppermute(value, 'chan', [(2 * a + c, 2 * b + c) for a, b in moves for...  9.17 us
    ppermute x3, starting transfers between devices, over_chips(): lax.ppermute(value, 'chan', [(2 * a + c, 2 * b + c) for a, b in moves for...  8.17 us
    ppermute x6, starting transfers between devices, over_seq(): moved.append(lax.ppermute(value, ('seq', 'chan'), pairs))  7.72 us
    ppermute x6, waiting for transfers between devices, over_seq(): moved.append(lax.ppermute(value, ('seq', 'chan'), pairs))  5.79 us
    pallas_call x6, Pallas kernels, run_kernel(): pl.pallas_call(kernel, out_shape=out_shape, in_specs=specs, out_specs=[vm...  5.16 us
    pallas_call x1, Pallas kernels, products(): pl.pallas_call(functools.partial(product_kernel, n_seq), out_shape=[here]...  1.24 us
    ppermute x2, waiting for transfers between devices, other_core(): return lax.ppermute(value, 'chan', [(i, i ^ 1) for i in range(n_chan)])  1.22 us
    pallas_call x1, Pallas kernels, fetch(): pl.pallas_call(fetch_kernel, out_shape=[jax.ShapeDtypeStruct(query_in.sha...  1.16 us
  transfers between devices with their start and end apart: 11, of which 9 were waited for; matrix products, arithmetic and copies ran while one was open for 0% of the time, Pallas kernels for 20%

profile of v6, /device:TPU:0, one launch (start us, length us, event | category | flops | bytes accessed | tf_op | source)
XLA Modules:
  0.0 42.2 jit_solution(3250779255384666641)
XLA Ops:
  0.0 0.5 %collective-permute-start.7 = (bf16[512,4096]{1,0:T(8,128)(2,1)}, bf16[512,4096]{1,0:T(8,128)(2,1)S(1)}, u32[]{:S(2)}, u32[]{:S(2)}) collective-permute-start(bf16[512,4096]{1,0:T(8,128)(2,1)} %own_weight.5), channel_id=1, source_target_pairs={{0,1},{1,0},{2,3},{3,2},{4,5},{5,4},{6,7},{7,6},{8,9},{9,8},{10,11... | collective-permute-start | bytes 12582920 | tf_op jit(solution)/shard_map/ppermute | solution.py:351
  0.5 1.2 %products.1 = (bf16[256,512]{1,0:T(8,128)(2,1)S(1)}, bf16[272,128]{1,0:T(8,128)(2,1)S(1)}, bf16[272,128]{1,0:T(8,128)(2,1)S(1)}, bf16[272,128]{1,0:T(8,128)(2,1)S(1)}, bf16[272,128]{1,0:T(8,128)(2,1)S(1)}) custom-call(bf16[256,512]{1,0:T(8,128)(2,1)} %key_hbm.1, bf16[256,512]{1,0:T(8,128)(2,1)} %value_hbm.1, bf16[32,256]{1,0:T(8,128)(2,1)} %taps_hbm.1), custom_call_target="tpu_custom_call" | custom-call | tf_op jit(solution)/shard_map/products/pallas_call | solution.py:89
  1.7 3.5 %collective-permute-start = (bf16[272,128]{1,0:T(8,128)(2,1)S(1)}, bf16[272,128]{1,0:T(8,128)(2,1)S(1)}, u32[]{:S(2)}, u32[]{:S(2)}) collective-permute-start(bf16[272,128]{1,0:T(8,128)(2,1)S(1)} %get-tuple-element.21), channel_id=1, source_target_pairs={{0,24},{1,17},{2,26},{3,19},{4,28},{5,21},{6,30},{7,23},{8,16},{9,... | collective-permute-start | bytes 208904 | tf_op jit(solution)/shard_map/ppermute | solution.py:342
  5.2 0.5 %collective-permute-start.1 = (bf16[272,128]{1,0:T(8,128)(2,1)S(1)}, bf16[272,128]{1,0:T(8,128)(2,1)S(1)}, u32[]{:S(2)}, u32[]{:S(2)}) collective-permute-start(bf16[272,128]{1,0:T(8,128)(2,1)S(1)} %get-tuple-element.22), channel_id=1, source_target_pairs={{0,8},{1,25},{2,10},{3,27},{4,12},{5,29},{6,14},{7,31},{8,0},{9,17... | collective-permute-start | bytes 208904 | tf_op jit(solution)/shard_map/ppermute | solution.py:342
  5.7 0.1 collective-permute-start.2
  5.8 1.9 %collective-permute-done.refs_0_ = bf16[272,128]{1,0:T(8,128)(2,1)S(1)} collective-permute-done((bf16[272,128]{1,0:T(8,128)(2,1)S(1)}, bf16[272,128]{1,0:T(8,128)(2,1)S(1)}, u32[]{:S(2)}, u32[]{:S(2)}) %collective-permute-start) | collective-permute-done | bytes 69664 | tf_op jit(solution)/shard_map/ppermute | solution.py:342
  7.8 2.1 %collective-permute-done.1.refs_1_ = bf16[272,128]{1,0:T(8,128)(2,1)S(1)} collective-permute-done((bf16[272,128]{1,0:T(8,128)(2,1)S(1)}, bf16[272,128]{1,0:T(8,128)(2,1)S(1)}, u32[]{:S(2)}, u32[]{:S(2)}) %collective-permute-start.1) | collective-permute-done | bytes 69664 | tf_op jit(solution)/shard_map/ppermute | solution.py:342
  9.9 0.2 collective-permute-done.2.refs_2_
  10.1 1.0 %convolve.1 = (bf16[256,128]{1,0:T(8,128)(2,1)S(1)}, bf16[256,128]{1,0:T(8,128)(2,1)S(1)}, bf16[256,128]{1,0:T(8,128)(2,1)S(1)}, bf16[256,128]{1,0:T(8,128)(2,1)S(1)}) custom-call(bf16[272,128]{1,0:T(8,128)(2,1)S(1)} %collective-permute-done.refs_0_, bf16[272,128]{1,0:T(8,128)(2,1)S(1)} %collective-permute-done.1.refs_1_, ...), custom_call_target="tpu_custom_call" | custom-call | tf_op jit(solution)/shard_map/convolve/pallas_call | solution.py:189
  11.1 1.7 %collective-permute-start.3 = (bf16[256,128]{1,0:T(8,128)(2,1)S(1)}, bf16[256,128]{1,0:T(8,128)(2,1)S(1)}, u32[]{:S(2)}, u32[]{:S(2)}) collective-permute-start(bf16[256,128]{1,0:T(8,128)(2,1)S(1)} %get-tuple-element.24), channel_id=1, source_target_pairs={{0,24},{1,17},{2,26},{3,19},{4,28},{5,21},{6,30},{7,23},{8,16},{9,... | collective-permute-start | bytes 196616 | tf_op jit(solution)/shard_map/ppermute | solution.py:342
  12.8 0.4 collective-permute-start.4
  13.2 1.5 %collective-permute-start.5 = (bf16[256,128]{1,0:T(8,128)(2,1)S(1)}, bf16[256,128]{1,0:T(8,128)(2,1)S(1)}, u32[]{:S(2)}, u32[]{:S(2)}) collective-permute-start(bf16[256,128]{1,0:T(8,128)(2,1)S(1)} %get-tuple-element.26), channel_id=1, source_target_pairs={{0,16},{1,9},{2,18},{3,11},{4,20},{5,13},{6,22},{7,15},{8,24},{9,1... | collective-permute-start | bytes 196616 | tf_op jit(solution)/shard_map/ppermute | solution.py:342
  14.7 1.2 %fetch.1 = (bf16[256,512]{1,0:T(8,128)(2,1)S(1)}, f32[1,512]{1,0:T(1,128)S(1)}, bf16[512,512]{1,0:T(8,128)(2,1)S(1)}) custom-call(bf16[272,128]{1,0:T(8,128)(2,1)S(1)} %get-tuple-element.17.after_hbm.refs_3_, bf16[256,512]{1,0:T(8,128)(2,1)} %query_hbm.1, f32[1,512]{1,0:T(1,128)} %bitcast.1, bf16[512,4096]{1,0:T(8,128)(2,1)} %own_weight.5), custom_call_target="tpu_custom_call" | custom-call | tf_op jit(solution)/shard_map/fetch/pallas_call | solution.py:121
  15.8 0.6 %collective-permute-done.3.refs_0_ = bf16[256,128]{1,0:T(8,128)(2,1)S(1)} collective-permute-done((bf16[256,128]{1,0:T(8,128)(2,1)S(1)}, bf16[256,128]{1,0:T(8,128)(2,1)S(1)}, u32[]{:S(2)}, u32[]{:S(2)}) %collective-permute-start.3) | collective-permute-done | bytes 65568 | tf_op jit(solution)/shard_map/ppermute | solution.py:342
  16.5 0.9 %collective-permute-done.4.refs_1_ = bf16[256,128]{1,0:T(8,128)(2,1)S(1)} collective-permute-done((bf16[256,128]{1,0:T(8,128)(2,1)S(1)}, bf16[256,128]{1,0:T(8,128)(2,1)S(1)}, u32[]{:S(2)}, u32[]{:S(2)}) %collective-permute-start.4) | collective-permute-done | bytes 65568 | tf_op jit(solution)/shard_map/ppermute | solution.py:342
  17.4 0.0 collective-permute-done.5.refs_2_
  17.4 0.1 gate.1.own_ref
  17.6 0.1 collective-permute-start.6
  17.7 0.3 half.1.half_ref
  18.0 1.2 %collective-permute-done.6.other_ref = bf16[256,512]{1,0:T(8,128)(2,1)S(1)} collective-permute-done((bf16[256,512]{1,0:T(8,128)(2,1)S(1)}, bf16[256,512]{1,0:T(8,128)(2,1)S(1)}, u32[]{:S(2)}, u32[]{:S(2)}) %collective-permute-start.6) | collective-permute-done | bytes 262176 | tf_op jit(solution)/shard_map/ppermute | solution.py:351
  19.2 0.0 collective-permute-done.7.other_weight
  19.2 0.3 by_two.1
  19.5 1.8 %collective-permute-start.8 = (bf16[256,512]{1,0:T(8,128)(2,1)S(1)}, bf16[256,512]{1,0:T(8,128)(2,1)S(1)}, u32[]{:S(2)}, u32[]{:S(2)}) collective-permute-start(bf16[256,512]{1,0:T(8,128)(2,1)S(1)} %by_two.1), channel_id=1, source_target_pairs={{0,2},{1,3},{6,4},{7,5},{2,6},{3,7},{4,0},{5,1},{8,10},{9,11},{14,... | collective-permute-start | bytes 786440 | tf_op jit(solution)/shard_map/ppermute | solution.py:346
  21.3 1.5 %by_one.1 = bf16[256,512]{1,0:T(8,128)(2,1)S(1)} custom-call(bf16[256,512]{1,0:T(8,128)(2,1)S(1)} %gate.1.own_ref, bf16[256,512]{1,0:T(8,128)(2,1)S(1)} %collective-permute-done.6.other_ref, bf16[512,4096]{1,0:T(8,128)(2,1)} %own_weight.5, bf16[512,4096]{1,0:T(8,128)(2,1)S(1)} %collective-permute-done.7.other_weight), custom_call_target="tpu_custom_call" | custom-call | tf_op jit(solution)/shard_map/by_one/pallas_call | solution.py:280
  22.8 2.7 %collective-permute-start.9 = (bf16[256,512]{1,0:T(8,128)(2,1)S(1)}, bf16[256,512]{1,0:T(8,128)(2,1)S(1)}, u32[]{:S(2)}, u32[]{:S(2)}) collective-permute-start(bf16[256,512]{1,0:T(8,128)(2,1)S(1)} %by_one.1), channel_id=1, source_target_pairs={{0,2},{1,3},{2,0},{3,1},{4,6},{5,7},{6,4},{7,5},{8,10},{9,11},{10,... | collective-permute-start | bytes 786440 | tf_op jit(solution)/shard_map/ppermute | solution.py:346
  25.5 1.5 %by_three.1.own_ref = bf16[256,512]{1,0:T(8,128)(2,1)S(1)} custom-call(bf16[256,512]{1,0:T(8,128)(2,1)S(1)} %gate.1.own_ref, bf16[256,512]{1,0:T(8,128)(2,1)S(1)} %collective-permute-done.6.other_ref, bf16[512,4096]{1,0:T(8,128)(2,1)} %own_weight.5, bf16[512,4096]{1,0:T(8,128)(2,1)S(1)} %collective-permute-done.7.other_weight), custom_call_target="tpu_custom_call" | custom-call | tf_op jit(solution)/shard_map/by_three/pallas_call | solution.py:280
  27.0 2.0 %collective-permute-done.8.first_ref.arrived_ref = bf16[256,512]{1,0:T(8,128)(2,1)S(1)} collective-permute-done((bf16[256,512]{1,0:T(8,128)(2,1)S(1)}, bf16[256,512]{1,0:T(8,128)(2,1)S(1)}, u32[]{:S(2)}, u32[]{:S(2)}) %collective-permute-start.8) | collective-permute-done | bytes 262176 | tf_op jit(solution)/shard_map/ppermute | solution.py:346
  29.0 3.7 %collective-permute-start.10 = (bf16[256,512]{1,0:T(8,128)(2,1)S(1)}, bf16[256,512]{1,0:T(8,128)(2,1)S(1)}, u32[]{:S(2)}, u32[]{:S(2)}) collective-permute-start(bf16[256,512]{1,0:T(8,128)(2,1)S(1)} %forward.1), channel_id=1, source_target_pairs={{0,6},{1,7},{6,0},{7,1},{2,4},{3,5},{4,2},{5,3},{8,14},{9,15},{14,... | collective-permute-start | bytes 786440 | tf_op jit(solution)/shard_map/ppermute | solution.py:346
  32.8 1.5 %base.1.base_ref = f32[256,512]{1,0:T(8,128)S(1)} custom-call(bf16[256,512]{1,0:T(8,128)(2,1)S(1)} %gate.1.own_ref, bf16[256,512]{1,0:T(8,128)(2,1)S(1)} %collective-permute-done.6.other_ref, bf16[512,4096]{1,0:T(8,128)(2,1)} %own_weight.5, bf16[512,4096]{1,0:T(8,128)(2,1)S(1)} %collective-permute-done.7.other_weight, ...), custom_call_target="tpu_custom_call" | custom-call | tf_op jit(solution)/shard_map/base/pallas_call | solution.py:280
  34.3 0.2 collective-permute-done.9.pair_ref
  34.5 6.9 %collective-permute-done.10.mirror_ref = bf16[256,512]{1,0:T(8,128)(2,1)S(1)} collective-permute-done((bf16[256,512]{1,0:T(8,128)(2,1)S(1)}, bf16[256,512]{1,0:T(8,128)(2,1)S(1)}, u32[]{:S(2)}, u32[]{:S(2)}) %collective-permute-start.10) | collective-permute-done | bytes 262176 | tf_op jit(solution)/shard_map/ppermute | solution.py:346
  41.4 0.8 %final.1 = bf16[256,512]{1,0:T(8,128)(2,1)} custom-call(f32[256,512]{1,0:T(8,128)S(1)} %base.1.base_ref, bf16[256,512]{1,0:T(8,128)(2,1)S(1)} %collective-permute-done.9.pair_ref, bf16[256,512]{1,0:T(8,128)(2,1)S(1)} %collective-permute-done.10.mirror_ref), custom_call_target="tpu_custom_call" | custom-call | tf_op jit(solution)/shard_map/final/pallas_call | solution.py:317
  (1 shorter events, 0.0 us)
Async XLA Ops:
  0.0 19.2 %collective-permute-start.7 = (bf16[512,4096]{1,0:T(8,128)(2,1)}, bf16[512,4096]{1,0:T(8,128)(2,1)S(1)}, u32[]{:S(2)}, u32[]{:S(2)}) collective-permute-start(bf16[512,4096]{1,0:T(8,128)(2,1)} %own_weight.5), channel_id=1, source_target_pairs={{0,1},{1,0},{2,3},{3,2},{4,5},{5,4},{6,7},{7,6},{8,9},{9,8},{10,11... | collective-permute-start | bytes 12582920 | tf_op jit(solution)/shard_map/ppermute | solution.py:351
  1.7 6.1 %collective-permute-start = (bf16[272,128]{1,0:T(8,128)(2,1)S(1)}, bf16[272,128]{1,0:T(8,128)(2,1)S(1)}, u32[]{:S(2)}, u32[]{:S(2)}) collective-permute-start(bf16[272,128]{1,0:T(8,128)(2,1)S(1)} %get-tuple-element.21), channel_id=1, source_target_pairs={{0,24},{1,17},{2,26},{3,19},{4,28},{5,21},{6,30},{7,23},{8,16},{9,... | collective-permute-start | bytes 208904 | tf_op jit(solution)/shard_map/ppermute | solution.py:342
  5.2 4.7 %collective-permute-start.1 = (bf16[272,128]{1,0:T(8,128)(2,1)S(1)}, bf16[272,128]{1,0:T(8,128)(2,1)S(1)}, u32[]{:S(2)}, u32[]{:S(2)}) collective-permute-start(bf16[272,128]{1,0:T(8,128)(2,1)S(1)} %get-tuple-element.22), channel_id=1, source_target_pairs={{0,8},{1,25},{2,10},{3,27},{4,12},{5,29},{6,14},{7,31},{8,0},{9,17... | collective-permute-start | bytes 208904 | tf_op jit(solution)/shard_map/ppermute | solution.py:342
  5.7 4.3 %collective-permute-start.2 = (bf16[272,128]{1,0:T(8,128)(2,1)S(1)}, bf16[272,128]{1,0:T(8,128)(2,1)S(1)}, u32[]{:S(2)}, u32[]{:S(2)}) collective-permute-start(bf16[272,128]{1,0:T(8,128)(2,1)S(1)} %get-tuple-element.23), channel_id=1, source_target_pairs={{0,16},{1,9},{2,18},{3,11},{4,20},{5,13},{6,22},{7,15},{8,24},{9,1... | collective-permute-start | bytes 208904 | tf_op jit(solution)/shard_map/ppermute | solution.py:342
  11.1 5.4 %collective-permute-start.3 = (bf16[256,128]{1,0:T(8,128)(2,1)S(1)}, bf16[256,128]{1,0:T(8,128)(2,1)S(1)}, u32[]{:S(2)}, u32[]{:S(2)}) collective-permute-start(bf16[256,128]{1,0:T(8,128)(2,1)S(1)} %get-tuple-element.24), channel_id=1, source_target_pairs={{0,24},{1,17},{2,26},{3,19},{4,28},{5,21},{6,30},{7,23},{8,16},{9,... | collective-permute-start | bytes 196616 | tf_op jit(solution)/shard_map/ppermute | solution.py:342
  12.8 4.6 %collective-permute-start.4 = (bf16[256,128]{1,0:T(8,128)(2,1)S(1)}, bf16[256,128]{1,0:T(8,128)(2,1)S(1)}, u32[]{:S(2)}, u32[]{:S(2)}) collective-permute-start(bf16[256,128]{1,0:T(8,128)(2,1)S(1)} %get-tuple-element.25), channel_id=1, source_target_pairs={{0,8},{1,25},{2,10},{3,27},{4,12},{5,29},{6,14},{7,31},{8,0},{9,17... | collective-permute-start | bytes 196616 | tf_op jit(solution)/shard_map/ppermute | solution.py:342
  13.2 4.3 %collective-permute-start.5 = (bf16[256,128]{1,0:T(8,128)(2,1)S(1)}, bf16[256,128]{1,0:T(8,128)(2,1)S(1)}, u32[]{:S(2)}, u32[]{:S(2)}) collective-permute-start(bf16[256,128]{1,0:T(8,128)(2,1)S(1)} %get-tuple-element.26), channel_id=1, source_target_pairs={{0,16},{1,9},{2,18},{3,11},{4,20},{5,13},{6,22},{7,15},{8,24},{9,1... | collective-permute-start | bytes 196616 | tf_op jit(solution)/shard_map/ppermute | solution.py:342
  17.6 1.6 %collective-permute-start.6 = (bf16[256,512]{1,0:T(8,128)(2,1)S(1)}, bf16[256,512]{1,0:T(8,128)(2,1)S(1)}, u32[]{:S(2)}, u32[]{:S(2)}) collective-permute-start(bf16[256,512]{1,0:T(8,128)(2,1)S(1)} %gate.1.own_ref), channel_id=1, source_target_pairs={{0,1},{1,0},{2,3},{3,2},{4,5},{5,4},{6,7},{7,6},{8,9},{9,8},{10,11... | collective-permute-start | bytes 786440 | tf_op jit(solution)/shard_map/ppermute | solution.py:351
  19.5 9.5 %collective-permute-start.8 = (bf16[256,512]{1,0:T(8,128)(2,1)S(1)}, bf16[256,512]{1,0:T(8,128)(2,1)S(1)}, u32[]{:S(2)}, u32[]{:S(2)}) collective-permute-start(bf16[256,512]{1,0:T(8,128)(2,1)S(1)} %by_two.1), channel_id=1, source_target_pairs={{0,2},{1,3},{6,4},{7,5},{2,6},{3,7},{4,0},{5,1},{8,10},{9,11},{14,... | collective-permute-start | bytes 786440 | tf_op jit(solution)/shard_map/ppermute | solution.py:346
  22.8 11.7 %collective-permute-start.9 = (bf16[256,512]{1,0:T(8,128)(2,1)S(1)}, bf16[256,512]{1,0:T(8,128)(2,1)S(1)}, u32[]{:S(2)}, u32[]{:S(2)}) collective-permute-start(bf16[256,512]{1,0:T(8,128)(2,1)S(1)} %by_one.1), channel_id=1, source_target_pairs={{0,2},{1,3},{2,0},{3,1},{4,6},{5,7},{6,4},{7,5},{8,10},{9,11},{10,... | collective-permute-start | bytes 786440 | tf_op jit(solution)/shard_map/ppermute | solution.py:346
  29.0 12.4 %collective-permute-start.10 = (bf16[256,512]{1,0:T(8,128)(2,1)S(1)}, bf16[256,512]{1,0:T(8,128)(2,1)S(1)}, u32[]{:S(2)}, u32[]{:S(2)}) collective-permute-start(bf16[256,512]{1,0:T(8,128)(2,1)S(1)} %forward.1), channel_id=1, source_target_pairs={{0,6},{1,7},{6,0},{7,1},{2,4},{3,5},{4,2},{5,3},{8,14},{9,15},{14,... | collective-permute-start | bytes 786440 | tf_op jit(solution)/shard_map/ppermute | solution.py:346

commit v7 on v6

--- a/solution.py
+++ b/solution.py
@@ -9,9 +9,10 @@
 from jax.sharding import PartitionSpec as P
 
 LANES = 128
+DISTANCES = (2, 1, 3, 0)
+EARLY_PARTS = 5
 GOING = ((3, 1, 2, 0), (2, 3, 1, 0))
 RETURNING = GOING
-OUT_PARTS = 2
 BF16 = jnp.bfloat16
 F32 = jnp.float32
 VMEM_LIMIT = 16 * 1024 * 1024
@@ -110,7 +111,8 @@
     ]
     for load in loads:
         load.start()
-    loads.append(load_block(2, weight_hbm, weight_ref, arrived.at[2])[1])
+    for i, distance in enumerate(DISTANCES):
+        loads.append(load_block(distance, weight_hbm, weight_ref.at[i], arrived.at[2 + i])[1])
     for load in loads:
         load.wait()
 
@@ -123,11 +125,11 @@
         out_shape=[
             jax.ShapeDtypeStruct(query_in.shape, BF16),
             jax.ShapeDtypeStruct((1, width), F32),
-            jax.ShapeDtypeStruct((width, columns), BF16),
+            jax.ShapeDtypeStruct((len(DISTANCES), width, columns), BF16),
         ],
         in_specs=[pl.BlockSpec(memory_space=pl.ANY)] * 4,
         out_specs=[vmem] * 3,
-        scratch_shapes=[pltpu.SemaphoreType.DMA((3,))],
+        scratch_shapes=[pltpu.SemaphoreType.DMA((2 + len(DISTANCES),))],
         compiler_params=params(),
         name="fetch",
     )(after, *in_hbm(query_in, skip_gain.reshape(1, -1), out_weight))
@@ -231,7 +233,7 @@
 
 
 def half_kernel(own_ref, weight, out_ref):
-    out_ref[...] = jnp.dot(own_ref[...], weight[...], preferred_element_type=F32)
+    out_ref[...] = jnp.dot(own_ref[...], weight[0], preferred_element_type=F32)
 
 
 def add_half_kernel(half_ref, other_ref, other_weight, out_ref):
@@ -240,26 +242,34 @@
     out_ref[...] = (half_ref[...] + late).astype(BF16)
 
 
-def both_halves(distance, own_ref, other_ref, own_weight, other_weight, weight, arrived):
-    block, load = load_block(distance, own_weight, weight, arrived)
+def both_halves(distance, own_ref, other_ref, own_weight, other_weight):
+    weight = own_weight.at[DISTANCES.index(distance)]
+    block = rows_at(2 * (chip_place() ^ distance) + core_place(), weight.shape[1])
     late = jnp.dot(other_ref[...], other_weight[:, block], preferred_element_type=F32)
-    load.wait()
     return late + jnp.dot(own_ref[...], weight[...], preferred_element_type=F32)
 
 
+def two_piece_kernel(distance, own_ref, other_ref, own_weight, other_weight, first_ref, second_ref):
+    block = both_halves(distance, own_ref, other_ref, own_weight, other_weight)
+    rows = first_ref.shape[0]
+    first_ref[...] = block[0:rows, :].astype(BF16)
+    second_ref[...] = block[rows:, :].astype(BF16)
+
+
+def after_kernel(from_ref, *refs):
+    refs[-1][...] = from_ref[...]
+
+
 def block_kernel(distance, own_ref, other_ref, own_weight, other_weight, *refs):
-    out_ref, weight, arrived = refs[-3:]
-    out_ref[...] = both_halves(
-        distance, own_ref, other_ref, own_weight, other_weight, weight, arrived
-    ).astype(BF16)
+    refs[-1][...] = both_halves(distance, own_ref, other_ref, own_weight, other_weight).astype(BF16)
 
 
 def is_end():
     return (chip_place() == 0) | (chip_place() == 3)
 
 
-def base_kernel(own_ref, other_ref, own_weight, other_weight, first_ref, out_ref, weight, arrived):
-    base = both_halves(0, own_ref, other_ref, own_weight, other_weight, weight, arrived)
+def base_kernel(own_ref, other_ref, own_weight, other_weight, first_ref, out_ref):
+    base = both_halves(0, own_ref, other_ref, own_weight, other_weight)
 
     @pl.when(is_end())
     def _():
@@ -298,31 +308,36 @@
         out_ref[...] = (own_ref[...].astype(F32) + arrived_ref[...].astype(F32)).astype(BF16)
 
 
-def final_kernel(base_ref, pair_ref, mirror_ref, out_hbm, out_ref, arrived):
-    rows = out_ref.shape[0] // OUT_PARTS
-    stores = []
-    for k in range(OUT_PARTS):
-        here = slice(k * rows, (k + 1) * rows)
-        arrivals = pair_ref[here, :].astype(F32) + mirror_ref[here, :].astype(F32)
-        out_ref[here, :] = (base_ref[here, :] + arrivals).astype(BF16)
-        store = pltpu.make_async_copy(out_ref.at[here, :], out_hbm.at[here, :], arrived.at[k])
-        store.start()
-        stores.append(store)
-    for store in stores:
-        store.wait()
-
-
-def finish(base, pair, mirror):
+def nearly_kernel(base_ref, beside_ref, mirror_ref, out_ref):
+    rows = beside_ref.shape[0]
+    sums = base_ref[...] + mirror_ref[...].astype(F32)
+    out_ref[0:rows, :] = sums[0:rows, :] + beside_ref[...].astype(F32)
+    out_ref[rows:, :] = sums[rows:, :]
+
+
+def final_kernel(base_ref, late_ref, out_hbm, out_ref, arrived):
+    rows = base_ref.shape[0] - late_ref.shape[0]
+    out_ref[0:rows, :] = base_ref[0:rows, :].astype(BF16)
+    first = pltpu.make_async_copy(out_ref.at[0:rows, :], out_hbm.at[0:rows, :], arrived.at[0])
+    first.start()
+    out_ref[rows:, :] = (base_ref[rows:, :] + late_ref[...].astype(F32)).astype(BF16)
+    second = pltpu.make_async_copy(out_ref.at[rows:, :], out_hbm.at[rows:, :], arrived.at[1])
+    second.start()
+    first.wait()
+    second.wait()
+
+
+def finish(base, late):
     vmem = pl.BlockSpec(memory_space=pltpu.VMEM)
     return pl.pallas_call(
         final_kernel,
         out_shape=jax.ShapeDtypeStruct(base.shape, BF16),
-        in_specs=[vmem] * 3,
+        in_specs=[vmem] * 2,
         out_specs=pl.BlockSpec(memory_space=pl.ANY),
-        scratch_shapes=[pltpu.VMEM(base.shape, BF16), pltpu.SemaphoreType.DMA((OUT_PARTS,))],
+        scratch_shapes=[pltpu.VMEM(base.shape, BF16), pltpu.SemaphoreType.DMA((2,))],
         compiler_params=params(),
         name="final",
-    )(base, pair, mirror)
+    )(base, late)
 
 
 def fast_body(n_seq, n_chan, query_in, key_in, value_in, filter_taps, skip_gain, out_weight):
@@ -361,23 +376,25 @@
 
     block = jax.ShapeDtypeStruct((rows, columns), BF16)
     block_f32 = jax.ShapeDtypeStruct((rows, columns), F32)
-    one_weight = [pltpu.VMEM((width, columns), BF16), pltpu.SemaphoreType.DMA(())]
-    halves = (gated, gated_other, out_weight, other_weight)
+    halves = (gated, gated_other, weight, other_weight)
 
     half = run_kernel(half_kernel, "half", block_f32, [], gated, weight)
     by_two = run_kernel(add_half_kernel, "by_two", block, [], half, gated_other, other_weight)
     first = over_chips(by_two, [(0, 1), (3, 2), (1, 3), (2, 0)])
-    by_one = run_kernel(
-        functools.partial(block_kernel, 1), "by_one", block, one_weight, *halves, hbm=(2,)
-    )
-    pair = over_chips(by_one, [(0, 1), (1, 0), (2, 3), (3, 2)])
-    by_three = run_kernel(
-        functools.partial(block_kernel, 3), "by_three", block, one_weight, *halves, hbm=(2,)
-    )
+    beside = [(0, 1), (1, 0), (2, 3), (3, 2)]
+    early = rows * EARLY_PARTS // 8 // 16 * 16
+    pieces = [jax.ShapeDtypeStruct((n, columns), BF16) for n in (early, rows - early)]
+    kernel = functools.partial(two_piece_kernel, 1)
+    by_one, by_one_rest = run_kernel(kernel, "by_one", pieces, [], *halves)
+    pair = over_chips(by_one, beside)
+    by_three = run_kernel(functools.partial(block_kernel, 3), "by_three", block, [], *halves)
     summed = run_kernel(forward_kernel, "forward", block, [], by_three, first)
     mirror = over_chips(summed, [(0, 3), (3, 0), (1, 2), (2, 1)])
-    base = run_kernel(base_kernel, "base", block_f32, one_weight, *halves, first, hbm=(2,))
-    return finish(base, pair, mirror)
+    by_one_rest = run_kernel(after_kernel, "after", pieces[1], [], by_one_rest, summed, pair)
+    late = over_chips(by_one_rest, beside)
+    base = run_kernel(base_kernel, "base", block_f32, [], *halves, first)
+    nearly = run_kernel(nearly_kernel, "nearly", block_f32, [], base, pair, mirror)
+    return finish(nearly, late)
 
 
 def window_matrix(window, tile_size):

time: 42.5 us -> 42.4 us (level)
  Pallas kernels: 9.5 us -> 6.84 us
  waiting for transfers between devices: 16.2 us -> 18.3 us
  starting transfers between devices: 16.4 us -> 16.9 us
    pallas_call x6 -> x8, Pallas kernels: 5.16 us -> 2.03 us  [run_kernel(): pl.pallas_call(kernel, out_shape=out_shape, in_specs=specs, out_specs=[vm...]
    ppermute x3 -> x4, waiting for transfers between devices: 9.17 us -> 11.8 us  [over_chips(): lax.ppermute(value, 'chan', [(2 * a + c, 2 * b + c) for a, b in moves for...]
    ppermute x6, waiting for transfers between devices: 5.79 us -> 5.28 us  [over_seq(): moved.append(lax.ppermute(value, ('seq', 'chan'), pairs))]
    pallas_call x1, Pallas kernels: 1.16 us -> 1.68 us  [fetch(): pl.pallas_call(fetch_kernel, out_shape=[jax.ShapeDtypeStruct(query_in.sha...]
    ppermute x3 -> x4, starting transfers between devices: 8.17 us -> 8.63 us  [over_chips(): lax.ppermute(value, 'chan', [(2 * a + c, 2 * b + c) for a, b in moves for...]
  transfers between devices with their start and end apart: 11 -> 12, of which waited for: 9 -> 9; matrix products, arithmetic and copies ran while one was open for 0% -> 0% of each run, Pallas kernels for 20% -> 14%
where the time goes in v7:
time: 42.4 us; the launch traced here: 42.2 us
  waiting for transfers between devices  18.3 us (43%)
  starting transfers between devices  16.9 us (40%)
  Pallas kernels  6.84 us (16%)
    ppermute x4, waiting for transfers between devices, over_chips(): lax.ppermute(value, 'chan', [(2 * a + c, 2 * b + c) for a, b in moves for...  11.8 us
    ppermute x4, starting transfers between devices, over_chips(): lax.ppermute(value, 'chan', [(2 * a + c, 2 * b + c) for a, b in moves for...  8.63 us
    ppermute x6, starting transfers between devices, over_seq(): moved.append(lax.ppermute(value, ('seq', 'chan'), pairs))  7.72 us
    ppermute x6, waiting for transfers between devices, over_seq(): moved.append(lax.ppermute(value, ('seq', 'chan'), pairs))  5.28 us
    pallas_call x8, Pallas kernels, run_kernel(): pl.pallas_call(kernel, out_shape=out_shape, in_specs=specs, out_specs=[vm...  2.03 us
    pallas_call x1, Pallas kernels, fetch(): pl.pallas_call(fetch_kernel, out_shape=[jax.ShapeDtypeStruct(query_in.sha...  1.68 us
    pallas_call x1, Pallas kernels, products(): pl.pallas_call(functools.partial(product_kernel, n_seq), out_shape=[here]...  1.24 us
    ppermute x2, waiting for transfers between devices, other_core(): return lax.ppermute(value, 'chan', [(i, i ^ 1) for i in range(n_chan)])  1.22 us
  transfers between devices with their start and end apart: 12, of which 9 were waited for; matrix products, arithmetic and copies ran while one was open for 0% of the time, Pallas kernels for 14%

profile of v7, /device:TPU:0, one launch (start us, length us, event | category | flops | bytes accessed | tf_op | source)
XLA Modules:
  0.0 42.2 jit_solution(7042082589984593907)
XLA Ops:
  0.0 0.5 %collective-permute-start.7 = (bf16[512,4096]{1,0:T(8,128)(2,1)}, bf16[512,4096]{1,0:T(8,128)(2,1)S(1)}, u32[]{:S(2)}, u32[]{:S(2)}) collective-permute-start(bf16[512,4096]{1,0:T(8,128)(2,1)} %weight_hbm.1), channel_id=1, source_target_pairs={{0,1},{1,0},{2,3},{3,2},{4,5},{5,4},{6,7},{7,6},{8,9},{9,8},{10,11... | collective-permute-start | bytes 12582920 | tf_op jit(solution)/shard_map/ppermute | solution.py:366
  0.5 1.2 %products.1 = (bf16[256,512]{1,0:T(8,128)(2,1)S(1)}, bf16[272,128]{1,0:T(8,128)(2,1)S(1)}, bf16[272,128]{1,0:T(8,128)(2,1)S(1)}, bf16[272,128]{1,0:T(8,128)(2,1)S(1)}, bf16[272,128]{1,0:T(8,128)(2,1)S(1)}) custom-call(bf16[256,512]{1,0:T(8,128)(2,1)} %key_hbm.1, bf16[256,512]{1,0:T(8,128)(2,1)} %value_hbm.1, bf16[32,256]{1,0:T(8,128)(2,1)} %taps_hbm.1), custom_call_target="tpu_custom_call" | custom-call | tf_op jit(solution)/shard_map/products/pallas_call | solution.py:90
  1.7 3.5 %collective-permute-start = (bf16[272,128]{1,0:T(8,128)(2,1)S(1)}, bf16[272,128]{1,0:T(8,128)(2,1)S(1)}, u32[]{:S(2)}, u32[]{:S(2)}) collective-permute-start(bf16[272,128]{1,0:T(8,128)(2,1)S(1)} %get-tuple-element.23), channel_id=1, source_target_pairs={{0,24},{1,17},{2,26},{3,19},{4,28},{5,21},{6,30},{7,23},{8,16},{9,... | collective-permute-start | bytes 208904 | tf_op jit(solution)/shard_map/ppermute | solution.py:357
  5.2 0.5 %collective-permute-start.1 = (bf16[272,128]{1,0:T(8,128)(2,1)S(1)}, bf16[272,128]{1,0:T(8,128)(2,1)S(1)}, u32[]{:S(2)}, u32[]{:S(2)}) collective-permute-start(bf16[272,128]{1,0:T(8,128)(2,1)S(1)} %get-tuple-element.24), channel_id=1, source_target_pairs={{0,8},{1,25},{2,10},{3,27},{4,12},{5,29},{6,14},{7,31},{8,0},{9,17... | collective-permute-start | bytes 208904 | tf_op jit(solution)/shard_map/ppermute | solution.py:357
  5.7 0.1 collective-permute-start.2
  5.8 1.9 %collective-permute-done.refs_0_ = bf16[272,128]{1,0:T(8,128)(2,1)S(1)} collective-permute-done((bf16[272,128]{1,0:T(8,128)(2,1)S(1)}, bf16[272,128]{1,0:T(8,128)(2,1)S(1)}, u32[]{:S(2)}, u32[]{:S(2)}) %collective-permute-start) | collective-permute-done | bytes 69664 | tf_op jit(solution)/shard_map/ppermute | solution.py:357
  7.8 2.1 %collective-permute-done.1.refs_1_ = bf16[272,128]{1,0:T(8,128)(2,1)S(1)} collective-permute-done((bf16[272,128]{1,0:T(8,128)(2,1)S(1)}, bf16[272,128]{1,0:T(8,128)(2,1)S(1)}, u32[]{:S(2)}, u32[]{:S(2)}) %collective-permute-start.1) | collective-permute-done | bytes 69664 | tf_op jit(solution)/shard_map/ppermute | solution.py:357
  9.9 0.2 collective-permute-done.2.refs_2_
  10.1 1.0 %convolve.1 = (bf16[256,128]{1,0:T(8,128)(2,1)S(1)}, bf16[256,128]{1,0:T(8,128)(2,1)S(1)}, bf16[256,128]{1,0:T(8,128)(2,1)S(1)}, bf16[256,128]{1,0:T(8,128)(2,1)S(1)}) custom-call(bf16[272,128]{1,0:T(8,128)(2,1)S(1)} %collective-permute-done.refs_0_, bf16[272,128]{1,0:T(8,128)(2,1)S(1)} %collective-permute-done.1.refs_1_, ...), custom_call_target="tpu_custom_call" | custom-call | tf_op jit(solution)/shard_map/convolve/pallas_call | solution.py:191
  11.1 1.7 %collective-permute-start.3 = (bf16[256,128]{1,0:T(8,128)(2,1)S(1)}, bf16[256,128]{1,0:T(8,128)(2,1)S(1)}, u32[]{:S(2)}, u32[]{:S(2)}) collective-permute-start(bf16[256,128]{1,0:T(8,128)(2,1)S(1)} %get-tuple-element.26), channel_id=1, source_target_pairs={{0,24},{1,17},{2,26},{3,19},{4,28},{5,21},{6,30},{7,23},{8,16},{9,... | collective-permute-start | bytes 196616 | tf_op jit(solution)/shard_map/ppermute | solution.py:357
  12.8 0.4 collective-permute-start.4
  13.2 1.5 %collective-permute-start.5 = (bf16[256,128]{1,0:T(8,128)(2,1)S(1)}, bf16[256,128]{1,0:T(8,128)(2,1)S(1)}, u32[]{:S(2)}, u32[]{:S(2)}) collective-permute-start(bf16[256,128]{1,0:T(8,128)(2,1)S(1)} %get-tuple-element.28), channel_id=1, source_target_pairs={{0,16},{1,9},{2,18},{3,11},{4,20},{5,13},{6,22},{7,15},{8,24},{9,1... | collective-permute-start | bytes 196616 | tf_op jit(solution)/shard_map/ppermute | solution.py:357
  14.7 1.7 %fetch.1 = (bf16[256,512]{1,0:T(8,128)(2,1)S(1)}, f32[1,512]{1,0:T(1,128)S(1)}, bf16[4,512,512]{2,1,0:T(8,128)(2,1)S(1)}) custom-call(bf16[272,128]{1,0:T(8,128)(2,1)S(1)} %get-tuple-element.19.after_hbm.refs_3_, bf16[256,512]{1,0:T(8,128)(2,1)} %query_hbm.1, f32[1,512]{1,0:T(1,128)} %bitcast.1, bf16[512,4096]{1,0:T(8,128)(2,1)} %weight_hbm.1), custom_call_target="tpu_custom_call" | custom-call | tf_op jit(solution)/shard_map/fetch/pallas_call | solution.py:123
  16.4 0.1 collective-permute-done.3.refs_0_
  16.5 0.9 %collective-permute-done.4.refs_1_ = bf16[256,128]{1,0:T(8,128)(2,1)S(1)} collective-permute-done((bf16[256,128]{1,0:T(8,128)(2,1)S(1)}, bf16[256,128]{1,0:T(8,128)(2,1)S(1)}, u32[]{:S(2)}, u32[]{:S(2)}) %collective-permute-start.4) | collective-permute-done | bytes 65568 | tf_op jit(solution)/shard_map/ppermute | solution.py:357
  17.4 0.1 gate.1.own_ref
  17.6 0.1 collective-permute-start.6
  17.7 0.3 half.1.half_ref
  18.0 1.2 %collective-permute-done.6.other_ref = bf16[256,512]{1,0:T(8,128)(2,1)S(1)} collective-permute-done((bf16[256,512]{1,0:T(8,128)(2,1)S(1)}, bf16[256,512]{1,0:T(8,128)(2,1)S(1)}, u32[]{:S(2)}, u32[]{:S(2)}) %collective-permute-start.6) | collective-permute-done | bytes 262176 | tf_op jit(solution)/shard_map/ppermute | solution.py:366
  19.2 0.3 by_two.1
  19.5 1.8 %collective-permute-start.8 = (bf16[256,512]{1,0:T(8,128)(2,1)S(1)}, bf16[256,512]{1,0:T(8,128)(2,1)S(1)}, u32[]{:S(2)}, u32[]{:S(2)}) collective-permute-start(bf16[256,512]{1,0:T(8,128)(2,1)S(1)} %by_two.1), channel_id=1, source_target_pairs={{0,2},{1,3},{6,4},{7,5},{2,6},{3,7},{4,0},{5,1},{8,10},{9,11},{14,... | collective-permute-start | bytes 786440 | tf_op jit(solution)/shard_map/ppermute | solution.py:361
  21.3 0.4 %by_one.1 = (bf16[160,512]{1,0:T(8,128)(2,1)S(1)}, bf16[96,512]{1,0:T(8,128)(2,1)S(1)}) custom-call(bf16[256,512]{1,0:T(8,128)(2,1)S(1)} %gate.1.own_ref, bf16[256,512]{1,0:T(8,128)(2,1)S(1)} %collective-permute-done.6.other_ref, bf16[4,512,512]{2,1,0:T(8,128)(2,1)S(1)} %get-tuple-element.30.weight.own_weight, ...), custom_call_target="tpu_custom_call" | custom-call | tf_op jit(solution)/shard_map/by_one/pallas_call | solution.py:290
  21.7 2.7 %collective-permute-start.9 = (bf16[160,512]{1,0:T(8,128)(2,1)S(1)}, bf16[160,512]{1,0:T(8,128)(2,1)S(1)}, u32[]{:S(2)}, u32[]{:S(2)}) collective-permute-start(bf16[160,512]{1,0:T(8,128)(2,1)S(1)} %get-tuple-element.31), channel_id=1, source_target_pairs={{0,2},{1,3},{2,0},{3,1},{4,6},{5,7},{6,4},{7,5},{8,10},{9,11},{10,... | collective-permute-start | bytes 491528 | tf_op jit(solution)/shard_map/ppermute | solution.py:361
  24.4 0.4 %by_three.1.own_ref = bf16[256,512]{1,0:T(8,128)(2,1)S(1)} custom-call(bf16[256,512]{1,0:T(8,128)(2,1)S(1)} %gate.1.own_ref, bf16[256,512]{1,0:T(8,128)(2,1)S(1)} %collective-permute-done.6.other_ref, bf16[4,512,512]{2,1,0:T(8,128)(2,1)S(1)} %get-tuple-element.30.weight.own_weight, bf16[512,4096]{1,0:T(8,128)(2,1)S(1)} %collective-permute-done.7.other_weight), custom_call_target="tpu_custom_call" | custom-call | tf_op jit(solution)/shard_map/by_three/pallas_call | solution.py:290
  24.8 4.2 %collective-permute-done.8.first_ref.arrived_ref = bf16[256,512]{1,0:T(8,128)(2,1)S(1)} collective-permute-done((bf16[256,512]{1,0:T(8,128)(2,1)S(1)}, bf16[256,512]{1,0:T(8,128)(2,1)S(1)}, u32[]{:S(2)}, u32[]{:S(2)}) %collective-permute-start.8) | collective-permute-done | bytes 262176 | tf_op jit(solution)/shard_map/ppermute | solution.py:361
  29.0 3.7 %collective-permute-start.10 = (bf16[256,512]{1,0:T(8,128)(2,1)S(1)}, bf16[256,512]{1,0:T(8,128)(2,1)S(1)}, u32[]{:S(2)}, u32[]{:S(2)}) collective-permute-start(bf16[256,512]{1,0:T(8,128)(2,1)S(1)} %forward.1.refs_0_), channel_id=1, source_target_pairs={{0,6},{1,7},{6,0},{7,1},{2,4},{3,5},{4,2},{5,3},{8,14},{9,15},{14,... | collective-permute-start | bytes 786440 | tf_op jit(solution)/shard_map/ppermute | solution.py:361
  32.8 0.5 %collective-permute-start.11 = (bf16[96,512]{1,0:T(8,128)(2,1)S(1)}, bf16[96,512]{1,0:T(8,128)(2,1)S(1)}, u32[]{:S(2)}, u32[]{:S(2)}) collective-permute-start(bf16[96,512]{1,0:T(8,128)(2,1)S(1)} %after.1), channel_id=1, source_target_pairs={{0,2},{1,3},{2,0},{3,1},{4,6},{5,7},{6,4},{7,5},{8,10},{9,11},{10,... | collective-permute-start | bytes 294920 | tf_op jit(solution)/shard_map/ppermute | solution.py:361
  33.2 0.5 %base.1.base_ref = f32[256,512]{1,0:T(8,128)S(1)} custom-call(bf16[256,512]{1,0:T(8,128)(2,1)S(1)} %gate.1.own_ref, bf16[256,512]{1,0:T(8,128)(2,1)S(1)} %collective-permute-done.6.other_ref, bf16[4,512,512]{2,1,0:T(8,128)(2,1)S(1)} %get-tuple-element.30.weight.own_weight, bf16[512,4096]{1,0:T(8,128)(2,1)S(1)} %collective-permute-done.7.other_weight, ...), custom_call_target="tpu_custom_call" | custom-call | tf_op jit(solution)/shard_map/base/pallas_call | solution.py:290
  33.7 6.5 %collective-permute-done.10.mirror_ref = bf16[256,512]{1,0:T(8,128)(2,1)S(1)} collective-permute-done((bf16[256,512]{1,0:T(8,128)(2,1)S(1)}, bf16[256,512]{1,0:T(8,128)(2,1)S(1)}, u32[]{:S(2)}, u32[]{:S(2)}) %collective-permute-start.10) | collective-permute-done | bytes 262176 | tf_op jit(solution)/shard_map/ppermute | solution.py:361
  40.2 0.1 nearly.1.base_ref
  40.3 1.1 %collective-permute-done.11.late_ref = bf16[96,512]{1,0:T(8,128)(2,1)S(1)} collective-permute-done((bf16[96,512]{1,0:T(8,128)(2,1)S(1)}, bf16[96,512]{1,0:T(8,128)(2,1)S(1)}, u32[]{:S(2)}, u32[]{:S(2)}) %collective-permute-start.11) | collective-permute-done | bytes 98336 | tf_op jit(solution)/shard_map/ppermute | solution.py:361
  41.4 0.7 %final.1 = bf16[256,512]{1,0:T(8,128)(2,1)} custom-call(f32[256,512]{1,0:T(8,128)S(1)} %nearly.1.base_ref, bf16[96,512]{1,0:T(8,128)(2,1)S(1)} %collective-permute-done.11.late_ref), custom_call_target="tpu_custom_call" | custom-call | tf_op jit(solution)/shard_map/final/pallas_call | solution.py:332
  (5 shorter events, 0.1 us)
Async XLA Ops:
  0.0 19.2 %collective-permute-start.7 = (bf16[512,4096]{1,0:T(8,128)(2,1)}, bf16[512,4096]{1,0:T(8,128)(2,1)S(1)}, u32[]{:S(2)}, u32[]{:S(2)}) collective-permute-start(bf16[512,4096]{1,0:T(8,128)(2,1)} %weight_hbm.1), channel_id=1, source_target_pairs={{0,1},{1,0},{2,3},{3,2},{4,5},{5,4},{6,7},{7,6},{8,9},{9,8},{10,11... | collective-permute-start | bytes 12582920 | tf_op jit(solution)/shard_map/ppermute | solution.py:366
  1.7 6.1 %collective-permute-start = (bf16[272,128]{1,0:T(8,128)(2,1)S(1)}, bf16[272,128]{1,0:T(8,128)(2,1)S(1)}, u32[]{:S(2)}, u32[]{:S(2)}) collective-permute-start(bf16[272,128]{1,0:T(8,128)(2,1)S(1)} %get-tuple-element.23), channel_id=1, source_target_pairs={{0,24},{1,17},{2,26},{3,19},{4,28},{5,21},{6,30},{7,23},{8,16},{9,... | collective-permute-start | bytes 208904 | tf_op jit(solution)/shard_map/ppermute | solution.py:357
  5.2 4.7 %collective-permute-start.1 = (bf16[272,128]{1,0:T(8,128)(2,1)S(1)}, bf16[272,128]{1,0:T(8,128)(2,1)S(1)}, u32[]{:S(2)}, u32[]{:S(2)}) collective-permute-start(bf16[272,128]{1,0:T(8,128)(2,1)S(1)} %get-tuple-element.24), channel_id=1, source_target_pairs={{0,8},{1,25},{2,10},{3,27},{4,12},{5,29},{6,14},{7,31},{8,0},{9,17... | collective-permute-start | bytes 208904 | tf_op jit(solution)/shard_map/ppermute | solution.py:357
  5.7 4.3 %collective-permute-start.2 = (bf16[272,128]{1,0:T(8,128)(2,1)S(1)}, bf16[272,128]{1,0:T(8,128)(2,1)S(1)}, u32[]{:S(2)}, u32[]{:S(2)}) collective-permute-start(bf16[272,128]{1,0:T(8,128)(2,1)S(1)} %get-tuple-element.25), channel_id=1, source_target_pairs={{0,16},{1,9},{2,18},{3,11},{4,20},{5,13},{6,22},{7,15},{8,24},{9,1... | collective-permute-start | bytes 208904 | tf_op jit(solution)/shard_map/ppermute | solution.py:357
  11.1 5.4 %collective-permute-start.3 = (bf16[256,128]{1,0:T(8,128)(2,1)S(1)}, bf16[256,128]{1,0:T(8,128)(2,1)S(1)}, u32[]{:S(2)}, u32[]{:S(2)}) collective-permute-start(bf16[256,128]{1,0:T(8,128)(2,1)S(1)} %get-tuple-element.26), channel_id=1, source_target_pairs={{0,24},{1,17},{2,26},{3,19},{4,28},{5,21},{6,30},{7,23},{8,16},{9,... | collective-permute-start | bytes 196616 | tf_op jit(solution)/shard_map/ppermute | solution.py:357
  12.8 4.6 %collective-permute-start.4 = (bf16[256,128]{1,0:T(8,128)(2,1)S(1)}, bf16[256,128]{1,0:T(8,128)(2,1)S(1)}, u32[]{:S(2)}, u32[]{:S(2)}) collective-permute-start(bf16[256,128]{1,0:T(8,128)(2,1)S(1)} %get-tuple-element.27), channel_id=1, source_target_pairs={{0,8},{1,25},{2,10},{3,27},{4,12},{5,29},{6,14},{7,31},{8,0},{9,17... | collective-permute-start | bytes 196616 | tf_op jit(solution)/shard_map/ppermute | solution.py:357
  13.2 4.3 %collective-permute-start.5 = (bf16[256,128]{1,0:T(8,128)(2,1)S(1)}, bf16[256,128]{1,0:T(8,128)(2,1)S(1)}, u32[]{:S(2)}, u32[]{:S(2)}) collective-permute-start(bf16[256,128]{1,0:T(8,128)(2,1)S(1)} %get-tuple-element.28), channel_id=1, source_target_pairs={{0,16},{1,9},{2,18},{3,11},{4,20},{5,13},{6,22},{7,15},{8,24},{9,1... | collective-permute-start | bytes 196616 | tf_op jit(solution)/shard_map/ppermute | solution.py:357
  17.6 1.6 %collective-permute-start.6 = (bf16[256,512]{1,0:T(8,128)(2,1)S(1)}, bf16[256,512]{1,0:T(8,128)(2,1)S(1)}, u32[]{:S(2)}, u32[]{:S(2)}) collective-permute-start(bf16[256,512]{1,0:T(8,128)(2,1)S(1)} %gate.1.own_ref), channel_id=1, source_target_pairs={{0,1},{1,0},{2,3},{3,2},{4,5},{5,4},{6,7},{7,6},{8,9},{9,8},{10,11... | collective-permute-start | bytes 786440 | tf_op jit(solution)/shard_map/ppermute | solution.py:366
  19.5 9.5 %collective-permute-start.8 = (bf16[256,512]{1,0:T(8,128)(2,1)S(1)}, bf16[256,512]{1,0:T(8,128)(2,1)S(1)}, u32[]{:S(2)}, u32[]{:S(2)}) collective-permute-start(bf16[256,512]{1,0:T(8,128)(2,1)S(1)} %by_two.1), channel_id=1, source_target_pairs={{0,2},{1,3},{6,4},{7,5},{2,6},{3,7},{4,0},{5,1},{8,10},{9,11},{14,... | collective-permute-start | bytes 786440 | tf_op jit(solution)/shard_map/ppermute | solution.py:361
  21.7 11.0 %collective-permute-start.9 = (bf16[160,512]{1,0:T(8,128)(2,1)S(1)}, bf16[160,512]{1,0:T(8,128)(2,1)S(1)}, u32[]{:S(2)}, u32[]{:S(2)}) collective-permute-start(bf16[160,512]{1,0:T(8,128)(2,1)S(1)} %get-tuple-element.31), channel_id=1, source_target_pairs={{0,2},{1,3},{2,0},{3,1},{4,6},{5,7},{6,4},{7,5},{8,10},{9,11},{10,... | collective-permute-start | bytes 491528 | tf_op jit(solution)/shard_map/ppermute | solution.py:361
  29.0 11.2 %collective-permute-start.10 = (bf16[256,512]{1,0:T(8,128)(2,1)S(1)}, bf16[256,512]{1,0:T(8,128)(2,1)S(1)}, u32[]{:S(2)}, u32[]{:S(2)}) collective-permute-start(bf16[256,512]{1,0:T(8,128)(2,1)S(1)} %forward.1.refs_0_), channel_id=1, source_target_pairs={{0,6},{1,7},{6,0},{7,1},{2,4},{3,5},{4,2},{5,3},{8,14},{9,15},{14,... | collective-permute-start | bytes 786440 | tf_op jit(solution)/shard_map/ppermute | solution.py:361
  32.8 8.6 %collective-permute-start.11 = (bf16[96,512]{1,0:T(8,128)(2,1)S(1)}, bf16[96,512]{1,0:T(8,128)(2,1)S(1)}, u32[]{:S(2)}, u32[]{:S(2)}) collective-permute-start(bf16[96,512]{1,0:T(8,128)(2,1)S(1)} %after.1), channel_id=1, source_target_pairs={{0,2},{1,3},{2,0},{3,1},{4,6},{5,7},{6,4},{7,5},{8,10},{9,11},{10,... | collective-permute-start | bytes 294920 | tf_op jit(solution)/shard_map/ppermute | solution.py:361

commit v8 on v7

--- a/solution.py
+++ b/solution.py
@@ -10,7 +10,8 @@
 
 LANES = 128
 DISTANCES = (2, 1, 3, 0)
-EARLY_PARTS = 5
+EARLY_PARTS = 4
+LEAD_PARTS = 4
 GOING = ((3, 1, 2, 0), (2, 3, 1, 0))
 RETURNING = GOING
 BF16 = jnp.bfloat16
@@ -236,10 +237,14 @@
     out_ref[...] = jnp.dot(own_ref[...], weight[0], preferred_element_type=F32)
 
 
-def add_half_kernel(half_ref, other_ref, other_weight, out_ref):
-    block = rows_at(2 * (chip_place() ^ 2) + core_place(), out_ref.shape[1])
+def add_half_kernel(half_ref, other_ref, other_weight, *out_refs):
+    block = rows_at(2 * (chip_place() ^ 2) + core_place(), half_ref.shape[1])
     late = jnp.dot(other_ref[...], other_weight[:, block], preferred_element_type=F32)
-    out_ref[...] = (half_ref[...] + late).astype(BF16)
+    sums = (half_ref[...] + late).astype(BF16)
+    start = 0
+    for out_ref in out_refs:
+        out_ref[...] = sums[start : start + out_ref.shape[0], :]
+        start += out_ref.shape[0]
 
 
 def both_halves(distance, own_ref, other_ref, own_weight, other_weight):
@@ -268,12 +273,14 @@
     return (chip_place() == 0) | (chip_place() == 3)
 
 
-def base_kernel(own_ref, other_ref, own_weight, other_weight, first_ref, out_ref):
+def base_kernel(own_ref, other_ref, own_weight, other_weight, *refs):
+    first_refs, out_ref = refs[:-1], refs[-1]
     base = both_halves(0, own_ref, other_ref, own_weight, other_weight)
 
     @pl.when(is_end())
     def _():
-        out_ref[...] = base + first_ref[...].astype(F32)
+        first = jnp.concatenate([first_ref[...].astype(F32) for first_ref in first_refs], axis=0)
+        out_ref[...] = base + first
 
     @pl.when(jnp.logical_not(is_end()))
     def _():
@@ -298,21 +305,26 @@
     )(*given)
 
 
-def forward_kernel(own_ref, arrived_ref, out_ref):
+def forward_kernel(start, own_ref, arrived_ref, out_ref):
+    own = own_ref[start : start + out_ref.shape[0], :]
+
     @pl.when(is_end())
     def _():
-        out_ref[...] = own_ref[...]
+        out_ref[...] = own
 
     @pl.when(jnp.logical_not(is_end()))
     def _():
-        out_ref[...] = (own_ref[...].astype(F32) + arrived_ref[...].astype(F32)).astype(BF16)
-
-
-def nearly_kernel(base_ref, beside_ref, mirror_ref, out_ref):
-    rows = beside_ref.shape[0]
-    sums = base_ref[...] + mirror_ref[...].astype(F32)
-    out_ref[0:rows, :] = sums[0:rows, :] + beside_ref[...].astype(F32)
-    out_ref[rows:, :] = sums[rows:, :]
+        out_ref[...] = (own.astype(F32) + arrived_ref[...].astype(F32)).astype(BF16)
+
+
+def nearly_kernel(base_ref, beside_ref, *refs):
+    mirror_refs, out_ref = refs[:-1], refs[-1]
+    start = 0
+    for mirror_ref in mirror_refs:
+        here = slice(start, start + mirror_ref.shape[0])
+        out_ref[here, :] = base_ref[here, :] + mirror_ref[...].astype(F32)
+        start += mirror_ref.shape[0]
+    out_ref[0 : beside_ref.shape[0], :] += beside_ref[...].astype(F32)
 
 
 def final_kernel(base_ref, late_ref, out_hbm, out_ref, arrived):
@@ -379,8 +391,10 @@
     halves = (gated, gated_other, weight, other_weight)
 
     half = run_kernel(half_kernel, "half", block_f32, [], gated, weight)
-    by_two = run_kernel(add_half_kernel, "by_two", block, [], half, gated_other, other_weight)
-    first = over_chips(by_two, [(0, 1), (3, 2), (1, 3), (2, 0)])
+    lead = rows * LEAD_PARTS // 8 // 16 * 16
+    parts = [jax.ShapeDtypeStruct((n, columns), BF16) for n in (lead, rows - lead)]
+    by_two = run_kernel(add_half_kernel, "by_two", parts, [], half, gated_other, other_weight)
+    first = [over_chips(part, [(0, 1), (3, 2), (1, 3), (2, 0)]) for part in by_two]
     beside = [(0, 1), (1, 0), (2, 3), (3, 2)]
     early = rows * EARLY_PARTS // 8 // 16 * 16
     pieces = [jax.ShapeDtypeStruct((n, columns), BF16) for n in (early, rows - early)]
@@ -388,12 +402,15 @@
     by_one, by_one_rest = run_kernel(kernel, "by_one", pieces, [], *halves)
     pair = over_chips(by_one, beside)
     by_three = run_kernel(functools.partial(block_kernel, 3), "by_three", block, [], *halves)
-    summed = run_kernel(forward_kernel, "forward", block, [], by_three, first)
-    mirror = over_chips(summed, [(0, 3), (3, 0), (1, 2), (2, 1)])
+    mirror = []
+    for part, start, arrived in zip(parts, (0, lead), first):
+        kernel = functools.partial(forward_kernel, start)
+        summed = run_kernel(kernel, "forward", part, [], by_three, arrived)
+        mirror.append(over_chips(summed, [(0, 3), (3, 0), (1, 2), (2, 1)]))
     by_one_rest = run_kernel(after_kernel, "after", pieces[1], [], by_one_rest, summed, pair)
     late = over_chips(by_one_rest, beside)
-    base = run_kernel(base_kernel, "base", block_f32, [], *halves, first)
-    nearly = run_kernel(nearly_kernel, "nearly", block_f32, [], base, pair, mirror)
+    base = run_kernel(base_kernel, "base", block_f32, [], *halves, *first)
+    nearly = run_kernel(nearly_kernel, "nearly", block_f32, [], base, pair, *mirror)
     return finish(nearly, late)
 
 

time: 42.4 us -> 42.4 us (level)
  starting transfers between devices: 16.9 us -> 19.9 us
  waiting for transfers between devices: 18.3 us -> 15.3 us
    ppermute x4 -> x6, waiting for transfers between devices: 11.8 us -> 8.77 us  [over_chips(): lax.ppermute(value, 'chan', [(2 * a + c, 2 * b + c) for a, b in moves for...]
    ppermute x4 -> x6, starting transfers between devices: 8.63 us -> 11.6 us  [over_chips(): lax.ppermute(value, 'chan', [(2 * a + c, 2 * b + c) for a, b in moves for...]
    pallas_call x8 -> x9, Pallas kernels: 2.03 us -> 2.06 us  [run_kernel(): pl.pallas_call(kernel, out_shape=out_shape, in_specs=specs, out_specs=[vm...]
  transfers between devices with their start and end apart: 12 -> 14, of which waited for: 9 -> 10; matrix products, arithmetic and copies ran while one was open for 0% -> 0% of each run, Pallas kernels for 14% -> 14%
where the time goes in v8:
time: 42.4 us; the launch traced here: 42.2 us
  starting transfers between devices  19.9 us (47%)
  waiting for transfers between devices  15.3 us (36%)
  Pallas kernels  6.87 us (16%)
    ppermute x6, starting transfers between devices, over_chips(): lax.ppermute(value, 'chan', [(2 * a + c, 2 * b + c) for a, b in moves for...  11.6 us
    ppermute x6, waiting for transfers between devices, over_chips(): lax.ppermute(value, 'chan', [(2 * a + c, 2 * b + c) for a, b in moves for...  8.77 us
    ppermute x6, starting transfers between devices, over_seq(): moved.append(lax.ppermute(value, ('seq', 'chan'), pairs))  7.72 us
    ppermute x6, waiting for transfers between devices, over_seq(): moved.append(lax.ppermute(value, ('seq', 'chan'), pairs))  5.28 us
    pallas_call x9, Pallas kernels, run_kernel(): pl.pallas_call(kernel, out_shape=out_shape, in_specs=specs, out_specs=[vm...  2.06 us
    pallas_call x1, Pallas kernels, fetch(): pl.pallas_call(fetch_kernel, out_shape=[jax.ShapeDtypeStruct(query_in.sha...  1.68 us
    pallas_call x1, Pallas kernels, products(): pl.pallas_call(functools.partial(product_kernel, n_seq), out_shape=[here]...  1.24 us
    ppermute x2, waiting for transfers between devices, other_core(): return lax.ppermute(value, 'chan', [(i, i ^ 1) for i in range(n_chan)])  1.22 us
  transfers between devices with their start and end apart: 14, of which 10 were waited for; matrix products, arithmetic and copies ran while one was open for 0% of the time, Pallas kernels for 14%

profile of v8, /device:TPU:0, one launch (start us, length us, event | category | flops | bytes accessed | tf_op | source)
XLA Modules:
  0.0 42.2 jit_solution(7145365888634151327)
XLA Ops:
  0.0 0.5 %collective-permute-start.7 = (bf16[512,4096]{1,0:T(8,128)(2,1)}, bf16[512,4096]{1,0:T(8,128)(2,1)S(1)}, u32[]{:S(2)}, u32[]{:S(2)}) collective-permute-start(bf16[512,4096]{1,0:T(8,128)(2,1)} %weight_hbm.1), channel_id=1, source_target_pairs={{0,1},{1,0},{2,3},{3,2},{4,5},{5,4},{6,7},{7,6},{8,9},{9,8},{10,11... | collective-permute-start | bytes 12582920 | tf_op jit(solution)/shard_map/ppermute | solution.py:378
  0.5 1.2 %products.1 = (bf16[256,512]{1,0:T(8,128)(2,1)S(1)}, bf16[272,128]{1,0:T(8,128)(2,1)S(1)}, bf16[272,128]{1,0:T(8,128)(2,1)S(1)}, bf16[272,128]{1,0:T(8,128)(2,1)S(1)}, bf16[272,128]{1,0:T(8,128)(2,1)S(1)}) custom-call(bf16[256,512]{1,0:T(8,128)(2,1)} %key_hbm.1, bf16[256,512]{1,0:T(8,128)(2,1)} %value_hbm.1, bf16[32,256]{1,0:T(8,128)(2,1)} %taps_hbm.1), custom_call_target="tpu_custom_call" | custom-call | tf_op jit(solution)/shard_map/products/pallas_call | solution.py:91
  1.7 3.5 %collective-permute-start = (bf16[272,128]{1,0:T(8,128)(2,1)S(1)}, bf16[272,128]{1,0:T(8,128)(2,1)S(1)}, u32[]{:S(2)}, u32[]{:S(2)}) collective-permute-start(bf16[272,128]{1,0:T(8,128)(2,1)S(1)} %get-tuple-element.25), channel_id=1, source_target_pairs={{0,24},{1,17},{2,26},{3,19},{4,28},{5,21},{6,30},{7,23},{8,16},{9,... | collective-permute-start | bytes 208904 | tf_op jit(solution)/shard_map/ppermute | solution.py:369
  5.2 0.5 %collective-permute-start.1 = (bf16[272,128]{1,0:T(8,128)(2,1)S(1)}, bf16[272,128]{1,0:T(8,128)(2,1)S(1)}, u32[]{:S(2)}, u32[]{:S(2)}) collective-permute-start(bf16[272,128]{1,0:T(8,128)(2,1)S(1)} %get-tuple-element.26), channel_id=1, source_target_pairs={{0,8},{1,25},{2,10},{3,27},{4,12},{5,29},{6,14},{7,31},{8,0},{9,17... | collective-permute-start | bytes 208904 | tf_op jit(solution)/shard_map/ppermute | solution.py:369
  5.7 0.1 collective-permute-start.2
  5.8 1.9 %collective-permute-done.refs_0_ = bf16[272,128]{1,0:T(8,128)(2,1)S(1)} collective-permute-done((bf16[272,128]{1,0:T(8,128)(2,1)S(1)}, bf16[272,128]{1,0:T(8,128)(2,1)S(1)}, u32[]{:S(2)}, u32[]{:S(2)}) %collective-permute-start) | collective-permute-done | bytes 69664 | tf_op jit(solution)/shard_map/ppermute | solution.py:369
  7.8 2.1 %collective-permute-done.1.refs_1_ = bf16[272,128]{1,0:T(8,128)(2,1)S(1)} collective-permute-done((bf16[272,128]{1,0:T(8,128)(2,1)S(1)}, bf16[272,128]{1,0:T(8,128)(2,1)S(1)}, u32[]{:S(2)}, u32[]{:S(2)}) %collective-permute-start.1) | collective-permute-done | bytes 69664 | tf_op jit(solution)/shard_map/ppermute | solution.py:369
  9.9 0.2 collective-permute-done.2.refs_2_
  10.1 1.0 %convolve.1 = (bf16[256,128]{1,0:T(8,128)(2,1)S(1)}, bf16[256,128]{1,0:T(8,128)(2,1)S(1)}, bf16[256,128]{1,0:T(8,128)(2,1)S(1)}, bf16[256,128]{1,0:T(8,128)(2,1)S(1)}) custom-call(bf16[272,128]{1,0:T(8,128)(2,1)S(1)} %collective-permute-done.refs_0_, bf16[272,128]{1,0:T(8,128)(2,1)S(1)} %collective-permute-done.1.refs_1_, ...), custom_call_target="tpu_custom_call" | custom-call | tf_op jit(solution)/shard_map/convolve/pallas_call | solution.py:192
  11.1 1.7 %collective-permute-start.3 = (bf16[256,128]{1,0:T(8,128)(2,1)S(1)}, bf16[256,128]{1,0:T(8,128)(2,1)S(1)}, u32[]{:S(2)}, u32[]{:S(2)}) collective-permute-start(bf16[256,128]{1,0:T(8,128)(2,1)S(1)} %get-tuple-element.28), channel_id=1, source_target_pairs={{0,24},{1,17},{2,26},{3,19},{4,28},{5,21},{6,30},{7,23},{8,16},{9,... | collective-permute-start | bytes 196616 | tf_op jit(solution)/shard_map/ppermute | solution.py:369
  12.8 0.4 collective-permute-start.4
  13.2 1.5 %collective-permute-start.5 = (bf16[256,128]{1,0:T(8,128)(2,1)S(1)}, bf16[256,128]{1,0:T(8,128)(2,1)S(1)}, u32[]{:S(2)}, u32[]{:S(2)}) collective-permute-start(bf16[256,128]{1,0:T(8,128)(2,1)S(1)} %get-tuple-element.30), channel_id=1, source_target_pairs={{0,16},{1,9},{2,18},{3,11},{4,20},{5,13},{6,22},{7,15},{8,24},{9,1... | collective-permute-start | bytes 196616 | tf_op jit(solution)/shard_map/ppermute | solution.py:369
  14.7 1.7 %fetch.1 = (bf16[256,512]{1,0:T(8,128)(2,1)S(1)}, f32[1,512]{1,0:T(1,128)S(1)}, bf16[4,512,512]{2,1,0:T(8,128)(2,1)S(1)}) custom-call(bf16[272,128]{1,0:T(8,128)(2,1)S(1)} %get-tuple-element.21.after_hbm.refs_3_, bf16[256,512]{1,0:T(8,128)(2,1)} %query_hbm.1, f32[1,512]{1,0:T(1,128)} %bitcast.1, bf16[512,4096]{1,0:T(8,128)(2,1)} %weight_hbm.1), custom_call_target="tpu_custom_call" | custom-call | tf_op jit(solution)/shard_map/fetch/pallas_call | solution.py:124
  16.4 0.1 collective-permute-done.3.refs_0_
  16.5 0.9 %collective-permute-done.4.refs_1_ = bf16[256,128]{1,0:T(8,128)(2,1)S(1)} collective-permute-done((bf16[256,128]{1,0:T(8,128)(2,1)S(1)}, bf16[256,128]{1,0:T(8,128)(2,1)S(1)}, u32[]{:S(2)}, u32[]{:S(2)}) %collective-permute-start.4) | collective-permute-done | bytes 65568 | tf_op jit(solution)/shard_map/ppermute | solution.py:369
  17.4 0.1 gate.1.own_ref
  17.7 0.3 half.1.half_ref
  18.0 1.2 %collective-permute-done.6.other_ref = bf16[256,512]{1,0:T(8,128)(2,1)S(1)} collective-permute-done((bf16[256,512]{1,0:T(8,128)(2,1)S(1)}, bf16[256,512]{1,0:T(8,128)(2,1)S(1)}, u32[]{:S(2)}, u32[]{:S(2)}) %collective-permute-start.6) | collective-permute-done | bytes 262176 | tf_op jit(solution)/shard_map/ppermute | solution.py:378
  19.2 0.3 by_two.1
  19.5 1.8 %collective-permute-start.8 = (bf16[128,512]{1,0:T(8,128)(2,1)S(1)}, bf16[128,512]{1,0:T(8,128)(2,1)S(1)}, u32[]{:S(2)}, u32[]{:S(2)}) collective-permute-start(bf16[128,512]{1,0:T(8,128)(2,1)S(1)} %get-tuple-element.33), channel_id=1, source_target_pairs={{0,2},{1,3},{6,4},{7,5},{2,6},{3,7},{4,0},{5,1},{8,10},{9,11},{14,... | collective-permute-start | bytes 393224 | tf_op jit(solution)/shard_map/ppermute | solution.py:373
  21.3 2.6 %collective-permute-start.9 = (bf16[128,512]{1,0:T(8,128)(2,1)S(1)}, bf16[128,512]{1,0:T(8,128)(2,1)S(1)}, u32[]{:S(2)}, u32[]{:S(2)}) collective-permute-start(bf16[128,512]{1,0:T(8,128)(2,1)S(1)} %get-tuple-element.34), channel_id=1, source_target_pairs={{0,2},{1,3},{6,4},{7,5},{2,6},{3,7},{4,0},{5,1},{8,10},{9,11},{14,... | collective-permute-start | bytes 393224 | tf_op jit(solution)/shard_map/ppermute | solution.py:373
  23.9 0.4 %by_one.1 = (bf16[128,512]{1,0:T(8,128)(2,1)S(1)}, bf16[128,512]{1,0:T(8,128)(2,1)S(1)}) custom-call(bf16[256,512]{1,0:T(8,128)(2,1)S(1)} %gate.1.own_ref, bf16[256,512]{1,0:T(8,128)(2,1)S(1)} %collective-permute-done.6.other_ref, bf16[4,512,512]{2,1,0:T(8,128)(2,1)S(1)} %get-tuple-element.32.weight.own_weight, ...), custom_call_target="tpu_custom_call" | custom-call | tf_op jit(solution)/shard_map/by_one/pallas_call | solution.py:297
  24.3 0.5 %collective-permute-start.10 = (bf16[128,512]{1,0:T(8,128)(2,1)S(1)}, bf16[128,512]{1,0:T(8,128)(2,1)S(1)}, u32[]{:S(2)}, u32[]{:S(2)}) collective-permute-start(bf16[128,512]{1,0:T(8,128)(2,1)S(1)} %get-tuple-element.35), channel_id=1, source_target_pairs={{0,2},{1,3},{2,0},{3,1},{4,6},{5,7},{6,4},{7,5},{8,10},{9,11},{10,... | collective-permute-start | bytes 393224 | tf_op jit(solution)/shard_map/ppermute | solution.py:373
  24.8 0.4 %by_three.1.own_ref = bf16[256,512]{1,0:T(8,128)(2,1)S(1)} custom-call(bf16[256,512]{1,0:T(8,128)(2,1)S(1)} %gate.1.own_ref, bf16[256,512]{1,0:T(8,128)(2,1)S(1)} %collective-permute-done.6.other_ref, bf16[4,512,512]{2,1,0:T(8,128)(2,1)S(1)} %get-tuple-element.32.weight.own_weight, bf16[512,4096]{1,0:T(8,128)(2,1)S(1)} %collective-permute-done.7.other_weight), custom_call_target="tpu_custom_call" | custom-call | tf_op jit(solution)/shard_map/by_three/pallas_call | solution.py:297
  25.3 1.5 %collective-permute-done.8.refs_0_.arrived_ref = bf16[128,512]{1,0:T(8,128)(2,1)S(1)} collective-permute-done((bf16[128,512]{1,0:T(8,128)(2,1)S(1)}, bf16[128,512]{1,0:T(8,128)(2,1)S(1)}, u32[]{:S(2)}, u32[]{:S(2)}) %collective-permute-start.8) | collective-permute-done | bytes 131104 | tf_op jit(solution)/shard_map/ppermute | solution.py:373
  26.8 3.9 %collective-permute-start.11 = (bf16[128,512]{1,0:T(8,128)(2,1)S(1)}, bf16[128,512]{1,0:T(8,128)(2,1)S(1)}, u32[]{:S(2)}, u32[]{:S(2)}) collective-permute-start(bf16[128,512]{1,0:T(8,128)(2,1)S(1)} %forward.2), channel_id=1, source_target_pairs={{0,6},{1,7},{6,0},{7,1},{2,4},{3,5},{4,2},{5,3},{8,14},{9,15},{14,... | collective-permute-start | bytes 393224 | tf_op jit(solution)/shard_map/ppermute | solution.py:373
  30.8 2.7 %collective-permute-start.12 = (bf16[128,512]{1,0:T(8,128)(2,1)S(1)}, bf16[128,512]{1,0:T(8,128)(2,1)S(1)}, u32[]{:S(2)}, u32[]{:S(2)}) collective-permute-start(bf16[128,512]{1,0:T(8,128)(2,1)S(1)} %forward.3.refs_0_), channel_id=1, source_target_pairs={{0,6},{1,7},{6,0},{7,1},{2,4},{3,5},{4,2},{5,3},{8,14},{9,15},{14,... | collective-permute-start | bytes 393224 | tf_op jit(solution)/shard_map/ppermute | solution.py:373
  33.6 0.5 %base.1.base_ref = f32[256,512]{1,0:T(8,128)S(1)} custom-call(bf16[256,512]{1,0:T(8,128)(2,1)S(1)} %gate.1.own_ref, bf16[256,512]{1,0:T(8,128)(2,1)S(1)} %collective-permute-done.6.other_ref, bf16[4,512,512]{2,1,0:T(8,128)(2,1)S(1)} %get-tuple-element.32.weight.own_weight, bf16[512,4096]{1,0:T(8,128)(2,1)S(1)} %collective-permute-done.7.other_weight, ...), custom_call_target="tpu_custom_call" | custom-call | tf_op jit(solution)/shard_map/base/pallas_call | solution.py:297
  34.1 2.6 %collective-permute-done.11.refs_0_ = bf16[128,512]{1,0:T(8,128)(2,1)S(1)} collective-permute-done((bf16[128,512]{1,0:T(8,128)(2,1)S(1)}, bf16[128,512]{1,0:T(8,128)(2,1)S(1)}, u32[]{:S(2)}, u32[]{:S(2)}) %collective-permute-start.11) | collective-permute-done | bytes 131104 | tf_op jit(solution)/shard_map/ppermute | solution.py:373
  36.7 2.0 %collective-permute-done.12.refs_1_ = bf16[128,512]{1,0:T(8,128)(2,1)S(1)} collective-permute-done((bf16[128,512]{1,0:T(8,128)(2,1)S(1)}, bf16[128,512]{1,0:T(8,128)(2,1)S(1)}, u32[]{:S(2)}, u32[]{:S(2)}) %collective-permute-start.12) | collective-permute-done | bytes 131104 | tf_op jit(solution)/shard_map/ppermute | solution.py:373
  38.8 2.6 %collective-permute-done.13.late_ref = bf16[128,512]{1,0:T(8,128)(2,1)S(1)} collective-permute-done((bf16[128,512]{1,0:T(8,128)(2,1)S(1)}, bf16[128,512]{1,0:T(8,128)(2,1)S(1)}, u32[]{:S(2)}, u32[]{:S(2)}) %collective-permute-start.13) | collective-permute-done | bytes 131104 | tf_op jit(solution)/shard_map/ppermute | solution.py:373
  41.4 0.7 %final.1 = bf16[256,512]{1,0:T(8,128)(2,1)} custom-call(f32[256,512]{1,0:T(8,128)S(1)} %nearly.1.base_ref, bf16[128,512]{1,0:T(8,128)(2,1)S(1)} %collective-permute-done.13.late_ref), custom_call_target="tpu_custom_call" | custom-call | tf_op jit(solution)/shard_map/final/pallas_call | solution.py:344
  (10 shorter events, 0.3 us)
Async XLA Ops:
  0.0 19.2 %collective-permute-start.7 = (bf16[512,4096]{1,0:T(8,128)(2,1)}, bf16[512,4096]{1,0:T(8,128)(2,1)S(1)}, u32[]{:S(2)}, u32[]{:S(2)}) collective-permute-start(bf16[512,4096]{1,0:T(8,128)(2,1)} %weight_hbm.1), channel_id=1, source_target_pairs={{0,1},{1,0},{2,3},{3,2},{4,5},{5,4},{6,7},{7,6},{8,9},{9,8},{10,11... | collective-permute-start | bytes 12582920 | tf_op jit(solution)/shard_map/ppermute | solution.py:378
  1.7 6.1 %collective-permute-start = (bf16[272,128]{1,0:T(8,128)(2,1)S(1)}, bf16[272,128]{1,0:T(8,128)(2,1)S(1)}, u32[]{:S(2)}, u32[]{:S(2)}) collective-permute-start(bf16[272,128]{1,0:T(8,128)(2,1)S(1)} %get-tuple-element.25), channel_id=1, source_target_pairs={{0,24},{1,17},{2,26},{3,19},{4,28},{5,21},{6,30},{7,23},{8,16},{9,... | collective-permute-start | bytes 208904 | tf_op jit(solution)/shard_map/ppermute | solution.py:369
  5.2 4.7 %collective-permute-start.1 = (bf16[272,128]{1,0:T(8,128)(2,1)S(1)}, bf16[272,128]{1,0:T(8,128)(2,1)S(1)}, u32[]{:S(2)}, u32[]{:S(2)}) collective-permute-start(bf16[272,128]{1,0:T(8,128)(2,1)S(1)} %get-tuple-element.26), channel_id=1, source_target_pairs={{0,8},{1,25},{2,10},{3,27},{4,12},{5,29},{6,14},{7,31},{8,0},{9,17... | collective-permute-start | bytes 208904 | tf_op jit(solution)/shard_map/ppermute | solution.py:369
  5.7 4.3 %collective-permute-start.2 = (bf16[272,128]{1,0:T(8,128)(2,1)S(1)}, bf16[272,128]{1,0:T(8,128)(2,1)S(1)}, u32[]{:S(2)}, u32[]{:S(2)}) collective-permute-start(bf16[272,128]{1,0:T(8,128)(2,1)S(1)} %get-tuple-element.27), channel_id=1, source_target_pairs={{0,16},{1,9},{2,18},{3,11},{4,20},{5,13},{6,22},{7,15},{8,24},{9,1... | collective-permute-start | bytes 208904 | tf_op jit(solution)/shard_map/ppermute | solution.py:369
  11.1 5.4 %collective-permute-start.3 = (bf16[256,128]{1,0:T(8,128)(2,1)S(1)}, bf16[256,128]{1,0:T(8,128)(2,1)S(1)}, u32[]{:S(2)}, u32[]{:S(2)}) collective-permute-start(bf16[256,128]{1,0:T(8,128)(2,1)S(1)} %get-tuple-element.28), channel_id=1, source_target_pairs={{0,24},{1,17},{2,26},{3,19},{4,28},{5,21},{6,30},{7,23},{8,16},{9,... | collective-permute-start | bytes 196616 | tf_op jit(solution)/shard_map/ppermute | solution.py:369
  12.8 4.6 %collective-permute-start.4 = (bf16[256,128]{1,0:T(8,128)(2,1)S(1)}, bf16[256,128]{1,0:T(8,128)(2,1)S(1)}, u32[]{:S(2)}, u32[]{:S(2)}) collective-permute-start(bf16[256,128]{1,0:T(8,128)(2,1)S(1)} %get-tuple-element.29), channel_id=1, source_target_pairs={{0,8},{1,25},{2,10},{3,27},{4,12},{5,29},{6,14},{7,31},{8,0},{9,17... | collective-permute-start | bytes 196616 | tf_op jit(solution)/shard_map/ppermute | solution.py:369
  13.2 4.3 %collective-permute-start.5 = (bf16[256,128]{1,0:T(8,128)(2,1)S(1)}, bf16[256,128]{1,0:T(8,128)(2,1)S(1)}, u32[]{:S(2)}, u32[]{:S(2)}) collective-permute-start(bf16[256,128]{1,0:T(8,128)(2,1)S(1)} %get-tuple-element.30), channel_id=1, source_target_pairs={{0,16},{1,9},{2,18},{3,11},{4,20},{5,13},{6,22},{7,15},{8,24},{9,1... | collective-permute-start | bytes 196616 | tf_op jit(solution)/shard_map/ppermute | solution.py:369
  17.6 1.6 %collective-permute-start.6 = (bf16[256,512]{1,0:T(8,128)(2,1)S(1)}, bf16[256,512]{1,0:T(8,128)(2,1)S(1)}, u32[]{:S(2)}, u32[]{:S(2)}) collective-permute-start(bf16[256,512]{1,0:T(8,128)(2,1)S(1)} %gate.1.own_ref), channel_id=1, source_target_pairs={{0,1},{1,0},{2,3},{3,2},{4,5},{5,4},{6,7},{7,6},{8,9},{9,8},{10,11... | collective-permute-start | bytes 786440 | tf_op jit(solution)/shard_map/ppermute | solution.py:378
  19.5 7.3 %collective-permute-start.8 = (bf16[128,512]{1,0:T(8,128)(2,1)S(1)}, bf16[128,512]{1,0:T(8,128)(2,1)S(1)}, u32[]{:S(2)}, u32[]{:S(2)}) collective-permute-start(bf16[128,512]{1,0:T(8,128)(2,1)S(1)} %get-tuple-element.33), channel_id=1, source_target_pairs={{0,2},{1,3},{6,4},{7,5},{2,6},{3,7},{4,0},{5,1},{8,10},{9,11},{14,... | collective-permute-start | bytes 393224 | tf_op jit(solution)/shard_map/ppermute | solution.py:373
  21.3 9.5 %collective-permute-start.9 = (bf16[128,512]{1,0:T(8,128)(2,1)S(1)}, bf16[128,512]{1,0:T(8,128)(2,1)S(1)}, u32[]{:S(2)}, u32[]{:S(2)}) collective-permute-start(bf16[128,512]{1,0:T(8,128)(2,1)S(1)} %get-tuple-element.34), channel_id=1, source_target_pairs={{0,2},{1,3},{6,4},{7,5},{2,6},{3,7},{4,0},{5,1},{8,10},{9,11},{14,... | collective-permute-start | bytes 393224 | tf_op jit(solution)/shard_map/ppermute | solution.py:373
  24.3 9.2 %collective-permute-start.10 = (bf16[128,512]{1,0:T(8,128)(2,1)S(1)}, bf16[128,512]{1,0:T(8,128)(2,1)S(1)}, u32[]{:S(2)}, u32[]{:S(2)}) collective-permute-start(bf16[128,512]{1,0:T(8,128)(2,1)S(1)} %get-tuple-element.35), channel_id=1, source_target_pairs={{0,2},{1,3},{2,0},{3,1},{4,6},{5,7},{6,4},{7,5},{8,10},{9,11},{10,... | collective-permute-start | bytes 393224 | tf_op jit(solution)/shard_map/ppermute | solution.py:373
  26.8 9.9 %collective-permute-start.11 = (bf16[128,512]{1,0:T(8,128)(2,1)S(1)}, bf16[128,512]{1,0:T(8,128)(2,1)S(1)}, u32[]{:S(2)}, u32[]{:S(2)}) collective-permute-start(bf16[128,512]{1,0:T(8,128)(2,1)S(1)} %forward.2), channel_id=1, source_target_pairs={{0,6},{1,7},{6,0},{7,1},{2,4},{3,5},{4,2},{5,3},{8,14},{9,15},{14,... | collective-permute-start | bytes 393224 | tf_op jit(solution)/shard_map/ppermute | solution.py:373
  30.8 7.9 %collective-permute-start.12 = (bf16[128,512]{1,0:T(8,128)(2,1)S(1)}, bf16[128,512]{1,0:T(8,128)(2,1)S(1)}, u32[]{:S(2)}, u32[]{:S(2)}) collective-permute-start(bf16[128,512]{1,0:T(8,128)(2,1)S(1)} %forward.3.refs_0_), channel_id=1, source_target_pairs={{0,6},{1,7},{6,0},{7,1},{2,4},{3,5},{4,2},{5,3},{8,14},{9,15},{14,... | collective-permute-start | bytes 393224 | tf_op jit(solution)/shard_map/ppermute | solution.py:373
  33.5 7.9 %collective-permute-start.13 = (bf16[128,512]{1,0:T(8,128)(2,1)S(1)}, bf16[128,512]{1,0:T(8,128)(2,1)S(1)}, u32[]{:S(2)}, u32[]{:S(2)}) collective-permute-start(bf16[128,512]{1,0:T(8,128)(2,1)S(1)} %after.1), channel_id=1, source_target_pairs={{0,2},{1,3},{2,0},{3,1},{4,6},{5,7},{6,4},{7,5},{8,10},{9,11},{10,... | collective-permute-start | bytes 393224 | tf_op jit(solution)/shard_map/ppermute | solution.py:373

commit v9 on v7

--- a/solution.py
+++ b/solution.py
@@ -10,7 +10,7 @@
 
 LANES = 128
 DISTANCES = (2, 1, 3, 0)
-EARLY_PARTS = 5
+EARLY_PARTS = 6
 GOING = ((3, 1, 2, 0), (2, 3, 1, 0))
 RETURNING = GOING
 BF16 = jnp.bfloat16
@@ -249,7 +249,7 @@
     return late + jnp.dot(own_ref[...], weight[...], preferred_element_type=F32)
 
 
-def two_piece_kernel(distance, own_ref, other_ref, own_weight, other_weight, first_ref, second_ref):
+def two_piece_kernel(distance, own_ref, other_ref, own_weight, other_weight, _, first_ref, second_ref):
     block = both_halves(distance, own_ref, other_ref, own_weight, other_weight)
     rows = first_ref.shape[0]
     first_ref[...] = block[0:rows, :].astype(BF16)
@@ -384,10 +384,10 @@
     beside = [(0, 1), (1, 0), (2, 3), (3, 2)]
     early = rows * EARLY_PARTS // 8 // 16 * 16
     pieces = [jax.ShapeDtypeStruct((n, columns), BF16) for n in (early, rows - early)]
+    by_three = run_kernel(functools.partial(block_kernel, 3), "by_three", block, [], *halves)
     kernel = functools.partial(two_piece_kernel, 1)
-    by_one, by_one_rest = run_kernel(kernel, "by_one", pieces, [], *halves)
+    by_one, by_one_rest = run_kernel(kernel, "by_one", pieces, [], *halves, by_three)
     pair = over_chips(by_one, beside)
-    by_three = run_kernel(functools.partial(block_kernel, 3), "by_three", block, [], *halves)
     summed = run_kernel(forward_kernel, "forward", block, [], by_three, first)
     mirror = over_chips(summed, [(0, 3), (3, 0), (1, 2), (2, 1)])
     by_one_rest = run_kernel(after_kernel, "after", pieces[1], [], by_one_rest, summed, pair)

time: 42.4 us -> 42.4 us (level)
  transfers between devices with their start and end apart: 12 -> 12, of which waited for: 9 -> 10; matrix products, arithmetic and copies ran while one was open for 0% -> 0% of each run, Pallas kernels for 14% -> 14%
where the time goes in v9:
time: 42.4 us; the launch traced here: 42.2 us
  waiting for transfers between devices  18.1 us (43%)
  starting transfers between devices  17.1 us (40%)
  Pallas kernels  6.86 us (16%)
    ppermute x4, waiting for transfers between devices, over_chips(): lax.ppermute(value, 'chan', [(2 * a + c, 2 * b + c) for a, b in moves for...  11.5 us
    ppermute x4, starting transfers between devices, over_chips(): lax.ppermute(value, 'chan', [(2 * a + c, 2 * b + c) for a, b in moves for...  8.9 us
    ppermute x6, starting transfers between devices, over_seq(): moved.append(lax.ppermute(value, ('seq', 'chan'), pairs))  7.72 us
    ppermute x6, waiting for transfers between devices, over_seq(): moved.append(lax.ppermute(value, ('seq', 'chan'), pairs))  5.28 us
    pallas_call x8, Pallas kernels, run_kernel(): pl.pallas_call(kernel, out_shape=out_shape, in_specs=specs, out_specs=[vm...  2.05 us
    pallas_call x1, Pallas kernels, fetch(): pl.pallas_call(fetch_kernel, out_shape=[jax.ShapeDtypeStruct(query_in.sha...  1.68 us
    pallas_call x1, Pallas kernels, products(): pl.pallas_call(functools.partial(product_kernel, n_seq), out_shape=[here]...  1.24 us
    ppermute x2, waiting for transfers between devices, other_core(): return lax.ppermute(value, 'chan', [(i, i ^ 1) for i in range(n_chan)])  1.22 us
  transfers between devices with their start and end apart: 12, of which 10 were waited for; matrix products, arithmetic and copies ran while one was open for 0% of the time, Pallas kernels for 14%

profile of v9, /device:TPU:0, one launch (start us, length us, event | category | flops | bytes accessed | tf_op | source)
XLA Modules:
  0.0 42.2 jit_solution(2065400192360999031)
XLA Ops:
  0.0 0.5 %collective-permute-start.7 = (bf16[512,4096]{1,0:T(8,128)(2,1)}, bf16[512,4096]{1,0:T(8,128)(2,1)S(1)}, u32[]{:S(2)}, u32[]{:S(2)}) collective-permute-start(bf16[512,4096]{1,0:T(8,128)(2,1)} %weight_hbm.1), channel_id=1, source_target_pairs={{0,1},{1,0},{2,3},{3,2},{4,5},{5,4},{6,7},{7,6},{8,9},{9,8},{10,11... | collective-permute-start | bytes 12582920 | tf_op jit(solution)/shard_map/ppermute | solution.py:366
  0.5 1.2 %products.1 = (bf16[256,512]{1,0:T(8,128)(2,1)S(1)}, bf16[272,128]{1,0:T(8,128)(2,1)S(1)}, bf16[272,128]{1,0:T(8,128)(2,1)S(1)}, bf16[272,128]{1,0:T(8,128)(2,1)S(1)}, bf16[272,128]{1,0:T(8,128)(2,1)S(1)}) custom-call(bf16[256,512]{1,0:T(8,128)(2,1)} %key_hbm.1, bf16[256,512]{1,0:T(8,128)(2,1)} %value_hbm.1, bf16[32,256]{1,0:T(8,128)(2,1)} %taps_hbm.1), custom_call_target="tpu_custom_call" | custom-call | tf_op jit(solution)/shard_map/products/pallas_call | solution.py:90
  1.7 3.5 %collective-permute-start = (bf16[272,128]{1,0:T(8,128)(2,1)S(1)}, bf16[272,128]{1,0:T(8,128)(2,1)S(1)}, u32[]{:S(2)}, u32[]{:S(2)}) collective-permute-start(bf16[272,128]{1,0:T(8,128)(2,1)S(1)} %get-tuple-element.23), channel_id=1, source_target_pairs={{0,24},{1,17},{2,26},{3,19},{4,28},{5,21},{6,30},{7,23},{8,16},{9,... | collective-permute-start | bytes 208904 | tf_op jit(solution)/shard_map/ppermute | solution.py:357
  5.2 0.5 %collective-permute-start.1 = (bf16[272,128]{1,0:T(8,128)(2,1)S(1)}, bf16[272,128]{1,0:T(8,128)(2,1)S(1)}, u32[]{:S(2)}, u32[]{:S(2)}) collective-permute-start(bf16[272,128]{1,0:T(8,128)(2,1)S(1)} %get-tuple-element.24), channel_id=1, source_target_pairs={{0,8},{1,25},{2,10},{3,27},{4,12},{5,29},{6,14},{7,31},{8,0},{9,17... | collective-permute-start | bytes 208904 | tf_op jit(solution)/shard_map/ppermute | solution.py:357
  5.7 0.1 collective-permute-start.2
  5.8 1.9 %collective-permute-done.refs_0_ = bf16[272,128]{1,0:T(8,128)(2,1)S(1)} collective-permute-done((bf16[272,128]{1,0:T(8,128)(2,1)S(1)}, bf16[272,128]{1,0:T(8,128)(2,1)S(1)}, u32[]{:S(2)}, u32[]{:S(2)}) %collective-permute-start) | collective-permute-done | bytes 69664 | tf_op jit(solution)/shard_map/ppermute | solution.py:357
  7.8 2.1 %collective-permute-done.1.refs_1_ = bf16[272,128]{1,0:T(8,128)(2,1)S(1)} collective-permute-done((bf16[272,128]{1,0:T(8,128)(2,1)S(1)}, bf16[272,128]{1,0:T(8,128)(2,1)S(1)}, u32[]{:S(2)}, u32[]{:S(2)}) %collective-permute-start.1) | collective-permute-done | bytes 69664 | tf_op jit(solution)/shard_map/ppermute | solution.py:357
  9.9 0.2 collective-permute-done.2.refs_2_
  10.1 1.0 %convolve.1 = (bf16[256,128]{1,0:T(8,128)(2,1)S(1)}, bf16[256,128]{1,0:T(8,128)(2,1)S(1)}, bf16[256,128]{1,0:T(8,128)(2,1)S(1)}, bf16[256,128]{1,0:T(8,128)(2,1)S(1)}) custom-call(bf16[272,128]{1,0:T(8,128)(2,1)S(1)} %collective-permute-done.refs_0_, bf16[272,128]{1,0:T(8,128)(2,1)S(1)} %collective-permute-done.1.refs_1_, ...), custom_call_target="tpu_custom_call" | custom-call | tf_op jit(solution)/shard_map/convolve/pallas_call | solution.py:191
  11.1 1.7 %collective-permute-start.3 = (bf16[256,128]{1,0:T(8,128)(2,1)S(1)}, bf16[256,128]{1,0:T(8,128)(2,1)S(1)}, u32[]{:S(2)}, u32[]{:S(2)}) collective-permute-start(bf16[256,128]{1,0:T(8,128)(2,1)S(1)} %get-tuple-element.26), channel_id=1, source_target_pairs={{0,24},{1,17},{2,26},{3,19},{4,28},{5,21},{6,30},{7,23},{8,16},{9,... | collective-permute-start | bytes 196616 | tf_op jit(solution)/shard_map/ppermute | solution.py:357
  12.8 0.4 collective-permute-start.4
  13.2 1.5 %collective-permute-start.5 = (bf16[256,128]{1,0:T(8,128)(2,1)S(1)}, bf16[256,128]{1,0:T(8,128)(2,1)S(1)}, u32[]{:S(2)}, u32[]{:S(2)}) collective-permute-start(bf16[256,128]{1,0:T(8,128)(2,1)S(1)} %get-tuple-element.28), channel_id=1, source_target_pairs={{0,16},{1,9},{2,18},{3,11},{4,20},{5,13},{6,22},{7,15},{8,24},{9,1... | collective-permute-start | bytes 196616 | tf_op jit(solution)/shard_map/ppermute | solution.py:357
  14.7 1.7 %fetch.1 = (bf16[256,512]{1,0:T(8,128)(2,1)S(1)}, f32[1,512]{1,0:T(1,128)S(1)}, bf16[4,512,512]{2,1,0:T(8,128)(2,1)S(1)}) custom-call(bf16[272,128]{1,0:T(8,128)(2,1)S(1)} %get-tuple-element.19.after_hbm.refs_3_, bf16[256,512]{1,0:T(8,128)(2,1)} %query_hbm.1, f32[1,512]{1,0:T(1,128)} %bitcast.1, bf16[512,4096]{1,0:T(8,128)(2,1)} %weight_hbm.1), custom_call_target="tpu_custom_call" | custom-call | tf_op jit(solution)/shard_map/fetch/pallas_call | solution.py:123
  16.4 0.1 collective-permute-done.3.refs_0_
  16.5 0.9 %collective-permute-done.4.refs_1_ = bf16[256,128]{1,0:T(8,128)(2,1)S(1)} collective-permute-done((bf16[256,128]{1,0:T(8,128)(2,1)S(1)}, bf16[256,128]{1,0:T(8,128)(2,1)S(1)}, u32[]{:S(2)}, u32[]{:S(2)}) %collective-permute-start.4) | collective-permute-done | bytes 65568 | tf_op jit(solution)/shard_map/ppermute | solution.py:357
  17.4 0.1 gate.1.own_ref
  17.6 0.1 collective-permute-start.6
  17.7 0.3 half.1.half_ref
  18.0 1.2 %collective-permute-done.6.other_ref = bf16[256,512]{1,0:T(8,128)(2,1)S(1)} collective-permute-done((bf16[256,512]{1,0:T(8,128)(2,1)S(1)}, bf16[256,512]{1,0:T(8,128)(2,1)S(1)}, u32[]{:S(2)}, u32[]{:S(2)}) %collective-permute-start.6) | collective-permute-done | bytes 262176 | tf_op jit(solution)/shard_map/ppermute | solution.py:366
  19.2 0.3 by_two.1
  19.5 1.8 %collective-permute-start.8 = (bf16[256,512]{1,0:T(8,128)(2,1)S(1)}, bf16[256,512]{1,0:T(8,128)(2,1)S(1)}, u32[]{:S(2)}, u32[]{:S(2)}) collective-permute-start(bf16[256,512]{1,0:T(8,128)(2,1)S(1)} %by_two.1), channel_id=1, source_target_pairs={{0,2},{1,3},{6,4},{7,5},{2,6},{3,7},{4,0},{5,1},{8,10},{9,11},{14,... | collective-permute-start | bytes 786440 | tf_op jit(solution)/shard_map/ppermute | solution.py:361
  21.3 0.4 %by_three.1._.own_ref = bf16[256,512]{1,0:T(8,128)(2,1)S(1)} custom-call(bf16[256,512]{1,0:T(8,128)(2,1)S(1)} %gate.1.own_ref, bf16[256,512]{1,0:T(8,128)(2,1)S(1)} %collective-permute-done.6.other_ref, bf16[4,512,512]{2,1,0:T(8,128)(2,1)S(1)} %get-tuple-element.30.weight.own_weight, bf16[512,4096]{1,0:T(8,128)(2,1)S(1)} %collective-permute-done.7.other_weight), custom_call_target="tpu_custom_call" | custom-call | tf_op jit(solution)/shard_map/by_three/pallas_call | solution.py:290
  21.7 0.4 %by_one.1 = (bf16[192,512]{1,0:T(8,128)(2,1)S(1)}, bf16[64,512]{1,0:T(8,128)(2,1)S(1)}) custom-call(bf16[256,512]{1,0:T(8,128)(2,1)S(1)} %gate.1.own_ref, bf16[256,512]{1,0:T(8,128)(2,1)S(1)} %collective-permute-done.6.other_ref, bf16[4,512,512]{2,1,0:T(8,128)(2,1)S(1)} %get-tuple-element.30.weight.own_weight, ...), custom_call_target="tpu_custom_call" | custom-call | tf_op jit(solution)/shard_map/by_one/pallas_call | solution.py:290
  22.2 2.7 %collective-permute-start.9 = (bf16[192,512]{1,0:T(8,128)(2,1)S(1)}, bf16[192,512]{1,0:T(8,128)(2,1)S(1)}, u32[]{:S(2)}, u32[]{:S(2)}) collective-permute-start(bf16[192,512]{1,0:T(8,128)(2,1)S(1)} %get-tuple-element.31), channel_id=1, source_target_pairs={{0,2},{1,3},{2,0},{3,1},{4,6},{5,7},{6,4},{7,5},{8,10},{9,11},{10,... | collective-permute-start | bytes 589832 | tf_op jit(solution)/shard_map/ppermute | solution.py:361
  24.8 4.2 %collective-permute-done.8.first_ref.arrived_ref = bf16[256,512]{1,0:T(8,128)(2,1)S(1)} collective-permute-done((bf16[256,512]{1,0:T(8,128)(2,1)S(1)}, bf16[256,512]{1,0:T(8,128)(2,1)S(1)}, u32[]{:S(2)}, u32[]{:S(2)}) %collective-permute-start.8) | collective-permute-done | bytes 262176 | tf_op jit(solution)/shard_map/ppermute | solution.py:361
  29.0 3.7 %collective-permute-start.10 = (bf16[256,512]{1,0:T(8,128)(2,1)S(1)}, bf16[256,512]{1,0:T(8,128)(2,1)S(1)}, u32[]{:S(2)}, u32[]{:S(2)}) collective-permute-start(bf16[256,512]{1,0:T(8,128)(2,1)S(1)} %forward.1.refs_0_), channel_id=1, source_target_pairs={{0,6},{1,7},{6,0},{7,1},{2,4},{3,5},{4,2},{5,3},{8,14},{9,15},{14,... | collective-permute-start | bytes 786440 | tf_op jit(solution)/shard_map/ppermute | solution.py:361
  32.8 0.4 collective-permute-done.9.beside_ref.refs_1_
  33.1 0.7 %collective-permute-start.11 = (bf16[64,512]{1,0:T(8,128)(2,1)S(1)}, bf16[64,512]{1,0:T(8,128)(2,1)S(1)}, u32[]{:S(2)}, u32[]{:S(2)}) collective-permute-start(bf16[64,512]{1,0:T(8,128)(2,1)S(1)} %after.1), channel_id=1, source_target_pairs={{0,2},{1,3},{2,0},{3,1},{4,6},{5,7},{6,4},{7,5},{8,10},{9,11},{10,... | collective-permute-start | bytes 196616 | tf_op jit(solution)/shard_map/ppermute | solution.py:361
  33.9 0.5 %base.1.base_ref = f32[256,512]{1,0:T(8,128)S(1)} custom-call(bf16[256,512]{1,0:T(8,128)(2,1)S(1)} %gate.1.own_ref, bf16[256,512]{1,0:T(8,128)(2,1)S(1)} %collective-permute-done.6.other_ref, bf16[4,512,512]{2,1,0:T(8,128)(2,1)S(1)} %get-tuple-element.30.weight.own_weight, bf16[512,4096]{1,0:T(8,128)(2,1)S(1)} %collective-permute-done.7.other_weight, ...), custom_call_target="tpu_custom_call" | custom-call | tf_op jit(solution)/shard_map/base/pallas_call | solution.py:290
  34.4 5.8 %collective-permute-done.10.mirror_ref = bf16[256,512]{1,0:T(8,128)(2,1)S(1)} collective-permute-done((bf16[256,512]{1,0:T(8,128)(2,1)S(1)}, bf16[256,512]{1,0:T(8,128)(2,1)S(1)}, u32[]{:S(2)}, u32[]{:S(2)}) %collective-permute-start.10) | collective-permute-done | bytes 262176 | tf_op jit(solution)/shard_map/ppermute | solution.py:361
  40.2 1.2 %collective-permute-done.11.late_ref = bf16[64,512]{1,0:T(8,128)(2,1)S(1)} collective-permute-done((bf16[64,512]{1,0:T(8,128)(2,1)S(1)}, bf16[64,512]{1,0:T(8,128)(2,1)S(1)}, u32[]{:S(2)}, u32[]{:S(2)}) %collective-permute-start.11) | collective-permute-done | bytes 65568 | tf_op jit(solution)/shard_map/ppermute | solution.py:361
  41.4 0.7 %final.1 = bf16[256,512]{1,0:T(8,128)(2,1)} custom-call(f32[256,512]{1,0:T(8,128)S(1)} %nearly.1.base_ref, bf16[64,512]{1,0:T(8,128)(2,1)S(1)} %collective-permute-done.11.late_ref), custom_call_target="tpu_custom_call" | custom-call | tf_op jit(solution)/shard_map/final/pallas_call | solution.py:332
  (5 shorter events, 0.1 us)
Async XLA Ops:
  0.0 19.2 %collective-permute-start.7 = (bf16[512,4096]{1,0:T(8,128)(2,1)}, bf16[512,4096]{1,0:T(8,128)(2,1)S(1)}, u32[]{:S(2)}, u32[]{:S(2)}) collective-permute-start(bf16[512,4096]{1,0:T(8,128)(2,1)} %weight_hbm.1), channel_id=1, source_target_pairs={{0,1},{1,0},{2,3},{3,2},{4,5},{5,4},{6,7},{7,6},{8,9},{9,8},{10,11... | collective-permute-start | bytes 12582920 | tf_op jit(solution)/shard_map/ppermute | solution.py:366
  1.7 6.1 %collective-permute-start = (bf16[272,128]{1,0:T(8,128)(2,1)S(1)}, bf16[272,128]{1,0:T(8,128)(2,1)S(1)}, u32[]{:S(2)}, u32[]{:S(2)}) collective-permute-start(bf16[272,128]{1,0:T(8,128)(2,1)S(1)} %get-tuple-element.23), channel_id=1, source_target_pairs={{0,24},{1,17},{2,26},{3,19},{4,28},{5,21},{6,30},{7,23},{8,16},{9,... | collective-permute-start | bytes 208904 | tf_op jit(solution)/shard_map/ppermute | solution.py:357
  5.2 4.7 %collective-permute-start.1 = (bf16[272,128]{1,0:T(8,128)(2,1)S(1)}, bf16[272,128]{1,0:T(8,128)(2,1)S(1)}, u32[]{:S(2)}, u32[]{:S(2)}) collective-permute-start(bf16[272,128]{1,0:T(8,128)(2,1)S(1)} %get-tuple-element.24), channel_id=1, source_target_pairs={{0,8},{1,25},{2,10},{3,27},{4,12},{5,29},{6,14},{7,31},{8,0},{9,17... | collective-permute-start | bytes 208904 | tf_op jit(solution)/shard_map/ppermute | solution.py:357
  5.7 4.3 %collective-permute-start.2 = (bf16[272,128]{1,0:T(8,128)(2,1)S(1)}, bf16[272,128]{1,0:T(8,128)(2,1)S(1)}, u32[]{:S(2)}, u32[]{:S(2)}) collective-permute-start(bf16[272,128]{1,0:T(8,128)(2,1)S(1)} %get-tuple-element.25), channel_id=1, source_target_pairs={{0,16},{1,9},{2,18},{3,11},{4,20},{5,13},{6,22},{7,15},{8,24},{9,1... | collective-permute-start | bytes 208904 | tf_op jit(solution)/shard_map/ppermute | solution.py:357
  11.1 5.4 %collective-permute-start.3 = (bf16[256,128]{1,0:T(8,128)(2,1)S(1)}, bf16[256,128]{1,0:T(8,128)(2,1)S(1)}, u32[]{:S(2)}, u32[]{:S(2)}) collective-permute-start(bf16[256,128]{1,0:T(8,128)(2,1)S(1)} %get-tuple-element.26), channel_id=1, source_target_pairs={{0,24},{1,17},{2,26},{3,19},{4,28},{5,21},{6,30},{7,23},{8,16},{9,... | collective-permute-start | bytes 196616 | tf_op jit(solution)/shard_map/ppermute | solution.py:357
  12.8 4.6 %collective-permute-start.4 = (bf16[256,128]{1,0:T(8,128)(2,1)S(1)}, bf16[256,128]{1,0:T(8,128)(2,1)S(1)}, u32[]{:S(2)}, u32[]{:S(2)}) collective-permute-start(bf16[256,128]{1,0:T(8,128)(2,1)S(1)} %get-tuple-element.27), channel_id=1, source_target_pairs={{0,8},{1,25},{2,10},{3,27},{4,12},{5,29},{6,14},{7,31},{8,0},{9,17... | collective-permute-start | bytes 196616 | tf_op jit(solution)/shard_map/ppermute | solution.py:357
  13.2 4.3 %collective-permute-start.5 = (bf16[256,128]{1,0:T(8,128)(2,1)S(1)}, bf16[256,128]{1,0:T(8,128)(2,1)S(1)}, u32[]{:S(2)}, u32[]{:S(2)}) collective-permute-start(bf16[256,128]{1,0:T(8,128)(2,1)S(1)} %get-tuple-element.28), channel_id=1, source_target_pairs={{0,16},{1,9},{2,18},{3,11},{4,20},{5,13},{6,22},{7,15},{8,24},{9,1... | collective-permute-start | bytes 196616 | tf_op jit(solution)/shard_map/ppermute | solution.py:357
  17.6 1.6 %collective-permute-start.6 = (bf16[256,512]{1,0:T(8,128)(2,1)S(1)}, bf16[256,512]{1,0:T(8,128)(2,1)S(1)}, u32[]{:S(2)}, u32[]{:S(2)}) collective-permute-start(bf16[256,512]{1,0:T(8,128)(2,1)S(1)} %gate.1.own_ref), channel_id=1, source_target_pairs={{0,1},{1,0},{2,3},{3,2},{4,5},{5,4},{6,7},{7,6},{8,9},{9,8},{10,11... | collective-permute-start | bytes 786440 | tf_op jit(solution)/shard_map/ppermute | solution.py:366
  19.5 9.5 %collective-permute-start.8 = (bf16[256,512]{1,0:T(8,128)(2,1)S(1)}, bf16[256,512]{1,0:T(8,128)(2,1)S(1)}, u32[]{:S(2)}, u32[]{:S(2)}) collective-permute-start(bf16[256,512]{1,0:T(8,128)(2,1)S(1)} %by_two.1), channel_id=1, source_target_pairs={{0,2},{1,3},{6,4},{7,5},{2,6},{3,7},{4,0},{5,1},{8,10},{9,11},{14,... | collective-permute-start | bytes 786440 | tf_op jit(solution)/shard_map/ppermute | solution.py:361
  22.2 10.9 %collective-permute-start.9 = (bf16[192,512]{1,0:T(8,128)(2,1)S(1)}, bf16[192,512]{1,0:T(8,128)(2,1)S(1)}, u32[]{:S(2)}, u32[]{:S(2)}) collective-permute-start(bf16[192,512]{1,0:T(8,128)(2,1)S(1)} %get-tuple-element.31), channel_id=1, source_target_pairs={{0,2},{1,3},{2,0},{3,1},{4,6},{5,7},{6,4},{7,5},{8,10},{9,11},{10,... | collective-permute-start | bytes 589832 | tf_op jit(solution)/shard_map/ppermute | solution.py:361
  29.0 11.1 %collective-permute-start.10 = (bf16[256,512]{1,0:T(8,128)(2,1)S(1)}, bf16[256,512]{1,0:T(8,128)(2,1)S(1)}, u32[]{:S(2)}, u32[]{:S(2)}) collective-permute-start(bf16[256,512]{1,0:T(8,128)(2,1)S(1)} %forward.1.refs_0_), channel_id=1, source_target_pairs={{0,6},{1,7},{6,0},{7,1},{2,4},{3,5},{4,2},{5,3},{8,14},{9,15},{14,... | collective-permute-start | bytes 786440 | tf_op jit(solution)/shard_map/ppermute | solution.py:361
  33.1 8.3 %collective-permute-start.11 = (bf16[64,512]{1,0:T(8,128)(2,1)S(1)}, bf16[64,512]{1,0:T(8,128)(2,1)S(1)}, u32[]{:S(2)}, u32[]{:S(2)}) collective-permute-start(bf16[64,512]{1,0:T(8,128)(2,1)S(1)} %after.1), channel_id=1, source_target_pairs={{0,2},{1,3},{2,0},{3,1},{4,6},{5,7},{6,4},{7,5},{8,10},{9,11},{10,... | collective-permute-start | bytes 196616 | tf_op jit(solution)/shard_map/ppermute | solution.py:361

commit v10 on v7

--- a/solution.py
+++ b/solution.py
@@ -147,8 +147,8 @@
         first = (seq_place() ^ away(GOING, slot)) * per_shard
         tap_rows = packed_ref[rows:, :].astype(F32)
         for k in range(per_shard):
-            tokens = packed_ref[k * LANES : (k + 1) * LANES, :].astype(F32)
-            signal[first + k] = tokens.T.astype(BF16)
+            tokens = packed_ref[k * LANES : (k + 1) * LANES, :]
+            signal[first + k] = tokens.T
             taps[first + k] = tap_rows[k * part : (k + 1) * part, :]
 
     below = lax.broadcasted_iota(jnp.int32, (LANES, LANES), 0)
@@ -182,7 +182,7 @@
     for slot, out_ref in enumerate(out_refs):
         first = (seq_place() ^ away(RETURNING, slot)) * per_shard
         for k in range(per_shard):
-            out_ref[k * LANES : (k + 1) * LANES, :] = total[first + k].T.astype(BF16)
+            out_ref[k * LANES : (k + 1) * LANES, :] = total[first + k].astype(BF16).T
 
 
 def convolve(packed, n_seq, rows, part):

time: 42.4 us -> 42.4 us (level)
  no operation moved by 1% of the time
where the time goes in v10:
time: 42.4 us; the launch traced here: 42.1 us
  waiting for transfers between devices  18.3 us (43%)
  starting transfers between devices  16.9 us (40%)
  Pallas kernels  6.8 us (16%)
    ppermute x4, waiting for transfers between devices, over_chips(): lax.ppermute(value, 'chan', [(2 * a + c, 2 * b + c) for a, b in moves for...  11.8 us
    ppermute x4, starting transfers between devices, over_chips(): lax.ppermute(value, 'chan', [(2 * a + c, 2 * b + c) for a, b in moves for...  8.63 us
    ppermute x6, starting transfers between devices, over_seq(): moved.append(lax.ppermute(value, ('seq', 'chan'), pairs))  7.72 us
    ppermute x6, waiting for transfers between devices, over_seq(): moved.append(lax.ppermute(value, ('seq', 'chan'), pairs))  5.28 us
    pallas_call x8, Pallas kernels, run_kernel(): pl.pallas_call(kernel, out_shape=out_shape, in_specs=specs, out_specs=[vm...  2.03 us
    pallas_call x1, Pallas kernels, fetch(): pl.pallas_call(fetch_kernel, out_shape=[jax.ShapeDtypeStruct(query_in.sha...  1.68 us
    pallas_call x1, Pallas kernels, products(): pl.pallas_call(functools.partial(product_kernel, n_seq), out_shape=[here]...  1.24 us
    ppermute x2, waiting for transfers between devices, other_core(): return lax.ppermute(value, 'chan', [(i, i ^ 1) for i in range(n_chan)])  1.22 us
  transfers between devices with their start and end apart: 12, of which 9 were waited for; matrix products, arithmetic and copies ran while one was open for 0% of the time, Pallas kernels for 14%

profile of v10, /device:TPU:0, one launch (start us, length us, event | category | flops | bytes accessed | tf_op | source)
XLA Modules:
  0.0 42.1 jit_solution(813424388735235903)
XLA Ops:
  0.0 0.5 %collective-permute-start.7 = (bf16[512,4096]{1,0:T(8,128)(2,1)}, bf16[512,4096]{1,0:T(8,128)(2,1)S(1)}, u32[]{:S(2)}, u32[]{:S(2)}) collective-permute-start(bf16[512,4096]{1,0:T(8,128)(2,1)} %weight_hbm.1), channel_id=1, source_target_pairs={{0,1},{1,0},{2,3},{3,2},{4,5},{5,4},{6,7},{7,6},{8,9},{9,8},{10,11... | collective-permute-start | bytes 12582920 | tf_op jit(solution)/shard_map/ppermute | solution.py:366
  0.5 1.2 %products.1 = (bf16[256,512]{1,0:T(8,128)(2,1)S(1)}, bf16[272,128]{1,0:T(8,128)(2,1)S(1)}, bf16[272,128]{1,0:T(8,128)(2,1)S(1)}, bf16[272,128]{1,0:T(8,128)(2,1)S(1)}, bf16[272,128]{1,0:T(8,128)(2,1)S(1)}) custom-call(bf16[256,512]{1,0:T(8,128)(2,1)} %key_hbm.1, bf16[256,512]{1,0:T(8,128)(2,1)} %value_hbm.1, bf16[32,256]{1,0:T(8,128)(2,1)} %taps_hbm.1), custom_call_target="tpu_custom_call" | custom-call | tf_op jit(solution)/shard_map/products/pallas_call | solution.py:90
  1.7 3.5 %collective-permute-start = (bf16[272,128]{1,0:T(8,128)(2,1)S(1)}, bf16[272,128]{1,0:T(8,128)(2,1)S(1)}, u32[]{:S(2)}, u32[]{:S(2)}) collective-permute-start(bf16[272,128]{1,0:T(8,128)(2,1)S(1)} %get-tuple-element.23), channel_id=1, source_target_pairs={{0,24},{1,17},{2,26},{3,19},{4,28},{5,21},{6,30},{7,23},{8,16},{9,... | collective-permute-start | bytes 208904 | tf_op jit(solution)/shard_map/ppermute | solution.py:357
  5.2 0.5 %collective-permute-start.1 = (bf16[272,128]{1,0:T(8,128)(2,1)S(1)}, bf16[272,128]{1,0:T(8,128)(2,1)S(1)}, u32[]{:S(2)}, u32[]{:S(2)}) collective-permute-start(bf16[272,128]{1,0:T(8,128)(2,1)S(1)} %get-tuple-element.24), channel_id=1, source_target_pairs={{0,8},{1,25},{2,10},{3,27},{4,12},{5,29},{6,14},{7,31},{8,0},{9,17... | collective-permute-start | bytes 208904 | tf_op jit(solution)/shard_map/ppermute | solution.py:357
  5.7 0.1 collective-permute-start.2
  5.8 1.9 %collective-permute-done.refs_0_ = bf16[272,128]{1,0:T(8,128)(2,1)S(1)} collective-permute-done((bf16[272,128]{1,0:T(8,128)(2,1)S(1)}, bf16[272,128]{1,0:T(8,128)(2,1)S(1)}, u32[]{:S(2)}, u32[]{:S(2)}) %collective-permute-start) | collective-permute-done | bytes 69664 | tf_op jit(solution)/shard_map/ppermute | solution.py:357
  7.8 2.1 %collective-permute-done.1.refs_1_ = bf16[272,128]{1,0:T(8,128)(2,1)S(1)} collective-permute-done((bf16[272,128]{1,0:T(8,128)(2,1)S(1)}, bf16[272,128]{1,0:T(8,128)(2,1)S(1)}, u32[]{:S(2)}, u32[]{:S(2)}) %collective-permute-start.1) | collective-permute-done | bytes 69664 | tf_op jit(solution)/shard_map/ppermute | solution.py:357
  9.9 0.2 collective-permute-done.2.refs_2_
  10.1 1.0 %convolve.1 = (bf16[256,128]{1,0:T(8,128)(2,1)S(1)}, bf16[256,128]{1,0:T(8,128)(2,1)S(1)}, bf16[256,128]{1,0:T(8,128)(2,1)S(1)}, bf16[256,128]{1,0:T(8,128)(2,1)S(1)}) custom-call(bf16[272,128]{1,0:T(8,128)(2,1)S(1)} %collective-permute-done.refs_0_, bf16[272,128]{1,0:T(8,128)(2,1)S(1)} %collective-permute-done.1.refs_1_, ...), custom_call_target="tpu_custom_call" | custom-call | tf_op jit(solution)/shard_map/convolve/pallas_call | solution.py:191
  11.1 1.7 %collective-permute-start.3 = (bf16[256,128]{1,0:T(8,128)(2,1)S(1)}, bf16[256,128]{1,0:T(8,128)(2,1)S(1)}, u32[]{:S(2)}, u32[]{:S(2)}) collective-permute-start(bf16[256,128]{1,0:T(8,128)(2,1)S(1)} %get-tuple-element.26), channel_id=1, source_target_pairs={{0,24},{1,17},{2,26},{3,19},{4,28},{5,21},{6,30},{7,23},{8,16},{9,... | collective-permute-start | bytes 196616 | tf_op jit(solution)/shard_map/ppermute | solution.py:357
  12.8 0.4 collective-permute-start.4
  13.1 1.5 %collective-permute-start.5 = (bf16[256,128]{1,0:T(8,128)(2,1)S(1)}, bf16[256,128]{1,0:T(8,128)(2,1)S(1)}, u32[]{:S(2)}, u32[]{:S(2)}) collective-permute-start(bf16[256,128]{1,0:T(8,128)(2,1)S(1)} %get-tuple-element.28), channel_id=1, source_target_pairs={{0,16},{1,9},{2,18},{3,11},{4,20},{5,13},{6,22},{7,15},{8,24},{9,1... | collective-permute-start | bytes 196616 | tf_op jit(solution)/shard_map/ppermute | solution.py:357
  14.6 1.7 %fetch.1 = (bf16[256,512]{1,0:T(8,128)(2,1)S(1)}, f32[1,512]{1,0:T(1,128)S(1)}, bf16[4,512,512]{2,1,0:T(8,128)(2,1)S(1)}) custom-call(bf16[272,128]{1,0:T(8,128)(2,1)S(1)} %get-tuple-element.19.after_hbm.refs_3_, bf16[256,512]{1,0:T(8,128)(2,1)} %query_hbm.1, f32[1,512]{1,0:T(1,128)} %bitcast.1, bf16[512,4096]{1,0:T(8,128)(2,1)} %weight_hbm.1), custom_call_target="tpu_custom_call" | custom-call | tf_op jit(solution)/shard_map/fetch/pallas_call | solution.py:123
  16.3 0.1 collective-permute-done.3.refs_0_
  16.5 0.9 %collective-permute-done.4.refs_1_ = bf16[256,128]{1,0:T(8,128)(2,1)S(1)} collective-permute-done((bf16[256,128]{1,0:T(8,128)(2,1)S(1)}, bf16[256,128]{1,0:T(8,128)(2,1)S(1)}, u32[]{:S(2)}, u32[]{:S(2)}) %collective-permute-start.4) | collective-permute-done | bytes 65568 | tf_op jit(solution)/shard_map/ppermute | solution.py:357
  17.4 0.1 gate.1.own_ref
  17.5 0.1 collective-permute-start.6
  17.6 0.3 half.1.half_ref
  17.9 1.2 %collective-permute-done.6.other_ref = bf16[256,512]{1,0:T(8,128)(2,1)S(1)} collective-permute-done((bf16[256,512]{1,0:T(8,128)(2,1)S(1)}, bf16[256,512]{1,0:T(8,128)(2,1)S(1)}, u32[]{:S(2)}, u32[]{:S(2)}) %collective-permute-start.6) | collective-permute-done | bytes 262176 | tf_op jit(solution)/shard_map/ppermute | solution.py:366
  19.1 0.3 by_two.1
  19.5 1.8 %collective-permute-start.8 = (bf16[256,512]{1,0:T(8,128)(2,1)S(1)}, bf16[256,512]{1,0:T(8,128)(2,1)S(1)}, u32[]{:S(2)}, u32[]{:S(2)}) collective-permute-start(bf16[256,512]{1,0:T(8,128)(2,1)S(1)} %by_two.1), channel_id=1, source_target_pairs={{0,2},{1,3},{6,4},{7,5},{2,6},{3,7},{4,0},{5,1},{8,10},{9,11},{14,... | collective-permute-start | bytes 786440 | tf_op jit(solution)/shard_map/ppermute | solution.py:361
  21.3 0.4 %by_one.1 = (bf16[160,512]{1,0:T(8,128)(2,1)S(1)}, bf16[96,512]{1,0:T(8,128)(2,1)S(1)}) custom-call(bf16[256,512]{1,0:T(8,128)(2,1)S(1)} %gate.1.own_ref, bf16[256,512]{1,0:T(8,128)(2,1)S(1)} %collective-permute-done.6.other_ref, bf16[4,512,512]{2,1,0:T(8,128)(2,1)S(1)} %get-tuple-element.30.weight.own_weight, ...), custom_call_target="tpu_custom_call" | custom-call | tf_op jit(solution)/shard_map/by_one/pallas_call | solution.py:290
  21.7 2.7 %collective-permute-start.9 = (bf16[160,512]{1,0:T(8,128)(2,1)S(1)}, bf16[160,512]{1,0:T(8,128)(2,1)S(1)}, u32[]{:S(2)}, u32[]{:S(2)}) collective-permute-start(bf16[160,512]{1,0:T(8,128)(2,1)S(1)} %get-tuple-element.31), channel_id=1, source_target_pairs={{0,2},{1,3},{2,0},{3,1},{4,6},{5,7},{6,4},{7,5},{8,10},{9,11},{10,... | collective-permute-start | bytes 491528 | tf_op jit(solution)/shard_map/ppermute | solution.py:361
  24.4 0.4 %by_three.1.own_ref = bf16[256,512]{1,0:T(8,128)(2,1)S(1)} custom-call(bf16[256,512]{1,0:T(8,128)(2,1)S(1)} %gate.1.own_ref, bf16[256,512]{1,0:T(8,128)(2,1)S(1)} %collective-permute-done.6.other_ref, bf16[4,512,512]{2,1,0:T(8,128)(2,1)S(1)} %get-tuple-element.30.weight.own_weight, bf16[512,4096]{1,0:T(8,128)(2,1)S(1)} %collective-permute-done.7.other_weight), custom_call_target="tpu_custom_call" | custom-call | tf_op jit(solution)/shard_map/by_three/pallas_call | solution.py:290
  24.8 4.2 %collective-permute-done.8.first_ref.arrived_ref = bf16[256,512]{1,0:T(8,128)(2,1)S(1)} collective-permute-done((bf16[256,512]{1,0:T(8,128)(2,1)S(1)}, bf16[256,512]{1,0:T(8,128)(2,1)S(1)}, u32[]{:S(2)}, u32[]{:S(2)}) %collective-permute-start.8) | collective-permute-done | bytes 262176 | tf_op jit(solution)/shard_map/ppermute | solution.py:361
  29.0 3.7 %collective-permute-start.10 = (bf16[256,512]{1,0:T(8,128)(2,1)S(1)}, bf16[256,512]{1,0:T(8,128)(2,1)S(1)}, u32[]{:S(2)}, u32[]{:S(2)}) collective-permute-start(bf16[256,512]{1,0:T(8,128)(2,1)S(1)} %forward.1.refs_0_), channel_id=1, source_target_pairs={{0,6},{1,7},{6,0},{7,1},{2,4},{3,5},{4,2},{5,3},{8,14},{9,15},{14,... | collective-permute-start | bytes 786440 | tf_op jit(solution)/shard_map/ppermute | solution.py:361
  32.7 0.4 %collective-permute-start.11 = (bf16[96,512]{1,0:T(8,128)(2,1)S(1)}, bf16[96,512]{1,0:T(8,128)(2,1)S(1)}, u32[]{:S(2)}, u32[]{:S(2)}) collective-permute-start(bf16[96,512]{1,0:T(8,128)(2,1)S(1)} %after.1), channel_id=1, source_target_pairs={{0,2},{1,3},{2,0},{3,1},{4,6},{5,7},{6,4},{7,5},{8,10},{9,11},{10,... | collective-permute-start | bytes 294920 | tf_op jit(solution)/shard_map/ppermute | solution.py:361
  33.2 0.5 %base.1.base_ref = f32[256,512]{1,0:T(8,128)S(1)} custom-call(bf16[256,512]{1,0:T(8,128)(2,1)S(1)} %gate.1.own_ref, bf16[256,512]{1,0:T(8,128)(2,1)S(1)} %collective-permute-done.6.other_ref, bf16[4,512,512]{2,1,0:T(8,128)(2,1)S(1)} %get-tuple-element.30.weight.own_weight, bf16[512,4096]{1,0:T(8,128)(2,1)S(1)} %collective-permute-done.7.other_weight, ...), custom_call_target="tpu_custom_call" | custom-call | tf_op jit(solution)/shard_map/base/pallas_call | solution.py:290
  33.7 6.5 %collective-permute-done.10.mirror_ref = bf16[256,512]{1,0:T(8,128)(2,1)S(1)} collective-permute-done((bf16[256,512]{1,0:T(8,128)(2,1)S(1)}, bf16[256,512]{1,0:T(8,128)(2,1)S(1)}, u32[]{:S(2)}, u32[]{:S(2)}) %collective-permute-start.10) | collective-permute-done | bytes 262176 | tf_op jit(solution)/shard_map/ppermute | solution.py:361
  40.2 0.1 nearly.1.base_ref
  40.3 1.1 %collective-permute-done.11.late_ref = bf16[96,512]{1,0:T(8,128)(2,1)S(1)} collective-permute-done((bf16[96,512]{1,0:T(8,128)(2,1)S(1)}, bf16[96,512]{1,0:T(8,128)(2,1)S(1)}, u32[]{:S(2)}, u32[]{:S(2)}) %collective-permute-start.11) | collective-permute-done | bytes 98336 | tf_op jit(solution)/shard_map/ppermute | solution.py:361
  41.4 0.7 %final.1 = bf16[256,512]{1,0:T(8,128)(2,1)} custom-call(f32[256,512]{1,0:T(8,128)S(1)} %nearly.1.base_ref, bf16[96,512]{1,0:T(8,128)(2,1)S(1)} %collective-permute-done.11.late_ref), custom_call_target="tpu_custom_call" | custom-call | tf_op jit(solution)/shard_map/final/pallas_call | solution.py:332
  (5 shorter events, 0.1 us)
Async XLA Ops:
  0.0 19.1 %collective-permute-start.7 = (bf16[512,4096]{1,0:T(8,128)(2,1)}, bf16[512,4096]{1,0:T(8,128)(2,1)S(1)}, u32[]{:S(2)}, u32[]{:S(2)}) collective-permute-start(bf16[512,4096]{1,0:T(8,128)(2,1)} %weight_hbm.1), channel_id=1, source_target_pairs={{0,1},{1,0},{2,3},{3,2},{4,5},{5,4},{6,7},{7,6},{8,9},{9,8},{10,11... | collective-permute-start | bytes 12582920 | tf_op jit(solution)/shard_map/ppermute | solution.py:366
  1.7 6.1 %collective-permute-start = (bf16[272,128]{1,0:T(8,128)(2,1)S(1)}, bf16[272,128]{1,0:T(8,128)(2,1)S(1)}, u32[]{:S(2)}, u32[]{:S(2)}) collective-permute-start(bf16[272,128]{1,0:T(8,128)(2,1)S(1)} %get-tuple-element.23), channel_id=1, source_target_pairs={{0,24},{1,17},{2,26},{3,19},{4,28},{5,21},{6,30},{7,23},{8,16},{9,... | collective-permute-start | bytes 208904 | tf_op jit(solution)/shard_map/ppermute | solution.py:357
  5.2 4.7 %collective-permute-start.1 = (bf16[272,128]{1,0:T(8,128)(2,1)S(1)}, bf16[272,128]{1,0:T(8,128)(2,1)S(1)}, u32[]{:S(2)}, u32[]{:S(2)}) collective-permute-start(bf16[272,128]{1,0:T(8,128)(2,1)S(1)} %get-tuple-element.24), channel_id=1, source_target_pairs={{0,8},{1,25},{2,10},{3,27},{4,12},{5,29},{6,14},{7,31},{8,0},{9,17... | collective-permute-start | bytes 208904 | tf_op jit(solution)/shard_map/ppermute | solution.py:357
  5.7 4.3 %collective-permute-start.2 = (bf16[272,128]{1,0:T(8,128)(2,1)S(1)}, bf16[272,128]{1,0:T(8,128)(2,1)S(1)}, u32[]{:S(2)}, u32[]{:S(2)}) collective-permute-start(bf16[272,128]{1,0:T(8,128)(2,1)S(1)} %get-tuple-element.25), channel_id=1, source_target_pairs={{0,16},{1,9},{2,18},{3,11},{4,20},{5,13},{6,22},{7,15},{8,24},{9,1... | collective-permute-start | bytes 208904 | tf_op jit(solution)/shard_map/ppermute | solution.py:357
  11.1 5.4 %collective-permute-start.3 = (bf16[256,128]{1,0:T(8,128)(2,1)S(1)}, bf16[256,128]{1,0:T(8,128)(2,1)S(1)}, u32[]{:S(2)}, u32[]{:S(2)}) collective-permute-start(bf16[256,128]{1,0:T(8,128)(2,1)S(1)} %get-tuple-element.26), channel_id=1, source_target_pairs={{0,24},{1,17},{2,26},{3,19},{4,28},{5,21},{6,30},{7,23},{8,16},{9,... | collective-permute-start | bytes 196616 | tf_op jit(solution)/shard_map/ppermute | solution.py:357
  12.8 4.6 %collective-permute-start.4 = (bf16[256,128]{1,0:T(8,128)(2,1)S(1)}, bf16[256,128]{1,0:T(8,128)(2,1)S(1)}, u32[]{:S(2)}, u32[]{:S(2)}) collective-permute-start(bf16[256,128]{1,0:T(8,128)(2,1)S(1)} %get-tuple-element.27), channel_id=1, source_target_pairs={{0,8},{1,25},{2,10},{3,27},{4,12},{5,29},{6,14},{7,31},{8,0},{9,17... | collective-permute-start | bytes 196616 | tf_op jit(solution)/shard_map/ppermute | solution.py:357
  13.1 4.3 %collective-permute-start.5 = (bf16[256,128]{1,0:T(8,128)(2,1)S(1)}, bf16[256,128]{1,0:T(8,128)(2,1)S(1)}, u32[]{:S(2)}, u32[]{:S(2)}) collective-permute-start(bf16[256,128]{1,0:T(8,128)(2,1)S(1)} %get-tuple-element.28), channel_id=1, source_target_pairs={{0,16},{1,9},{2,18},{3,11},{4,20},{5,13},{6,22},{7,15},{8,24},{9,1... | collective-permute-start | bytes 196616 | tf_op jit(solution)/shard_map/ppermute | solution.py:357
  17.5 1.6 %collective-permute-start.6 = (bf16[256,512]{1,0:T(8,128)(2,1)S(1)}, bf16[256,512]{1,0:T(8,128)(2,1)S(1)}, u32[]{:S(2)}, u32[]{:S(2)}) collective-permute-start(bf16[256,512]{1,0:T(8,128)(2,1)S(1)} %gate.1.own_ref), channel_id=1, source_target_pairs={{0,1},{1,0},{2,3},{3,2},{4,5},{5,4},{6,7},{7,6},{8,9},{9,8},{10,11... | collective-permute-start | bytes 786440 | tf_op jit(solution)/shard_map/ppermute | solution.py:366
  19.5 9.5 %collective-permute-start.8 = (bf16[256,512]{1,0:T(8,128)(2,1)S(1)}, bf16[256,512]{1,0:T(8,128)(2,1)S(1)}, u32[]{:S(2)}, u32[]{:S(2)}) collective-permute-start(bf16[256,512]{1,0:T(8,128)(2,1)S(1)} %by_two.1), channel_id=1, source_target_pairs={{0,2},{1,3},{6,4},{7,5},{2,6},{3,7},{4,0},{5,1},{8,10},{9,11},{14,... | collective-permute-start | bytes 786440 | tf_op jit(solution)/shard_map/ppermute | solution.py:361
  21.7 11.0 %collective-permute-start.9 = (bf16[160,512]{1,0:T(8,128)(2,1)S(1)}, bf16[160,512]{1,0:T(8,128)(2,1)S(1)}, u32[]{:S(2)}, u32[]{:S(2)}) collective-permute-start(bf16[160,512]{1,0:T(8,128)(2,1)S(1)} %get-tuple-element.31), channel_id=1, source_target_pairs={{0,2},{1,3},{2,0},{3,1},{4,6},{5,7},{6,4},{7,5},{8,10},{9,11},{10,... | collective-permute-start | bytes 491528 | tf_op jit(solution)/shard_map/ppermute | solution.py:361
  29.0 11.2 %collective-permute-start.10 = (bf16[256,512]{1,0:T(8,128)(2,1)S(1)}, bf16[256,512]{1,0:T(8,128)(2,1)S(1)}, u32[]{:S(2)}, u32[]{:S(2)}) collective-permute-start(bf16[256,512]{1,0:T(8,128)(2,1)S(1)} %forward.1.refs_0_), channel_id=1, source_target_pairs={{0,6},{1,7},{6,0},{7,1},{2,4},{3,5},{4,2},{5,3},{8,14},{9,15},{14,... | collective-permute-start | bytes 786440 | tf_op jit(solution)/shard_map/ppermute | solution.py:361
  32.7 8.6 %collective-permute-start.11 = (bf16[96,512]{1,0:T(8,128)(2,1)S(1)}, bf16[96,512]{1,0:T(8,128)(2,1)S(1)}, u32[]{:S(2)}, u32[]{:S(2)}) collective-permute-start(bf16[96,512]{1,0:T(8,128)(2,1)S(1)} %after.1), channel_id=1, source_target_pairs={{0,2},{1,3},{2,0},{3,1},{4,6},{5,7},{6,4},{7,5},{8,10},{9,11},{10,... | collective-permute-start | bytes 294920 | tf_op jit(solution)/shard_map/ppermute | solution.py:361
